TPU v7x, 32 devices: a whole 2x2x4 slice. The times are simulated.
32 devices in a mesh: dp: 8 (over z, x), tensor: 4 (over y, core).
Axes of the slice: x: 2, y: 2, z: 4, core: 2. Of those that a mesh axis runs over, the one named last changes fastest.
Arguments:
- inputs: bfloat16 [8, 1024, 768], P('dp'), may hold values from -6 to 6
- segments: int32 [8, 1024], P('dp'), may hold values from 0 to 3, never falling along the last dimension, each value on 1 to 512 neighbouring positions
- cotangent: bfloat16 [8, 1024, 768], P('dp'), may hold values from -6 to 6
- owner: int32 [768], replicated, may hold values from 0 to 7, as said below
- masters: float32 [4, 768, 48, 48], P('tensor', 'dp')
- first_moment: float32 [4, 768, 48, 48], P('tensor', 'dp')
- second_moment: float32 [4, 768, 48, 48], P('tensor', 'dp'), as said below
- left_stats: float32 [4, 768, 48, 48], P('tensor', 'dp'), as said below
- right_stats: float32 [4, 768, 48, 48], P('tensor', 'dp'), as said below
- left_basis: float32 [4, 768, 48, 48], P('tensor', 'dp'), as said below
- right_basis: float32 [4, 768, 48, 48], P('tensor', 'dp'), as said below
- norm_master: float32 [3072], P('dp')
- norm_first: float32 [3072], P('dp')
- norm_second: float32 [3072], P('dp'), as said below
Outputs:
- output: bfloat16 [8, 1024, 768], P('dp')
- input_grad: float32 [8, 1024, 768], P('dp')
- new_first: float32 [4, 768, 48, 48], P('tensor', 'dp')
- new_second: float32 [4, 768, 48, 48], P('tensor', 'dp')
- new_master: float32 [4, 768, 48, 48], P('tensor', 'dp')
- new_left_stats: float32 [4, 768, 48, 48], P('tensor', 'dp')
- new_right_stats: float32 [4, 768, 48, 48], P('tensor', 'dp')
- new_left_basis: float32 [4, 768, 48, 48], P('tensor', 'dp')
- renewed_right_rotation: float32 [4, 768, 48, 48], P('tensor', 'dp')
- new_norm_first: float32 [3072], P('dp')
- new_norm_second: float32 [3072], P('dp')
- new_norm: float32 [3072], P('dp')
Inputs may be any that keep to these rules, and one draw needn't show every extreme that they name: `owner`: every data index owns exactly 96 blocks. `segments`: ids never fall along a row; a row holds 4 documents of at most 512 tokens, one of exactly that many. `left_basis`: each block is orthogonal. `right_basis`: each block is orthogonal. `left_stats`: each block is symmetric positive definite. `right_stats`: each block is symmetric positive definite. `second_moment`: Positive. `norm_second`: Positive.
All inputs are finite; a program needn't handle non-finite values.
Results may differ from a plain program's by a relative error of at most 0.012.
Values may be sent and summed in bfloat16 or wider, within the bound.
A program may use at most 192 MiB of HBM per device.

v0:
```python
import math

import jax
import jax.numpy as jnp
from jax import lax
from jax.sharding import PartitionSpec as P

HD = 64
STEP = 10


highest = lax.Precision.HIGHEST
norm_eps = 1e-05
beta_one = 0.9
beta_two = 0.95
beta_stats = 0.95
learn_rate = 0.03
norm_rate = 0.4
weight_decay = 0.01
adam_eps = 1e-08


def spread(shard, axis, root):
    mine = lax.axis_index(axis) == root
    return lax.psum(jnp.where(mine, shard, jnp.zeros_like(shard)), axis)


def entering(part, axis, combine, identity):
    count = lax.axis_size(axis)
    place = lax.axis_index(axis)
    ahead = count - 1 - place
    gathered = lax.all_gather(part, axis)
    state = jnp.zeros_like(part) + jnp.asarray(identity, part.dtype)

    def one(lap, state):
        source = count - 1 - lap
        return combine(state, lax.dynamic_index_in_dim(gathered, source, 0, False))

    return lax.fori_loop(0, ahead, one, state)


def shift_for(length):
    return math.log(length / 8.0)


def block_slots(owner, per_dev):
    count = owner.shape[0]
    index = jnp.arange(count, dtype=jnp.int32)
    earlier = (owner[:, None] == owner[None, :]) & (index[None, :] < index[:, None])
    rank = jnp.sum(earlier.astype(jnp.int32), axis=1)
    slots = owner * per_dev + rank
    inverse = jnp.sum(jnp.where(slots[None, :] == index[:, None], index[None, :], 0), axis=1)
    return (slots, inverse)


def blocks_to_matrix(blocks, grid_rows):
    block = blocks.shape[-1]
    grid_cols = blocks.shape[0] // grid_rows
    return (
        blocks.reshape(grid_rows, grid_cols, block, block)
        .transpose(0, 2, 1, 3)
        .reshape(grid_rows * block, grid_cols * block)
    )


def matrix_to_blocks(weight_matrix, block):
    grid_rows = weight_matrix.shape[0] // block
    grid_cols = weight_matrix.shape[1] // block
    return (
        weight_matrix.reshape(grid_rows, block, grid_cols, block)
        .transpose(0, 2, 1, 3)
        .reshape(grid_rows * grid_cols, block, block)
    )


def normalize(rows):
    centered = rows - jnp.mean(rows, axis=-1, keepdims=True)
    inverse_std = lax.rsqrt(jnp.mean(centered * centered, axis=-1, keepdims=True) + norm_eps)
    return (centered * inverse_std, inverse_std)


def norm_back(plain, inverse_std, grad):
    return inverse_std * (
        grad
        - jnp.mean(grad, axis=-1, keepdims=True)
        - plain * jnp.mean(grad * plain, axis=-1, keepdims=True)
    )


def contract_rows(left, right):
    return lax.dot_general(
        left, right, (((0,), (0,)), ((), ())), preferred_element_type=jnp.float32
    )


def contract_cols(left, right):
    return lax.dot_general(
        left, right, (((1,), (1,)), ((), ())), preferred_element_type=jnp.float32
    )


def row_masks(row_seg):
    position = jnp.arange(row_seg.shape[0], dtype=jnp.int32)
    same = row_seg[:, None] == row_seg[None, :]
    return (
        same & (position[None, :] <= position[:, None]),
        same & (position[None, :] < position[:, None]),
    )


def penalty_from(first_raw, strict):
    picks = jnp.where(strict, jax.nn.softplus(first_raw - shift_for(first_raw.shape[0])), 0.0)
    running = jnp.cumsum(picks, axis=0)
    return jnp.concatenate([jnp.zeros((1, picks.shape[1]), picks.dtype), running[:-1]], axis=0)


def later_sums(grads):
    suffix = jnp.cumsum(grads[::-1], axis=0)[::-1]
    return jnp.concatenate([suffix[1:], jnp.zeros((1, suffix.shape[1]), suffix.dtype)], axis=0)


def append_column_block(earlier, latter):
    return earlier + latter


def split_heads(row_proj, rank_attn):
    length = row_proj.shape[0]

    def heads_of(piece):
        return piece.reshape(length, -1, HD).transpose(1, 0, 2)

    return (
        heads_of(row_proj[:, :rank_attn]),
        heads_of(row_proj[:, rank_attn : 2 * rank_attn]),
        heads_of(row_proj[:, 2 * rank_attn :]),
    )


def merge_heads(heads):
    return heads.transpose(1, 0, 2).reshape(heads.shape[1], -1)


def batch_prod(left, right):
    return jnp.einsum("nij,njk->nik", left, right, precision=highest)


def swap_last(weight_matrix):
    return jnp.swapaxes(weight_matrix, -1, -2)


def orthonormal(weight_matrix):
    gram = batch_prod(swap_last(weight_matrix), weight_matrix)
    factor = jnp.linalg.cholesky(gram)
    solved = jax.scipy.linalg.solve_triangular(factor, swap_last(weight_matrix), lower=True)
    return swap_last(solved)


def soap_update(grad, master, first, second, left_stats, right_stats, left_basis, right_basis):
    new_left = beta_stats * left_stats + (1.0 - beta_stats) * batch_prod(grad, swap_last(grad))
    new_right = beta_stats * right_stats + (1.0 - beta_stats) * batch_prod(swap_last(grad), grad)
    rotated = batch_prod(batch_prod(swap_last(left_basis), grad), right_basis)
    new_first = beta_one * first + (1.0 - beta_one) * rotated
    new_second = beta_two * second + (1.0 - beta_two) * rotated * rotated
    direction = (
        new_first
        / (1.0 - beta_one**STEP)
        / (jnp.sqrt(new_second / (1.0 - beta_two**STEP)) + adam_eps)
    )
    moved = batch_prod(batch_prod(left_basis, direction), swap_last(right_basis))
    new_master = master - learn_rate * (moved + weight_decay * master)
    count = grad.shape[0]
    both_sides = jnp.concatenate(
        [batch_prod(new_left, left_basis), batch_prod(new_right, right_basis)], axis=0
    )
    renewed = orthonormal(both_sides)
    return (
        new_first,
        new_second,
        new_master,
        new_left,
        new_right,
        renewed[:count],
        renewed[count:],
    )


def norm_update(grad, master, first, second):
    new_first = beta_one * first + (1.0 - beta_one) * grad
    new_second = beta_two * second + (1.0 - beta_two) * grad * grad
    direction = (
        new_first
        / (1.0 - beta_one**STEP)
        / (jnp.sqrt(new_second / (1.0 - beta_two**STEP)) + adam_eps)
    )
    return (new_first, new_second, master - norm_rate * direction)


def body(
    inputs,
    segments,
    cotangent,
    owner,
    masters,
    first_moment,
    second_moment,
    left_stats,
    right_stats,
    left_basis,
    right_basis,
    norm_master,
    norm_first,
    norm_second,
):
    rows_here = inputs.shape[0]
    length = inputs.shape[1]
    width = inputs.shape[2]
    tensor_count = lax.axis_size("tensor")
    rank_attn = width // tensor_count
    per_dev = masters.shape[1]
    block = masters.shape[-1]
    scale = HD ** (-0.5)
    sel_shift = shift_for(length)
    tensor_index = lax.axis_index("tensor")
    shared_blocks, shared_norms = (
        lax.all_gather(masters[0].astype(jnp.bfloat16), "dp", axis=0, tiled=True),
        lax.all_gather(norm_master.astype(jnp.bfloat16), "dp", axis=0, tiled=True),
    )
    slots, inverse = block_slots(owner, per_dev)
    weight_matrix = blocks_to_matrix(jnp.take(shared_blocks, slots, axis=0), width // block)
    rank_mlp = (weight_matrix.shape[1] - 4 * rank_attn) // 2
    w_project = weight_matrix[:, : 3 * rank_attn]
    w_up = weight_matrix[:, 3 * rank_attn : 3 * rank_attn + rank_mlp]
    w_out_side = weight_matrix[:, 3 * rank_attn + rank_mlp : 4 * rank_attn + rank_mlp]
    w_down_side = weight_matrix[:, 4 * rank_attn + rank_mlp :]
    norms = shared_norms.astype(jnp.float32).reshape(4, width)
    tokens = inputs.reshape(rows_here * length, width).astype(jnp.float32)
    plain_one, inverse_one = normalize(tokens)
    normed_one = (plain_one * norms[0] + norms[1]).astype(jnp.bfloat16)
    projected = jnp.dot(normed_one, w_project, preferred_element_type=jnp.float32).astype(
        jnp.bfloat16
    )
    projection_rows = projected.reshape(rows_here, length, 3 * rank_attn)

    def attention_single_row(packed):
        row_proj, row_seg = packed
        queries, keys, values = split_heads(row_proj, rank_attn)
        raw = jnp.einsum("hqd,hkd->hqk", queries, keys, preferred_element_type=jnp.float32) * scale
        allowed, strict = row_masks(row_seg)

        def make_penalty(first_raw):
            return penalty_from(first_raw, strict).astype(jnp.bfloat16)

        def blank_penalty(first_raw):
            return jnp.zeros(first_raw.shape, jnp.bfloat16)

        local = lax.cond(tensor_index == 0, make_penalty, blank_penalty, raw[0])
        penalty = spread(local, "tensor", 0)
        logits = jnp.where(allowed[None], raw - penalty.astype(jnp.float32)[None], -1e30)
        top = jnp.max(logits, axis=-1, keepdims=True)
        weights = jnp.exp(logits - top)
        total = jnp.sum(weights, axis=-1, keepdims=True)
        probs = weights / total
        mixed = jnp.einsum(
            "hqk,hkd->hqd", probs.astype(jnp.bfloat16), values, preferred_element_type=jnp.float32
        )
        return (
            merge_heads(mixed).astype(jnp.bfloat16),
            top[..., 0] + jnp.log(total[..., 0]),
            penalty,
        )

    attention_output, logarithm_row_totals, selection_penalty = lax.map(
        attention_single_row, (projection_rows, segments)
    )
    attended_flat = attention_output.reshape(rows_here * length, rank_attn)
    attn_total = lax.psum(contract_cols(attended_flat, w_out_side), "tensor")
    resid = tokens + attn_total
    plain_two, inverse_two = normalize(resid)
    normed_two = (plain_two * norms[2] + norms[3]).astype(jnp.bfloat16)
    up_pre = jnp.dot(normed_two, w_up, preferred_element_type=jnp.float32)
    activated = jax.nn.gelu(up_pre, approximate=True).astype(jnp.bfloat16)
    mlp_total = lax.psum(contract_cols(activated, w_down_side), "tensor")
    output = (resid + mlp_total).astype(jnp.bfloat16).reshape(inputs.shape)
    back_out = cotangent.reshape(rows_here * length, width)
    d_act = jnp.dot(back_out, w_down_side, preferred_element_type=jnp.float32)
    grad_down_side = contract_rows(back_out, activated)

    def gelu_tanh(values):
        return jax.nn.gelu(values, approximate=True)

    gelu_pull = jax.vjp(gelu_tanh, up_pre)[1]
    d_up = gelu_pull(d_act)[0].astype(jnp.bfloat16)
    grad_up = contract_rows(normed_two, d_up)
    d_two = lax.psum(contract_cols(d_up, w_up), "tensor")
    grad_gain_two = jnp.sum(d_two * plain_two, axis=0)
    grad_bias_two = jnp.sum(d_two, axis=0)
    d_resid = back_out.astype(jnp.float32) + norm_back(plain_two, inverse_two, d_two * norms[2])
    d_resid_low = d_resid.astype(jnp.bfloat16)
    d_attended = jnp.dot(d_resid_low, w_out_side, preferred_element_type=jnp.float32).astype(
        jnp.bfloat16
    )
    grad_out_side = contract_rows(d_resid_low, attended_flat)

    def attend_back(packed):
        row_proj, row_seg, row_back, row_log, row_pen = packed
        queries, keys, values = split_heads(row_proj, rank_attn)
        back_heads = row_back.reshape(length, -1, HD).transpose(1, 0, 2)
        raw = jnp.einsum("hqd,hkd->hqk", queries, keys, preferred_element_type=jnp.float32) * scale
        allowed, strict = row_masks(row_seg)
        logits = jnp.where(allowed[None], raw - row_pen.astype(jnp.float32)[None], -1e30)
        probs = jnp.exp(logits - row_log[..., None])
        d_probs = jnp.einsum("hqd,hkd->hqk", back_heads, values, preferred_element_type=jnp.float32)
        inner = jnp.sum(d_probs * probs, axis=-1, keepdims=True)
        d_logits = probs * (d_probs - inner)
        pen_terms = -jnp.sum(d_logits, axis=0)
        share = lax.psum_scatter(pen_terms, "tensor", scatter_dimension=0, tiled=True)
        carried = entering(
            jnp.sum(share, axis=0),
            "tensor",
            append_column_block,
            jnp.zeros((share.shape[1],), jnp.float32),
        )
        later = lax.all_gather(later_sums(share) + carried[None], "tensor", axis=0, tiled=True)

        def with_selection(first):
            return first + jnp.where(strict, jax.nn.sigmoid(raw[0] - sel_shift) * later, 0.0)

        def without_selection(first):
            return first

        first_head = lax.cond(tensor_index == 0, with_selection, without_selection, d_logits[0])
        d_raw = jnp.concatenate([first_head[None], d_logits[1:]], axis=0).astype(jnp.bfloat16)
        d_query = (
            jnp.einsum("hqk,hkd->hqd", d_raw, keys, preferred_element_type=jnp.float32) * scale
        )
        d_key = (
            jnp.einsum("hqk,hqd->hkd", d_raw, queries, preferred_element_type=jnp.float32) * scale
        )
        d_value = jnp.einsum(
            "hqk,hqd->hkd",
            probs.astype(jnp.bfloat16),
            back_heads,
            preferred_element_type=jnp.float32,
        )
        return jnp.concatenate(
            [merge_heads(d_query), merge_heads(d_key), merge_heads(d_value)], axis=1
        ).astype(jnp.bfloat16)

    d_projected = lax.map(
        attend_back,
        (
            projection_rows,
            segments,
            d_attended.reshape(rows_here, length, rank_attn),
            logarithm_row_totals,
            selection_penalty,
        ),
    )
    d_projected = d_projected.reshape(rows_here * length, 3 * rank_attn)
    d_one = lax.psum(contract_cols(d_projected, w_project), "tensor")
    grad_project = contract_rows(normed_one, d_projected)
    grad_gain_one = jnp.sum(d_one * plain_one, axis=0)
    grad_bias_one = jnp.sum(d_one, axis=0)
    input_grad = (d_resid + norm_back(plain_one, inverse_one, d_one * norms[0])).reshape(
        inputs.shape
    )
    grad_matrix = jnp.concatenate([grad_project, grad_up, grad_out_side, grad_down_side], axis=1)
    stored_grads = jnp.take(matrix_to_blocks(grad_matrix, block), inverse, axis=0)
    norm_grads = jnp.concatenate(
        [grad_gain_one, grad_bias_one, grad_gain_two, grad_bias_two], axis=0
    )
    own_grads, own_norm_grads = (
        lax.psum_scatter(stored_grads, "dp", scatter_dimension=0, tiled=True),
        lax.psum_scatter(norm_grads, "dp", scatter_dimension=0, tiled=True),
    )
    new_first, new_second, new_master, new_left, new_right, left_next, right_next = soap_update(
        own_grads,
        masters[0],
        first_moment[0],
        second_moment[0],
        left_stats[0],
        right_stats[0],
        left_basis[0],
        right_basis[0],
    )
    norm_first_new, norm_second_new, norm_new = norm_update(
        own_norm_grads, norm_master, norm_first, norm_second
    )
    return (
        output,
        input_grad,
        new_first[None],
        new_second[None],
        new_master[None],
        new_left[None],
        new_right[None],
        left_next[None],
        right_next[None],
        norm_first_new,
        norm_second_new,
        norm_new,
    )


def solution(mesh):
    in_specs = (
        P("dp", None, None),
        P("dp", None),
        P("dp", None, None),
        P(),
        P("tensor", "dp", None, None),
        P("tensor", "dp", None, None),
        P("tensor", "dp", None, None),
        P("tensor", "dp", None, None),
        P("tensor", "dp", None, None),
        P("tensor", "dp", None, None),
        P("tensor", "dp", None, None),
        P("dp"),
        P("dp"),
        P("dp"),
    )
    out_specs = (
        P("dp", None, None),
        P("dp", None, None),
        P("tensor", "dp", None, None),
        P("tensor", "dp", None, None),
        P("tensor", "dp", None, None),
        P("tensor", "dp", None, None),
        P("tensor", "dp", None, None),
        P("tensor", "dp", None, None),
        P("tensor", "dp", None, None),
        P("dp"),
        P("dp"),
        P("dp"),
    )
    return jax.shard_map(body, mesh=mesh, in_specs=in_specs, out_specs=out_specs, check_vma=False)
```

profile of v0, /device:TPU:0, one launch (start us, length us, event | category | flops | bytes accessed | tf_op | source)
XLA Modules:
  0.0 2124.3 jit_solution(5292105255492167036)
XLA Ops:
  13.7 28.1 %all-gather.1 = bf16[8,1,384]{2,1,0:T(2,128)(2,1)S(1)} all-gather(bf16[1,1,384]{2,1,0:T(2,128)(2,1)S(1)} %reshape.315), channel_id=1, replica_groups=mesh['dp'=8,'tensor'=4] {'dp'}, dimensions={0}, use_global_device_ids=true | all-gather | bytes 6912 | tf_op jit(solution)/shard_map/all_gather | solution.py:226
  45.9 108.3 %all-gather.5.cloned.1.call-done = bf16[768,48,48]{2,1,0:T(8,128)(2,1)} async-done(((bf16[96,48,48]{2,1,0:T(8,128)(2,1)}), bf16[768,48,48]{2,1,0:T(8,128)(2,1)}) %all-gather.5.cloned.1.call-update) | async-done | bytes 3538960 | tf_op jit(solution)/shard_map/all_gather | solution.py:225
  173.6 13.8 reshape.280
  196.6 26.8 %conditional.2 = (bf16[1024,1024]{1,0:T(8,128)(2,1)S(1)}) conditional(s32[]{:T(128)} %convert_element_type.90, () %tuple.47, (f32[3,1024,1024]{1,2,0:T(8,128)}, pred[1024,1024]{1,0:T(8,128)(4,1)S(1)}) %tuple.48), branch_computations={%region_3.4_spmd, %region_4.7_spmd} | conditional | flops 143719424 | bytes 74680360 | solution.py:256
  196.8 12.6 copy.156
  226.9 46.7 %all-reduce.9.cloned.1.call-done = bf16[1024,1024]{1,0:T(8,128)(2,1)} async-done(((bf16[1024,1024]{1,0:T(8,128)(2,1)}), bf16[1024,1024]{1,0:T(8,128)(2,1)}) %all-reduce.9.cloned.1.call-update) | async-done | bytes 2097168 | tf_op jit(solution)/shard_map/while/body/eval_jaxpr/psum | solution.py:25
  296.1 68.2 %all-reduce.11.cloned.1.call-done = f32[1024,768]{1,0:T(8,128)} async-done(((f32[1024,768]{1,0:T(8,128)}), f32[1024,768]{1,0:T(8,128)}) %all-reduce.11.cloned.1.call-update) | async-done | bytes 3145744 | tf_op jit(solution)/shard_map/psum | solution.py:276
  380.2 68.0 %all-reduce.13.cloned.1.call-done = f32[1024,768]{1,0:T(8,128)} async-done(((f32[1024,768]{1,0:T(8,128)}), f32[1024,768]{1,0:T(8,128)}) %all-reduce.13.cloned.1.call-update) | async-done | bytes 3145744 | tf_op jit(solution)/shard_map/psum | solution.py:294
  456.8 10.4 multiply_reduce_fusion
  469.4 12.7 fusion.116
  484.8 44.5 %reduce-scatter.3.cloned.1.call-done = f32[256,1024]{0,1:T(8,128)} async-done(((f32[1024,1024]{0,1:T(8,128)}), f32[256,1024]{0,1:T(8,128)}) %reduce-scatter.3.cloned.1.call-update) | async-done | bytes 1048592 | tf_op jit(solution)/shard_map/while/body/eval_jaxpr/reduce_scatter | solution.py:316
  611.4 25.1 %conditional.3 = (bf16[1024,1024]{1,0:T(8,128)(2,1)}) conditional(s32[]{:T(128)} %convert_element_type.90, (f32[1024,1024]{0,1:T(8,128)}) %tuple.64, (f32[3,1024,1024]{1,2,0:T(8,128)}, f32[1024,1024]{1,0:T(8,128)}, pred[1024,1024]{1,0:T(8,128)(4,1)}, f32[1024,1024]{0,1:T(8,128)}) %tuple.119), branch_computations={%region_25.26_spmd, %region_26.27_spmd} | conditional | flops 8388608 | bytes 49283080 | solution.py:331
  616.8 12.6 copy.164
  662.9 15.8 reshape.293
  678.7 18.8 copy.210
  697.5 15.0 gather_fusion.1
  712.5 15.9 broadcast_select_fusion
  747.5 24.6 %all-reduce.15.cloned.1.call-done = (f32[1024,768]{1,0:T(8,128)}, f32[1024,768]{1,0:T(8,128)}) async-done(((f32[1024,768]{1,0:T(8,128)}, f32[1024,768]{1,0:T(8,128)}), (f32[1024,768]{1,0:T(8,128)}, f32[1024,768]{1,0:T(8,128)})) %all-reduce.15.cloned.1.call-update) | async-done | bytes 6291472 | tf_op jit(solution)/shard_map/psum | solution.py:282
  775.3 39.6 %all-reduce.2 = f32[3072]{0:T(1024)S(1)} all-reduce(f32[3072]{0:T(1024)S(1)} %pad_maximum_fusion.18), channel_id=5, replica_groups=mesh['dp'=8,'tensor'=4] {'dp'}, use_global_device_ids=true, to_apply=%region_38.39.clone | all-reduce | flops 3072 | bytes 24576
  823.1 266.4 %reduce-scatter.5.cloned.1.call-done = f32[96,48,48]{2,1,0:T(8,128)} async-done(((f32[768,48,48]{2,1,0:T(8,128)}), f32[96,48,48]{2,1,0:T(8,128)}) %reduce-scatter.5.cloned.1.call-update) | async-done | bytes 884752 | tf_op jit(solution)/shard_map/reduce_scatter | solution.py:373
  1148.0 10.6 fusion.25
  1171.5 846.6 %custom-call.8 = f32[192,48,48]{2,1,0:T(8,128)} custom-call(f32[192,48,48]{2,1,0:T(8,128)} %fusion.19), custom_call_target="Cholesky" | custom-call | tf_op jit(solution)/shard_map/jit(cholesky)/cholesky | solution.py:153
  2027.8 66.8 %custom-call.9 = f32[192,1,48,48]{0,2,3,1:T(8,128)} custom-call(f32[192,1,48,48]{0,3,2,1:T(8,128)} %select_bitcast_fusion), custom_call_target="InvertDiagBlocksLowerTriangular" | custom-call | tf_op jit(solution)/shard_map/jit(_solve_triangular)/vmap()/triangular_solve | solution.py:154
  2100.4 10.4 fusion.24
  (312 shorter events, 357.0 us)
Async XLA Ops:
  7.2 147.0 %all-gather.5.cloned.1.call-start = ((), (), s32[]{:S(2)}) async-start(), calls=%async_computation.2 | async-start | bytes 10616832 | tf_op jit(solution)/shard_map/all_gather | solution.py:225
  10.2 31.8 %copy-start.5 = (bf16[1,1024,768]{2,1,0:T(8,128)(2,1)S(1)}, bf16[1,1024,768]{2,1,0:T(8,128)(2,1)}, u32[]{:S(2)}) copy-start(bf16[1,1024,768]{2,1,0:T(8,128)(2,1)} %param.20) | copy-start | bytes 4718596
  10.2 32.7 %copy-start.54 = (s32[1,1024]{1,0:T(1,128)S(1)}, s32[1,1024]{1,0:T(1,128)}, u32[]{:S(2)}) copy-start(s32[1,1024]{1,0:T(1,128)} %param.21) | copy-start | bytes 12292
  13.1 260.5 %all-reduce.9.cloned.1.call-start = ((), (), s32[]{:S(2)}) async-start(), calls=%async_computation.3 | async-start | bytes 4194304 | tf_op jit(solution)/shard_map/while/body/eval_jaxpr/psum | solution.py:25
  13.6 28.6 %copy-start.53 = (s32[768]{0:T(1024)}, s32[768]{0:T(1024)S(1)}, u32[]{:S(2)}) copy-start(s32[768]{0:T(1024)S(1)} %get-tuple-element.255) | copy-start | bytes 9220
  41.9 145.5 %copy-start.61 = (f32[768]{0:T(1024)}, f32[768]{0:T(1024)S(1)}, u32[]{:S(2)}) copy-start(f32[768]{0:T(1024)S(1)} %reshape.319) | copy-start | bytes 9220
  41.9 145.5 %copy-start.48 = (f32[768]{0:T(1024)}, f32[768]{0:T(1024)S(1)}, u32[]{:S(2)}) copy-start(f32[768]{0:T(1024)S(1)} %reshape.318) | copy-start | bytes 9220
  42.2 145.2 %copy-start.44 = (f32[1024]{0:T(1024)}, f32[1024]{0:T(1024)S(1)}, u32[]{:S(2)}) copy-start(f32[1024]{0:T(1024)S(1)} %broadcast_multiply_fusion.6) | copy-start | bytes 12292
  42.9 144.5 %copy-start.50 = (f32[1024]{0:T(1024)}, f32[1024]{0:T(1024)S(1)}, u32[]{:S(2)}) copy-start(f32[1024]{0:T(1024)S(1)} %add_rsqrt_fusion.1) | copy-start | bytes 12292
  45.9 150.7 %copy-start.21 = (pred[1024,1024]{1,0:T(8,128)(4,1)}, pred[1024,1024]{1,0:T(8,128)(4,1)S(1)}, u32[]{:S(2)}) copy-start(pred[1024,1024]{1,0:T(8,128)(4,1)S(1)} %get-tuple-element.264) | copy-start | bytes 3145732
  190.2 96.5 %copy-start.27 = (bf16[1024,192]{0,1:T(8,128)(2,1)}, bf16[1024,192]{0,1:T(8,128)(2,1)S(1)}, u32[]{:S(2)}) copy-start(bf16[1024,192]{0,1:T(8,128)(2,1)S(1)} %get-tuple-element.261) | copy-start | bytes 1179652
  224.9 139.4 %all-reduce.11.cloned.1.call-start = ((), (), s32[]{:S(2)}) async-start(), calls=%async_computation.4 | async-start | bytes 6291456 | tf_op jit(solution)/shard_map/psum | solution.py:276
  295.6 152.5 %all-reduce.13.cloned.1.call-start = ((), (), s32[]{:S(2)}) async-start(), calls=%async_computation.5 | async-start | bytes 6291456 | tf_op jit(solution)/shard_map/psum | solution.py:294
  379.5 149.9 %reduce-scatter.3.cloned.1.call-start = ((), (), s32[]{:S(2)}) async-start(), calls=%async_computation.6 | async-start | bytes 5242880 | tf_op jit(solution)/shard_map/while/body/eval_jaxpr/reduce_scatter | solution.py:316
  484.6 126.8 %all-gather.7.cloned.1.call-start = ((), (), s32[]{:S(2)}) async-start(), calls=%async_computation.7 | async-start | bytes 5242880 | tf_op jit(solution)/shard_map/while/body/eval_jaxpr/all_gather | solution.py:323
  576.8 195.3 %all-reduce.15.cloned.1.call-start = ((), (), s32[]{:S(2)}) async-start(), calls=%async_computation.9 | async-start | bytes 12582912 | tf_op jit(solution)/shard_map/psum | solution.py:282
  652.1 437.4 %reduce-scatter.5.cloned.1.call-start = ((), (), s32[]{:S(2)}) async-start(), calls=%async_computation.8 | async-start | bytes 21233664 | tf_op jit(solution)/shard_map/reduce_scatter | solution.py:373
  678.7 18.8 copy-start.55
  746.1 29.1 %copy-start.56 = (f32[768]{0:T(1024)S(1)}, f32[768]{0:T(1024)}, u32[]{:S(2)}) copy-start(f32[768]{0:T(1024)} %get-tuple-element.223) | copy-start | bytes 9220
  746.1 29.1 %copy-start.57 = (f32[768]{0:T(1024)S(1)}, f32[768]{0:T(1024)}, u32[]{:S(2)}) copy-start(f32[768]{0:T(1024)} %get-tuple-element.230) | copy-start | bytes 9220
  746.1 68.7 %copy-start.59 = (f32[384]{0:T(512)S(1)}, f32[384]{0:T(512)}, u32[]{:S(2)}) copy-start(f32[384]{0:T(512)} %param.31) | copy-start | bytes 4612
  746.1 68.7 %copy-start.63 = (f32[384]{0:T(512)S(1)}, f32[384]{0:T(512)}, u32[]{:S(2)}) copy-start(f32[384]{0:T(512)} %param.33) | copy-start | bytes 4612
  746.2 68.7 %copy-start.64 = (f32[384]{0:T(512)S(1)}, f32[384]{0:T(512)}, u32[]{:S(2)}) copy-start(f32[384]{0:T(512)} %param.32) | copy-start | bytes 4612
  823.1 272.2 %copy-start.8 = (f32[96,48,48]{2,1,0:T(8,128)S(1)}, f32[96,48,48]{2,1,0:T(8,128)}, u32[]{:S(2)}) copy-start(f32[96,48,48]{2,1,0:T(8,128)} %copy.176) | copy-start | bytes 2654212
  (63 other events, 266.1 us)
Sparse Core Ops, SparseCore 0:
  13.3 140.8 all-gather.4
  225.0 48.6 all-reduce.8
  295.7 68.5 all-reduce.10
  379.6 68.5 all-reduce.12
  484.7 44.5 reduce-scatter.2
  576.9 34.4 all-gather.6
  652.2 119.7 all-reduce.14
  775.9 313.5 reduce-scatter.4
where the time goes:
time: 2140 us; the launch traced here: 2120 us
  other arithmetic  1040 us (49%)
  waiting for transfers between devices  636 us (30%)
  local copies, waits for them, and re-layouts  233 us (11%)
  matrix products  125 us (6%)
  blocking collectives  73.5 us (3%)
    another operation x4, other arithmetic, orthonormal(): factor = jnp.linalg.cholesky(gram)  849 us
    reduce_scatter x1, waiting for transfers between devices, body(): lax.psum_scatter(stored_grads, 'dp', scatter_dimension=0, tiled=True)  266 us
    all_gather x1, waiting for transfers between devices, body(): lax.all_gather(masters[0].astype(jnp.bfloat16), 'dp', axis=0, tiled=True)  108 us
    another operation x3, other arithmetic, orthonormal(): jax.scipy.linalg.solve_triangular(factor, swap_last(weight_matrix), lower...  68.6 us
    psum x1, waiting for transfers between devices, body(): attn_total = lax.psum(contract_cols(attended_flat, w_out_side), 'tensor')  68.2 us
    psum x1, waiting for transfers between devices, body(): d_two = lax.psum(contract_cols(d_up, w_up), 'tensor')  68 us
    dot_general x9, matrix products, batch_prod(): return jnp.einsum('nij,njk->nik', left, right, precision=highest)  51.3 us
    unnamed x171, local copies, waits for them, and re-layouts  50.8 us
  transfers between devices with their start and end apart: 8, of which 8 were waited for; matrix products, arithmetic and copies ran while one was open for 6% of the time, Pallas kernels for 0%

commit v1 on v0

--- a/solution.py
+++ b/solution.py
@@ -1,12 +1,17 @@
+import functools
 import math
 
 import jax
 import jax.numpy as jnp
 from jax import lax
+from jax.experimental import pallas as pl
+from jax.experimental.pallas import tpu as pltpu
 from jax.sharding import PartitionSpec as P
 
 HD = 64
 STEP = 10
+F32 = jnp.float32
+BF16 = jnp.bfloat16
 
 
 highest = lax.Precision.HIGHEST
@@ -140,48 +145,110 @@
     return heads.transpose(1, 0, 2).reshape(heads.shape[1], -1)
 
 
-def batch_prod(left, right):
-    return jnp.einsum("nij,njk->nik", left, right, precision=highest)
-
-
-def swap_last(weight_matrix):
-    return jnp.swapaxes(weight_matrix, -1, -2)
-
-
-def orthonormal(weight_matrix):
-    gram = batch_prod(swap_last(weight_matrix), weight_matrix)
-    factor = jnp.linalg.cholesky(gram)
-    solved = jax.scipy.linalg.solve_triangular(factor, swap_last(weight_matrix), lower=True)
-    return swap_last(solved)
-
-
-def soap_update(grad, master, first, second, left_stats, right_stats, left_basis, right_basis):
-    new_left = beta_stats * left_stats + (1.0 - beta_stats) * batch_prod(grad, swap_last(grad))
-    new_right = beta_stats * right_stats + (1.0 - beta_stats) * batch_prod(swap_last(grad), grad)
-    rotated = batch_prod(batch_prod(swap_last(left_basis), grad), right_basis)
-    new_first = beta_one * first + (1.0 - beta_one) * rotated
-    new_second = beta_two * second + (1.0 - beta_two) * rotated * rotated
-    direction = (
-        new_first
-        / (1.0 - beta_one**STEP)
-        / (jnp.sqrt(new_second / (1.0 - beta_two**STEP)) + adam_eps)
-    )
-    moved = batch_prod(batch_prod(left_basis, direction), swap_last(right_basis))
-    new_master = master - learn_rate * (moved + weight_decay * master)
-    count = grad.shape[0]
-    both_sides = jnp.concatenate(
-        [batch_prod(new_left, left_basis), batch_prod(new_right, right_basis)], axis=0
-    )
-    renewed = orthonormal(both_sides)
-    return (
-        new_first,
-        new_second,
-        new_master,
-        new_left,
-        new_right,
-        renewed[:count],
-        renewed[count:],
-    )
+def split3(v):
+    hi = v.astype(BF16)
+    return hi, (v - hi.astype(F32)).astype(BF16)
+
+def prod(left, right, dims):
+    lh, ll = left
+    rh, rl = right
+    spec = (dims, ((), ()))
+    def one(a, b):
+        return lax.dot_general(a, b, spec, preferred_element_type=F32)
+    return one(lh, rh) + (one(lh, rl) + one(ll, rh))
+
+NN = ((1,), (0,))
+NT = ((1,), (1,))
+TN = ((0,), (0,))
+
+def soap_kernel(count, chunk, block, g_ref, m_ref, f_ref, s_ref, l_ref, r_ref, ql_ref, qr_ref,
+                nf_ref, ns_ref, nm_ref, nl_ref, nr_ref, bl_ref, br_ref, a_scr, t_scr):
+    step = pl.program_id(0)
+    tiles = block // 8
+    for c in range(chunk):
+        g = g_ref[c]
+        ql, qr = split3(ql_ref[c]), split3(qr_ref[c])
+        gs = split3(g)
+        gt = split3(g.T)
+        new_left = beta_stats * l_ref[c] + (1.0 - beta_stats) * prod(gs, gs, NT)
+        new_right = beta_stats * r_ref[c] + (1.0 - beta_stats) * prod(gt, gt, NT)
+        nl_ref[c] = new_left
+        nr_ref[c] = new_right
+        half = prod(gt, ql, NN)
+        rot = prod(split3(half.T), qr, NN)
+        first = beta_one * f_ref[c] + (1.0 - beta_one) * rot
+        second = beta_two * s_ref[c] + (1.0 - beta_two) * rot * rot
+        nf_ref[c] = first
+        ns_ref[c] = second
+        direction = first / (1.0 - beta_one**STEP) / (
+            jnp.sqrt(second / (1.0 - beta_two**STEP)) + adam_eps)
+        moved = prod(split3(prod(ql, split3(direction), NN)), qr, NT)
+        master = m_ref[c]
+        nm_ref[c] = master - learn_rate * (moved + weight_decay * master)
+        a_scr[0, step * chunk + c] = prod(split3(new_left), ql, NN)
+        a_scr[1, step * chunk + c] = prod(split3(new_right), qr, NN)
+
+    @pl.when(step == pl.num_programs(0) - 1)
+    def _():
+        def bring(i, _):
+            for s in range(2):
+                slab = a_scr[s, :, pl.ds(i, 1), :].reshape(128, block)
+                t_scr[s, i] = slab.T
+            return 0
+        lax.fori_loop(0, block, bring, 0, unroll=4)
+        sub = lax.broadcasted_iota(jnp.int32, (8, 128), 0)
+        norms = [[None] * tiles, [None] * tiles]
+        for kt in range(tiles):
+            def one(kk, carry):
+                k = kt * 8 + kk
+                acc = [[jnp.zeros((8, 128), F32) for _ in range(kt, tiles)] for _ in range(2)]
+                for i in range(block):
+                    for s in range(2):
+                        row = jnp.broadcast_to(t_scr[s, i, pl.ds(k, 1), :], (8, 128))
+                        for j in range(kt, tiles):
+                            acc[s][j - kt] += row * t_scr[s, i, 8 * j : 8 * j + 8, :]
+                out = []
+                for s in range(2):
+                    here = sub == kk
+                    size = jnp.sum(jnp.where(here, acc[s][0], 0.0), axis=0, keepdims=True)
+                    size = jnp.broadcast_to(size, (8, 128))
+                    inv = 1.0 / size
+                    acc[s] = [v * inv for v in acc[s]]
+                    acc[s][0] = jnp.where(sub > kk, acc[s][0], 0.0)
+                    out.append(jnp.where(here, size, carry[s]))
+                for i in range(block):
+                    for s in range(2):
+                        row = jnp.broadcast_to(t_scr[s, i, pl.ds(k, 1), :], (8, 128))
+                        for j in range(kt, tiles):
+                            t_scr[s, i, 8 * j : 8 * j + 8, :] -= row * acc[s][j - kt]
+                return tuple(out)
+            res = lax.fori_loop(0, 8, one, (jnp.ones((8, 128), F32),) * 2)
+            for s in range(2):
+                norms[s][kt] = lax.rsqrt(res[s])
+        scale = [jnp.concatenate(norms[s], axis=0) for s in range(2)]
+        def back(i, _):
+            for s, ref in ((0, bl_ref), (1, br_ref)):
+                done = (t_scr[s, i] * scale[s]).T
+                ref[:, pl.ds(i, 1), :] = done[:count].reshape(count, 1, block)
+            return 0
+        lax.fori_loop(0, block, back, 0, unroll=4)
+
+def soap(g, m, f, s, l, r, ql, qr):
+    count, block = g.shape[0], g.shape[-1]
+    chunk = math.gcd(count, 8)
+    spec = pl.BlockSpec((chunk, block, block), lambda i: (i, 0, 0))
+    whole = pl.BlockSpec((count, block, block), lambda i: (0, 0, 0))
+    shape = jax.ShapeDtypeStruct(g.shape, F32)
+    return pl.pallas_call(
+        functools.partial(soap_kernel, count, chunk, block),
+        grid=(count // chunk,),
+        in_specs=[spec] * 8,
+        out_specs=[spec] * 5 + [whole] * 2,
+        out_shape=[shape] * 7,
+        scratch_shapes=[pltpu.VMEM((2, 128, block, block), F32), pltpu.VMEM((2, block, block, 128), F32)],
+        compiler_params=pltpu.CompilerParams(vmem_limit_bytes=48 * 2**20),
+        name="soap",
+    )(g, m, f, s, l, r, ql, qr)
 
 
 def norm_update(grad, master, first, second):
@@ -373,7 +440,7 @@
         lax.psum_scatter(stored_grads, "dp", scatter_dimension=0, tiled=True),
         lax.psum_scatter(norm_grads, "dp", scatter_dimension=0, tiled=True),
     )
-    new_first, new_second, new_master, new_left, new_right, left_next, right_next = soap_update(
+    new_first, new_second, new_master, new_left, new_right, left_next, right_next = soap(
         own_grads,
         masters[0],
         first_moment[0],

time: 2140 us -> 1210 us (0.57)
  other arithmetic: 1040 us -> 112 us
  Pallas kernels: 0 us -> 85.7 us
  matrix products: 125 us -> 63.8 us
    another operation x13 -> x6, other arithmetic: 927 us -> 10.1 us  [the longest x4 849 us: orthonormal(): factor = jnp.linalg.cholesky(gram)]
    pallas_call x0 -> x1, Pallas kernels: none -> 85.7 us  [soap(): pl.pallas_call(functools.partial(soap_kernel, count, chunk, block), grid=...]
    dot_general x9 -> x0, matrix products: 51.3 us -> none  [batch_prod(): return jnp.einsum('nij,njk->nik', left, right, precision=highest)]
    another operation x13 -> x11, local copies, waits for them, and re-layouts: 48.9 us -> 37.5 us
    unnamed x171 -> x157, local copies, waits for them, and re-layouts: 50.8 us -> 55.1 us
  transfers between devices with their start and end apart: 8 -> 8, of which waited for: 8 -> 8; matrix products, arithmetic and copies ran while one was open for 6% -> 11% of each run, Pallas kernels for 0% -> 0%
where the time goes in v1:
time: 1210 us; the launch traced here: 1200 us
  waiting for transfers between devices  636 us (53%)
  local copies, waits for them, and re-layouts  212 us (18%)
  other arithmetic  112 us (9%)
  Pallas kernels  85.7 us (7%)
  blocking collectives  73.2 us (6%)
  matrix products  63.8 us (5%)
  between operations  16.1 us (1%)
    reduce_scatter x1, waiting for transfers between devices, body(): lax.psum_scatter(stored_grads, 'dp', scatter_dimension=0, tiled=True)  266 us
    all_gather x1, waiting for transfers between devices, body(): lax.all_gather(masters[0].astype(jnp.bfloat16), 'dp', axis=0, tiled=True)  108 us
    pallas_call x1, Pallas kernels, soap(): pl.pallas_call(functools.partial(soap_kernel, count, chunk, block), grid=...  85.7 us
    psum x1, waiting for transfers between devices, body(): attn_total = lax.psum(contract_cols(attended_flat, w_out_side), 'tensor')  68.2 us
    psum x1, waiting for transfers between devices, body(): d_two = lax.psum(contract_cols(d_up, w_up), 'tensor')  68 us
    unnamed x157, local copies, waits for them, and re-layouts  55.1 us
    psum x1, waiting for transfers between devices, spread(): return lax.psum(jnp.where(mine, shard, jnp.zeros_like(shard)), axis)  46.8 us
    reduce_scatter x1, waiting for transfers between devices, attend_back(): lax.psum_scatter(pen_terms, 'tensor', scatter_dimension=0, tiled=True)  44.5 us
  transfers between devices with their start and end apart: 8, of which 8 were waited for; matrix products, arithmetic and copies ran while one was open for 11% of the time, Pallas kernels for 0%

profile of v1, /device:TPU:0, one launch (start us, length us, event | category | flops | bytes accessed | tf_op | source)
XLA Modules:
  0.0 1200.0 jit_solution(8667498522134779288)
XLA Ops:
  13.7 28.1 %all-gather.1 = bf16[8,1,384]{2,1,0:T(2,128)(2,1)S(1)} all-gather(bf16[1,1,384]{2,1,0:T(2,128)(2,1)S(1)} %reshape.296), channel_id=1, replica_groups=mesh['dp'=8,'tensor'=4] {'dp'}, dimensions={0}, use_global_device_ids=true | all-gather | bytes 6912 | tf_op jit(solution)/shard_map/all_gather | solution.py:293
  45.9 108.3 %all-gather.5.cloned.1.call-done = bf16[768,48,48]{2,1,0:T(8,128)(2,1)} async-done(((bf16[96,48,48]{2,1,0:T(8,128)(2,1)}), bf16[768,48,48]{2,1,0:T(8,128)(2,1)}) %all-gather.5.cloned.1.call-update) | async-done | bytes 3538960 | tf_op jit(solution)/shard_map/all_gather | solution.py:292
  154.2 9.8 gather_fusion
  164.0 9.5 fusion.14
  173.6 13.8 %reshape.261 = bf16[768,2304]{1,0:T(8,128)(2,1)} reshape(bf16[16,48,48,48]{3,2,1,0:T(8,128)(2,1)} %fusion.14) | data formatting | bytes 7077888 | tf_op jit(solution)/shard_map/reshape | solution.py:67
  196.5 26.8 %conditional.2 = (bf16[1024,1024]{1,0:T(8,128)(2,1)S(1)}) conditional(s32[]{:T(128)} %convert_element_type.90, () %tuple.47, (f32[3,1024,1024]{1,2,0:T(8,128)}, pred[1024,1024]{1,0:T(8,128)(4,1)S(1)}) %tuple.48), branch_computations={%region_3.4_spmd, %region_4.7_spmd} | conditional | flops 143719424 | bytes 74680360 | solution.py:323
  196.7 12.6 %copy.156 = f32[3,1024,1024]{2,1,0:T(8,128)} copy(f32[3,1024,1024]{1,2,0:T(8,128)} %get-tuple-element.235) | data formatting | bytes 25165824 | tf_op jit(solution)/shard_map
  226.9 46.8 %all-reduce.9.cloned.1.call-done = bf16[1024,1024]{1,0:T(8,128)(2,1)} async-done(((bf16[1024,1024]{1,0:T(8,128)(2,1)}), bf16[1024,1024]{1,0:T(8,128)(2,1)}) %all-reduce.9.cloned.1.call-update) | async-done | bytes 2097168 | tf_op jit(solution)/shard_map/while/body/eval_jaxpr/psum | solution.py:30
  296.0 68.2 %all-reduce.11.cloned.1.call-done = f32[1024,768]{1,0:T(8,128)} async-done(((f32[1024,768]{1,0:T(8,128)}), f32[1024,768]{1,0:T(8,128)}) %all-reduce.11.cloned.1.call-update) | async-done | bytes 3145744 | tf_op jit(solution)/shard_map/psum | solution.py:343
  380.1 68.0 %all-reduce.13.cloned.1.call-done = f32[1024,768]{1,0:T(8,128)} async-done(((f32[1024,768]{1,0:T(8,128)}), f32[1024,768]{1,0:T(8,128)}) %all-reduce.13.cloned.1.call-update) | async-done | bytes 3145744 | tf_op jit(solution)/shard_map/psum | solution.py:361
  456.7 10.4 multiply_reduce_fusion
  469.3 12.7 %fusion.88 = (f32[1024,1024]{0,1:T(8,128)S(1)}, f32[3,1024,1024]{1,2,0:T(8,128)}) fusion(f32[3,1024,1024]{1,2,0:T(8,128)} %get-tuple-element.294, f32[3,1024]{1,0:T(4,128)S(1)} %get-tuple-element.293, f32[3,1024,1024]{1,2,0:T(8,128)S(1)} %bitcast.172, f32[3,1024]{1,0:T(4,128)S(1)} %log_add_fusion), kind=kLoop, calls=%fused_computation.163 | loop fusion | flops 11534336 | bytes 41967616 | tf_op jit(solution)/shard_map/while/body/eval_jaxpr/reduce_sum | solution.py:382
  484.7 44.5 %reduce-scatter.3.cloned.1.call-done = f32[256,1024]{0,1:T(8,128)} async-done(((f32[1024,1024]{0,1:T(8,128)}), f32[256,1024]{0,1:T(8,128)}) %reduce-scatter.3.cloned.1.call-update) | async-done | bytes 1048592 | tf_op jit(solution)/shard_map/while/body/eval_jaxpr/reduce_scatter | solution.py:383
  529.2 9.3 rev.6
  611.3 25.1 %conditional.3 = (bf16[1024,1024]{1,0:T(8,128)(2,1)}) conditional(s32[]{:T(128)} %convert_element_type.90, (f32[1024,1024]{0,1:T(8,128)}) %tuple.67, (f32[3,1024,1024]{1,2,0:T(8,128)}, f32[1024,1024]{1,0:T(8,128)}, pred[1024,1024]{1,0:T(8,128)(4,1)}, f32[1024,1024]{0,1:T(8,128)}) %tuple.120), branch_computations={%region_25.26_spmd, %region_26.27_spmd} | conditional | flops 8388608 | bytes 49283080 | solution.py:398
  616.6 12.6 %copy.164 = f32[3,1024,1024]{2,1,0:T(8,128)} copy(f32[3,1024,1024]{1,2,0:T(8,128)} %get-tuple-element.237) | data formatting | bytes 25165824 | tf_op jit(solution)/shard_map
  662.7 15.8 %reshape.274 = f32[16,48,48,48]{1,0,3,2:T(8,128)} reshape(f32[768,2304]{0,1:T(8,128)} %pad_maximum_fusion) | data formatting | bytes 14155776 | tf_op jit(solution)/shard_map/reshape | solution.py:75
  678.6 18.8 %copy.190 = f32[16,48,48,48]{3,2,1,0:T(8,128)} copy(f32[16,48,48,48]{2,0,3,1:T(8,128)} %bitcast.176) | data formatting | bytes 14155776 | tf_op jit(solution)/shard_map/reshape | solution.py:77
  697.4 15.0 %gather_fusion.1 = f32[768,48,48]{2,1,0:T(8,128)} fusion(f32[768,48,48]{2,1,0:T(8,128)} %bitcast.175, s32[1024]{0:T(1024)S(1)} %copy-done.47), kind=kCustom, calls=%fused_computation.1 | custom fusion | bytes 14158848 | tf_op jit(solution)/shard_map/jit(_take)/gather | solution.py:435
  712.3 15.9 %broadcast_select_fusion = f32[768,48,48]{2,1,0:T(8,128)} fusion(f32[768,48,48]{2,1,0:T(8,128)} %gather_fusion.1, pred[768]{0:T(1024)(128)(4,1)S(1)} %copy-done.52), kind=kLoop, calls=%fused_computation.30 | loop fusion | flops 1769472 | bytes 14156544 | tf_op jit(solution)/shard_map/jit(_take)/select_n | solution.py:435
  747.2 24.6 %all-reduce.15.cloned.1.call-done = (f32[1024,768]{1,0:T(8,128)}, f32[1024,768]{1,0:T(8,128)}) async-done(((f32[1024,768]{1,0:T(8,128)}, f32[1024,768]{1,0:T(8,128)}), (f32[1024,768]{1,0:T(8,128)}, f32[1024,768]{1,0:T(8,128)})) %all-reduce.15.cloned.1.call-update) | async-done | bytes 6291472 | tf_op jit(solution)/shard_map/psum | solution.py:349
  775.1 39.3 %all-reduce.2 = f32[3072]{0:T(1024)S(1)} all-reduce(f32[3072]{0:T(1024)S(1)} %pad_maximum_fusion.15), channel_id=5, replica_groups=mesh['dp'=8,'tensor'=4] {'dp'}, use_global_device_ids=true, to_apply=%region_36.37.clone | all-reduce | flops 3072 | bytes 24576
  822.6 266.3 %reduce-scatter.5.cloned.1.call-done.g_ref = f32[96,48,48]{2,1,0:T(8,128)} async-done(((f32[768,48,48]{2,1,0:T(8,128)}), f32[96,48,48]{2,1,0:T(8,128)}) %reduce-scatter.5.cloned.1.call-update) | async-done | bytes 884752 | tf_op jit(solution)/shard_map/reduce_scatter | solution.py:440
  1088.9 85.7 %soap.1 = (f32[96,48,48]{2,1,0:T(8,128)S(1)}, f32[96,48,48]{2,1,0:T(8,128)S(1)}, f32[96,48,48]{2,1,0:T(8,128)}, f32[96,48,48]{2,1,0:T(8,128)}, f32[96,48,48]{2,1...) custom-call(f32[96,48,48]{2,1,0:T(8,128)} %reduce-scatter.5.cloned.1.call-done.g_ref, f32[96,48,48]{2,1,0:T(8,128)} %bitcast.178, ...), custom_call_target="tpu_custom_call" | custom-call | tf_op jit(solution)/shard_map/soap/pallas_call | solution.py:242
  (274 shorter events, 253.4 us)
Async XLA Ops:
  7.2 147.0 %all-gather.5.cloned.1.call-start = ((), (), s32[]{:S(2)}) async-start(), calls=%async_computation.2 | async-start | bytes 10616832 | tf_op jit(solution)/shard_map/all_gather | solution.py:292
  10.2 31.8 %copy-start.5 = (bf16[1,1024,768]{2,1,0:T(8,128)(2,1)S(1)}, bf16[1,1024,768]{2,1,0:T(8,128)(2,1)}, u32[]{:S(2)}) copy-start(bf16[1,1024,768]{2,1,0:T(8,128)(2,1)} %param.20) | copy-start | bytes 4718596
  10.2 32.7 %copy-start.46 = (s32[1,1024]{1,0:T(1,128)S(1)}, s32[1,1024]{1,0:T(1,128)}, u32[]{:S(2)}) copy-start(s32[1,1024]{1,0:T(1,128)} %param.21) | copy-start | bytes 12292
  13.2 260.5 %all-reduce.9.cloned.1.call-start = ((), (), s32[]{:S(2)}) async-start(), calls=%async_computation.3 | async-start | bytes 4194304 | tf_op jit(solution)/shard_map/while/body/eval_jaxpr/psum | solution.py:30
  13.6 28.6 %copy-start.45 = (s32[768]{0:T(1024)}, s32[768]{0:T(1024)S(1)}, u32[]{:S(2)}) copy-start(s32[768]{0:T(1024)S(1)} %get-tuple-element.287) | copy-start | bytes 9220
  41.9 145.5 %copy-start.53 = (f32[768]{0:T(1024)}, f32[768]{0:T(1024)S(1)}, u32[]{:S(2)}) copy-start(f32[768]{0:T(1024)S(1)} %reshape.300) | copy-start | bytes 9220
  41.9 145.5 %copy-start.40 = (f32[768]{0:T(1024)}, f32[768]{0:T(1024)S(1)}, u32[]{:S(2)}) copy-start(f32[768]{0:T(1024)S(1)} %reshape.299) | copy-start | bytes 9220
  42.2 145.1 %copy-start.36 = (f32[1024]{0:T(1024)}, f32[1024]{0:T(1024)S(1)}, u32[]{:S(2)}) copy-start(f32[1024]{0:T(1024)S(1)} %broadcast_multiply_fusion.6) | copy-start | bytes 12292
  42.9 144.5 %copy-start.42 = (f32[1024]{0:T(1024)}, f32[1024]{0:T(1024)S(1)}, u32[]{:S(2)}) copy-start(f32[1024]{0:T(1024)S(1)} %add_rsqrt_fusion.1) | copy-start | bytes 12292
  45.9 150.6 %copy-start.11 = (pred[1024,1024]{1,0:T(8,128)(4,1)}, pred[1024,1024]{1,0:T(8,128)(4,1)S(1)}, u32[]{:S(2)}) copy-start(pred[1024,1024]{1,0:T(8,128)(4,1)S(1)} %get-tuple-element.292) | copy-start | bytes 3145732
  190.1 96.4 %copy-start.19 = (bf16[1024,192]{0,1:T(8,128)(2,1)}, bf16[1024,192]{0,1:T(8,128)(2,1)S(1)}, u32[]{:S(2)}) copy-start(bf16[1024,192]{0,1:T(8,128)(2,1)S(1)} %get-tuple-element.289) | copy-start | bytes 1179652
  224.8 139.4 %all-reduce.11.cloned.1.call-start = ((), (), s32[]{:S(2)}) async-start(), calls=%async_computation.4 | async-start | bytes 6291456 | tf_op jit(solution)/shard_map/psum | solution.py:343
  295.6 152.5 %all-reduce.13.cloned.1.call-start = ((), (), s32[]{:S(2)}) async-start(), calls=%async_computation.5 | async-start | bytes 6291456 | tf_op jit(solution)/shard_map/psum | solution.py:361
  379.4 149.9 %reduce-scatter.3.cloned.1.call-start = ((), (), s32[]{:S(2)}) async-start(), calls=%async_computation.6 | async-start | bytes 5242880 | tf_op jit(solution)/shard_map/while/body/eval_jaxpr/reduce_scatter | solution.py:383
  484.5 126.8 %all-gather.7.cloned.1.call-start = ((), (), s32[]{:S(2)}) async-start(), calls=%async_computation.7 | async-start | bytes 5242880 | tf_op jit(solution)/shard_map/while/body/eval_jaxpr/all_gather | solution.py:390
  576.6 195.2 %all-reduce.15.cloned.1.call-start = ((), (), s32[]{:S(2)}) async-start(), calls=%async_computation.9 | async-start | bytes 12582912 | tf_op jit(solution)/shard_map/psum | solution.py:349
  651.9 437.0 %reduce-scatter.5.cloned.1.call-start = ((), (), s32[]{:S(2)}) async-start(), calls=%async_computation.8 | async-start | bytes 21233664 | tf_op jit(solution)/shard_map/reduce_scatter | solution.py:440
  678.6 18.8 %copy-start.47 = (s32[1024]{0:T(1024)S(1)}, s32[1024]{0:T(1024)}, u32[]{:S(2)}) copy-start(s32[1024]{0:T(1024)} %pad_clamp_fusion) | copy-start | bytes 12292
  697.4 15.0 %copy-start.52 = (pred[768]{0:T(1024)(128)(4,1)S(1)}, pred[768]{0:T(1024)(128)(4,1)}, u32[]{:S(2)}) copy-start(pred[768]{0:T(1024)(128)(4,1)} %compare_and_fusion.2) | copy-start | bytes 2308
  746.0 29.1 %copy-start.48 = (f32[768]{0:T(1024)S(1)}, f32[768]{0:T(1024)}, u32[]{:S(2)}) copy-start(f32[768]{0:T(1024)} %get-tuple-element.255) | copy-start | bytes 9220
  746.0 29.1 %copy-start.49 = (f32[768]{0:T(1024)S(1)}, f32[768]{0:T(1024)}, u32[]{:S(2)}) copy-start(f32[768]{0:T(1024)} %get-tuple-element.262) | copy-start | bytes 9220
  746.0 68.5 %copy-start.51 = (f32[384]{0:T(512)S(1)}, f32[384]{0:T(512)}, u32[]{:S(2)}) copy-start(f32[384]{0:T(512)} %param.31) | copy-start | bytes 4612
  746.0 68.5 %copy-start.55 = (f32[384]{0:T(512)S(1)}, f32[384]{0:T(512)}, u32[]{:S(2)}) copy-start(f32[384]{0:T(512)} %param.33) | copy-start | bytes 4612
  746.0 68.5 %copy-start.56 = (f32[384]{0:T(512)S(1)}, f32[384]{0:T(512)}, u32[]{:S(2)}) copy-start(f32[384]{0:T(512)} %param.32) | copy-start | bytes 4612
  (55 other events, 225.4 us)
Sparse Core Ops, SparseCore 0:
  13.3 140.8 all-gather.4
  224.9 48.6 all-reduce.8
  295.7 68.5 all-reduce.10
  379.5 68.5 all-reduce.12
  484.6 44.5 reduce-scatter.2
  576.7 34.4 all-gather.6
  652.1 119.7 all-reduce.14
  775.7 313.1 reduce-scatter.4

commit v2 on v1

--- a/solution.py
+++ b/solution.py
@@ -25,25 +25,6 @@
 adam_eps = 1e-08
 
 
-def spread(shard, axis, root):
-    mine = lax.axis_index(axis) == root
-    return lax.psum(jnp.where(mine, shard, jnp.zeros_like(shard)), axis)
-
-
-def entering(part, axis, combine, identity):
-    count = lax.axis_size(axis)
-    place = lax.axis_index(axis)
-    ahead = count - 1 - place
-    gathered = lax.all_gather(part, axis)
-    state = jnp.zeros_like(part) + jnp.asarray(identity, part.dtype)
-
-    def one(lap, state):
-        source = count - 1 - lap
-        return combine(state, lax.dynamic_index_in_dim(gathered, source, 0, False))
-
-    return lax.fori_loop(0, ahead, one, state)
-
-
 def shift_for(length):
     return math.log(length / 8.0)
 
@@ -58,24 +39,463 @@
     return (slots, inverse)
 
 
-def blocks_to_matrix(blocks, grid_rows):
+MESH = pl.DeviceIdType.MESH
+VM = pl.BlockSpec(memory_space=pltpu.VMEM)
+MIB = 2**20
+
+
+def tiles_up(value):
+    return -(-value // 128) * 128
+
+
+def remote(src, dst, send, recv, where):
+    return pltpu.make_async_remote_copy(
+        src_ref=src, dst_ref=dst, send_sem=send, recv_sem=recv, device_id=where, device_id_type=MESH
+    )
+
+
+def greet(devices):
+    barrier = pltpu.get_barrier_semaphore()
+    for device in devices:
+        pl.semaphore_signal(barrier, inc=1, device_id=device, device_id_type=MESH)
+    pl.semaphore_wait(barrier, len(devices))
+
+
+def line_greet(dp, t, m):
+    place, side = dp // 2, lax.rem(dp, 2)
+    barrier = pltpu.get_barrier_semaphore()
+    pl.semaphore_signal(barrier, inc=1, device_id=(place * 2 + 1 - side, t), device_id_type=MESH)
+
+    @pl.when(place > 0)
+    def _():
+        pl.semaphore_signal(barrier, inc=1, device_id=(dp - 2, t), device_id_type=MESH)
+
+    @pl.when(place < m - 1)
+    def _():
+        pl.semaphore_signal(barrier, inc=1, device_id=(dp + 2, t), device_id_type=MESH)
+
+    ends = (place == 0).astype(jnp.int32) + (place == m - 1).astype(jnp.int32)
+    pl.semaphore_wait(barrier, 3 - ends)
+
+
+def gather_kernel(n, count, block, wide, norm_rows, m_ref, norm_ref, u_ref, nout_ref, held, send_sem, recv_sem):
+    m = n // 2
+    dp, t = lax.axis_index("dp"), lax.axis_index("tensor")
+    place, side = dp // 2, lax.rem(dp, 2)
+    pair = (place * 2 + 1 - side, t)
+    for k in range(count):
+        held[dp, :, k * block : (k + 1) * block] = m_ref[k].astype(BF16)
+    if wide > count * block:
+        held[dp, :, count * block : wide] = jnp.zeros((block, wide - count * block), BF16)
+    held[dp, :, wide : wide + 128] = jnp.concatenate(
+        [norm_ref[...], jnp.zeros((block - norm_rows, 128), F32)], axis=0
+    ).astype(BF16)
+    line_greet(dp, t, m)
+
+    def send(source, way, where):
+        return remote(held.at[source], held.at[source], send_sem.at[source, way], recv_sem.at[source], where)
+
+    def unpack(source):
+        for k in range(count):
+            u_ref[source * count + k] = held[source, :, k * block : (k + 1) * block]
+        nout_ref[source] = held[source, :16, wide : wide + 128]
+
+    def spread(source, left, right):
+        send(source, 2, pair).start()
+
+        @pl.when(left)
+        def _():
+            send(source, 0, (dp - 2, t)).start()
+
+        @pl.when(right)
+        def _():
+            send(source, 1, (dp + 2, t)).start()
+
+    def spread_done(source, left, right):
+        send(source, 2, pair).wait_send()
+
+        @pl.when(left)
+        def _():
+            send(source, 0, (dp - 2, t)).wait_send()
+
+        @pl.when(right)
+        def _():
+            send(source, 1, (dp + 2, t)).wait_send()
+
+    spread(dp, place > 0, place < m - 1)
+    unpack(dp)
+
+    def one(hop, _):
+        @pl.when(place - hop >= 0)
+        def _():
+            source = dp - 2 * hop
+            send(source, 2, pair).wait_recv()
+            spread(source, False, place < m - 1)
+
+        @pl.when(place + hop < m)
+        def _():
+            source = dp + 2 * hop
+            send(source, 2, pair).wait_recv()
+            spread(source, place > 0, False)
+
+        @pl.when(place - hop >= 0)
+        def _():
+            unpack(dp - 2 * hop)
+
+        @pl.when(place + hop < m)
+        def _():
+            unpack(dp + 2 * hop)
+
+        return 0
+
+    lax.fori_loop(1, m, one, 0)
+
+    def other(step, _):
+        source = step * 2 + 1 - side
+        send(source, 2, pair).wait_recv()
+        unpack(source)
+        return 0
+
+    lax.fori_loop(0, m, other, 0)
+
+    def finish(step, _):
+        source = step * 2 + side
+        spread_done(
+            source,
+            (place > 0) & (step >= place),
+            (place < m - 1) & (step <= place),
+        )
+        return 0
+
+    lax.fori_loop(0, m, finish, 0)
+
+
+def gather_masters(masters, norm, n):
+    count, block = masters.shape[0], masters.shape[-1]
+    wide = tiles_up(count * block)
+    norm_rows = -(-norm.shape[0] // 128)
+    norm_tile = jnp.pad(norm, (0, norm_rows * 128 - norm.shape[0])).reshape(norm_rows, 128)
+    blocks, norms = pl.pallas_call(
+        functools.partial(gather_kernel, n, count, block, wide, norm_rows),
+        out_shape=[
+            jax.ShapeDtypeStruct((n * count, block, block), BF16),
+            jax.ShapeDtypeStruct((n, 16, 128), BF16),
+        ],
+        in_specs=[VM, VM],
+        out_specs=[VM, VM],
+        scratch_shapes=[
+            pltpu.VMEM((n, block, wide + 128), BF16),
+            pltpu.SemaphoreType.DMA((n, 3)),
+            pltpu.SemaphoreType.DMA((n,)),
+        ],
+        compiler_params=pltpu.CompilerParams(collective_id=1, has_side_effects=True, vmem_limit_bytes=10 * MIB),
+        name="gather_masters",
+    )(masters, norm_tile)
+    return blocks, norms.reshape(n, 16 * 128)[:, : norm.shape[0]].reshape(-1)
+
+
+def assemble_kernel(rows, cols, block, slot_ref, u_ref, w_ref):
+    def one(row, _):
+        strip = jnp.concatenate([u_ref[slot_ref[row * cols + c]] for c in range(cols)], axis=1)
+        w_ref[pl.ds(pl.multiple_of(row * block, block), block), :] = strip
+        return 0
+
+    lax.fori_loop(0, rows, one, 0)
+
+
+def assemble(slots, blocks, rows):
     block = blocks.shape[-1]
-    grid_cols = blocks.shape[0] // grid_rows
-    return (
-        blocks.reshape(grid_rows, grid_cols, block, block)
-        .transpose(0, 2, 1, 3)
-        .reshape(grid_rows * block, grid_cols * block)
-    )
-
-
-def matrix_to_blocks(weight_matrix, block):
-    grid_rows = weight_matrix.shape[0] // block
-    grid_cols = weight_matrix.shape[1] // block
-    return (
-        weight_matrix.reshape(grid_rows, block, grid_cols, block)
-        .transpose(0, 2, 1, 3)
-        .reshape(grid_rows * grid_cols, block, block)
-    )
+    cols = blocks.shape[0] // rows
+    return pl.pallas_call(
+        functools.partial(assemble_kernel, rows, cols, block),
+        out_shape=jax.ShapeDtypeStruct((rows * block, cols * block), BF16),
+        in_specs=[pl.BlockSpec(memory_space=pltpu.SMEM), VM],
+        out_specs=VM,
+        compiler_params=pltpu.CompilerParams(vmem_limit_bytes=4 * MIB),
+        name="assemble",
+    )(slots, blocks)
+
+
+def disperse_kernel(rows, cols, block, n, count, wide, inverse_ref, g_ref, p_ref, u_scr):
+    def cut(row, _):
+        strip = g_ref[pl.ds(pl.multiple_of(row * block, block), block), :]
+        for c in range(cols):
+            u_scr[row * cols + c] = strip[:, c * block : (c + 1) * block].astype(BF16)
+        return 0
+
+    lax.fori_loop(0, rows, cut, 0)
+
+    def lay(d, _):
+        for k in range(count):
+            p_ref[d, :, k * block : (k + 1) * block] = u_scr[inverse_ref[d * count + k]]
+        if wide > count * block:
+            p_ref[d, :, count * block : wide] = jnp.zeros((block, wide - count * block), BF16)
+        return 0
+
+    lax.fori_loop(0, n, lay, 0)
+
+
+def disperse(inverse, grads, n, block):
+    rows, cols = grads.shape[0] // block, grads.shape[1] // block
+    count = rows * cols // n
+    wide = tiles_up(count * block)
+    return pl.pallas_call(
+        functools.partial(disperse_kernel, rows, cols, block, n, count, wide),
+        out_shape=jax.ShapeDtypeStruct((n, block, wide), BF16),
+        in_specs=[pl.BlockSpec(memory_space=pltpu.SMEM), VM],
+        out_specs=VM,
+        scratch_shapes=[pltpu.VMEM((rows * cols, block, block), BF16)],
+        compiler_params=pltpu.CompilerParams(vmem_limit_bytes=16 * MIB),
+        name="disperse",
+    )(inverse, grads)
+
+
+def scatter_kernel(n, p_ref, g_ref, xin, lin, rin, x_send, x_recv, l_send, l_recv, r_send, r_recv):
+    m = n // 2
+    dp, t = lax.axis_index("dp"), lax.axis_index("tensor")
+    place, side = dp // 2, lax.rem(dp, 2)
+    pair = (place * 2 + 1 - side, t)
+    line_greet(dp, t, m)
+
+    def across(q):
+        return remote(p_ref.at[q * 2 + 1 - side], xin.at[q], x_send.at[q], x_recv.at[q], pair)
+
+    def rightward(q, src):
+        return remote(src.at[q], lin.at[q], r_send.at[q], l_recv.at[q], (dp + 2, t))
+
+    def leftward(q, src):
+        return remote(src.at[q], rin.at[q], l_send.at[q], r_recv.at[q], (dp - 2, t))
+
+    def far_first(one):
+        def both(step, _):
+            hop = m - 1 - step
+
+            @pl.when(place + hop < m)
+            def _():
+                one(place + hop, True)
+
+            @pl.when((place - hop >= 0) & (hop > 0))
+            def _():
+                one(place - hop, False)
+
+            return 0
+
+        lax.fori_loop(0, m, both, 0)
+
+    far_first(lambda q, right: across(q).start())
+
+    def work(q, right):
+        across(q).wait_recv()
+        own = p_ref[q * 2 + side].astype(F32) + xin[q].astype(F32)
+        if right:
+            @pl.when((q > place) & (place > 0))
+            def _():
+                rightward(q, lin).wait_recv()
+                lin[q] = (own + lin[q].astype(F32)).astype(BF16)
+
+            @pl.when((q > place) & (place == 0))
+            def _():
+                lin[q] = own.astype(BF16)
+
+            @pl.when(q > place)
+            def _():
+                rightward(q, lin).start()
+
+            @pl.when((q == place) & (place > 0) & (place < m - 1))
+            def _():
+                rightward(q, lin).wait_recv()
+                leftward(q, rin).wait_recv()
+                g_ref[...] = own + (lin[q].astype(F32) + rin[q].astype(F32))
+
+            @pl.when((q == place) & (place == 0))
+            def _():
+                leftward(q, rin).wait_recv()
+                g_ref[...] = own + rin[q].astype(F32)
+
+            @pl.when((q == place) & (place == m - 1))
+            def _():
+                rightward(q, lin).wait_recv()
+                g_ref[...] = own + lin[q].astype(F32)
+        else:
+            @pl.when(place < m - 1)
+            def _():
+                leftward(q, rin).wait_recv()
+                rin[q] = (own + rin[q].astype(F32)).astype(BF16)
+
+            @pl.when(place == m - 1)
+            def _():
+                rin[q] = own.astype(BF16)
+
+            leftward(q, rin).start()
+
+    far_first(work)
+
+    def finish(q, _):
+        across(q).wait_send()
+
+        @pl.when(q > place)
+        def _():
+            rightward(q, lin).wait_send()
+
+        @pl.when(q < place)
+        def _():
+            leftward(q, rin).wait_send()
+
+        return 0
+
+    lax.fori_loop(0, m, finish, 0)
+
+
+def scatter_grads(packed):
+    n, block, wide = packed.shape
+    m = n // 2
+    return pl.pallas_call(
+        functools.partial(scatter_kernel, n),
+        out_shape=jax.ShapeDtypeStruct((block, wide), F32),
+        in_specs=[VM],
+        out_specs=VM,
+        scratch_shapes=[pltpu.VMEM((m, block, wide), BF16)] * 3 + [pltpu.SemaphoreType.DMA((m,))] * 6,
+        compiler_params=pltpu.CompilerParams(collective_id=2, has_side_effects=True, vmem_limit_bytes=16 * MIB),
+        name="scatter_grads",
+    )(packed)
+
+
+def total_kernel(pieces, x_ref, out_ref, near, mine, far, near_mine, near_far, *sems):
+    (a_send, a_recv, b_send, b_recv, c_send, c_recv, d_send, d_recv) = sems
+    dp, t = lax.axis_index("dp"), lax.axis_index("tensor")
+    up, core = t // 2, lax.rem(t, 2)
+    beside = (dp, up * 2 + 1 - core)
+    over = (dp, (1 - up) * 2 + core)
+    half = x_ref.shape[0] // 2
+    piece = half // pieces
+    greet([beside, over])
+
+    def rows(base, j):
+        return pl.ds(pl.multiple_of(base * half + j * piece, piece), piece)
+
+    def part(ref, j):
+        return ref.at[pl.ds(j * piece, piece)]
+
+    first = [
+        remote(x_ref.at[rows(1 - core, j)], part(near, j), a_send.at[j], a_recv.at[j], beside)
+        for j in range(pieces)
+    ]
+    cross = [remote(part(mine, j), part(far, j), b_send.at[j], b_recv.at[j], over) for j in range(pieces)]
+    share = [remote(part(mine, j), part(near_mine, j), c_send.at[j], c_recv.at[j], beside) for j in range(pieces)]
+    relay = [remote(part(far, j), part(near_far, j), d_send.at[j], d_recv.at[j], beside) for j in range(pieces)]
+    for j in range(pieces):
+        first[j].start()
+    for j in range(pieces):
+        here = pl.ds(j * piece, piece)
+        first[j].wait_recv()
+        mine[here] = (x_ref[rows(core, j)].astype(F32) + near[here].astype(F32)).astype(BF16)
+        cross[j].start()
+        share[j].start()
+    for j in range(pieces):
+        here = pl.ds(j * piece, piece)
+        cross[j].wait_recv()
+        relay[j].start()
+        out_ref[rows(core, j)] = mine[here].astype(F32) + far[here].astype(F32)
+    for j in range(pieces):
+        here = pl.ds(j * piece, piece)
+        share[j].wait_recv()
+        relay[j].wait_recv()
+        out_ref[rows(1 - core, j)] = near_mine[here].astype(F32) + near_far[here].astype(F32)
+    for j in range(pieces):
+        first[j].wait_send()
+        cross[j].wait_send()
+        share[j].wait_send()
+        relay[j].wait_send()
+
+
+def tensor_total(part, ident):
+    length, width = part.shape
+    pieces = 4
+    half = length // 2
+    return pl.pallas_call(
+        functools.partial(total_kernel, pieces),
+        out_shape=jax.ShapeDtypeStruct((length, width), F32),
+        in_specs=[VM],
+        out_specs=VM,
+        scratch_shapes=[pltpu.VMEM((half, width), BF16)] * 5 + [pltpu.SemaphoreType.DMA((pieces,))] * 8,
+        compiler_params=pltpu.CompilerParams(collective_id=ident, has_side_effects=True, vmem_limit_bytes=16 * MIB),
+        name="tensor_total",
+    )(part)
+
+
+def everyone(dp, t):
+    return [(dp, lax.rem(t + hop, 4)) for hop in (1, 2, 3)]
+
+
+def share_kernel(x_ref, out_ref, held, send_sem, recv_sem):
+    dp, t = lax.axis_index("dp"), lax.axis_index("tensor")
+    greet(everyone(dp, t))
+
+    @pl.when(t == 0)
+    def _():
+        copies = [remote(x_ref, held, send_sem.at[i], recv_sem, (dp, i + 1)) for i in range(3)]
+        for copy in copies:
+            copy.start()
+        out_ref[...] = x_ref[...]
+        for copy in copies:
+            copy.wait_send()
+
+    @pl.when(t > 0)
+    def _():
+        remote(x_ref, held, send_sem.at[0], recv_sem, (dp, 0)).wait_recv()
+        out_ref[...] = held[...]
+
+
+def share_first(first):
+    return pl.pallas_call(
+        share_kernel,
+        out_shape=jax.ShapeDtypeStruct(first.shape, first.dtype),
+        in_specs=[VM],
+        out_specs=VM,
+        scratch_shapes=[
+            pltpu.VMEM(first.shape, first.dtype),
+            pltpu.SemaphoreType.DMA((3,)),
+            pltpu.SemaphoreType.DMA,
+        ],
+        compiler_params=pltpu.CompilerParams(collective_id=3, has_side_effects=True),
+        name="share_first",
+    )(first)
+
+
+def collect_kernel(x_ref, out_ref, held, send_sem, recv_sem):
+    dp, t = lax.axis_index("dp"), lax.axis_index("tensor")
+    greet(everyone(dp, t))
+
+    @pl.when(t > 0)
+    def _():
+        copy = remote(x_ref, held.at[t - 1], send_sem, recv_sem.at[t - 1], (dp, 0))
+        copy.start()
+        out_ref[...] = jnp.zeros_like(out_ref)
+        copy.wait_send()
+
+    @pl.when(t == 0)
+    def _():
+        total = x_ref[...].astype(F32)
+        for i in range(3):
+            remote(x_ref, held.at[i], send_sem, recv_sem.at[i], (dp, i + 1)).wait_recv()
+            total = total + held[i].astype(F32)
+        out_ref[...] = total
+
+
+def collect_first(part):
+    return pl.pallas_call(
+        collect_kernel,
+        out_shape=jax.ShapeDtypeStruct(part.shape, F32),
+        in_specs=[VM],
+        out_specs=VM,
+        scratch_shapes=[
+            pltpu.VMEM((3,) + part.shape, BF16),
+            pltpu.SemaphoreType.DMA,
+            pltpu.SemaphoreType.DMA((3,)),
+        ],
+        compiler_params=pltpu.CompilerParams(collective_id=4, has_side_effects=True),
+        name="collect_first",
+    )(part)
 
 
 def normalize(rows):
@@ -122,10 +542,6 @@
 def later_sums(grads):
     suffix = jnp.cumsum(grads[::-1], axis=0)[::-1]
     return jnp.concatenate([suffix[1:], jnp.zeros((1, suffix.shape[1]), suffix.dtype)], axis=0)
-
-
-def append_column_block(earlier, latter):
-    return earlier + latter
 
 
 def split_heads(row_proj, rank_attn):
@@ -278,9 +694,9 @@
     norm_first,
     norm_second,
 ):
-    rows_here = inputs.shape[0]
     length = inputs.shape[1]
     width = inputs.shape[2]
+    n_dp = lax.axis_size("dp")
     tensor_count = lax.axis_size("tensor")
     rank_attn = width // tensor_count
     per_dev = masters.shape[1]
@@ -288,158 +704,95 @@
     scale = HD ** (-0.5)
     sel_shift = shift_for(length)
     tensor_index = lax.axis_index("tensor")
-    shared_blocks, shared_norms = (
-        lax.all_gather(masters[0].astype(jnp.bfloat16), "dp", axis=0, tiled=True),
-        lax.all_gather(norm_master.astype(jnp.bfloat16), "dp", axis=0, tiled=True),
-    )
+    blocks, shared_norms = gather_masters(masters[0], norm_master, n_dp)
     slots, inverse = block_slots(owner, per_dev)
-    weight_matrix = blocks_to_matrix(jnp.take(shared_blocks, slots, axis=0), width // block)
+    weight_matrix = assemble(slots, blocks, width // block)
     rank_mlp = (weight_matrix.shape[1] - 4 * rank_attn) // 2
-    w_project = weight_matrix[:, : 3 * rank_attn]
+    w_first = share_first(
+        jnp.concatenate([weight_matrix[:, :HD], weight_matrix[:, rank_attn : rank_attn + HD]], axis=1)
+    )
+    w_project = jnp.concatenate([weight_matrix[:, : 3 * rank_attn], w_first], axis=1)
     w_up = weight_matrix[:, 3 * rank_attn : 3 * rank_attn + rank_mlp]
     w_out_side = weight_matrix[:, 3 * rank_attn + rank_mlp : 4 * rank_attn + rank_mlp]
     w_down_side = weight_matrix[:, 4 * rank_attn + rank_mlp :]
-    norms = shared_norms.astype(jnp.float32).reshape(4, width)
-    tokens = inputs.reshape(rows_here * length, width).astype(jnp.float32)
+    norms = shared_norms.astype(F32).reshape(4, width)
+    tokens = inputs.reshape(length, width).astype(F32)
     plain_one, inverse_one = normalize(tokens)
-    normed_one = (plain_one * norms[0] + norms[1]).astype(jnp.bfloat16)
-    projected = jnp.dot(normed_one, w_project, preferred_element_type=jnp.float32).astype(
-        jnp.bfloat16
-    )
-    projection_rows = projected.reshape(rows_here, length, 3 * rank_attn)
-
-    def attention_single_row(packed):
-        row_proj, row_seg = packed
-        queries, keys, values = split_heads(row_proj, rank_attn)
-        raw = jnp.einsum("hqd,hkd->hqk", queries, keys, preferred_element_type=jnp.float32) * scale
-        allowed, strict = row_masks(row_seg)
-
-        def make_penalty(first_raw):
-            return penalty_from(first_raw, strict).astype(jnp.bfloat16)
-
-        def blank_penalty(first_raw):
-            return jnp.zeros(first_raw.shape, jnp.bfloat16)
-
-        local = lax.cond(tensor_index == 0, make_penalty, blank_penalty, raw[0])
-        penalty = spread(local, "tensor", 0)
-        logits = jnp.where(allowed[None], raw - penalty.astype(jnp.float32)[None], -1e30)
-        top = jnp.max(logits, axis=-1, keepdims=True)
-        weights = jnp.exp(logits - top)
-        total = jnp.sum(weights, axis=-1, keepdims=True)
-        probs = weights / total
-        mixed = jnp.einsum(
-            "hqk,hkd->hqd", probs.astype(jnp.bfloat16), values, preferred_element_type=jnp.float32
-        )
-        return (
-            merge_heads(mixed).astype(jnp.bfloat16),
-            top[..., 0] + jnp.log(total[..., 0]),
-            penalty,
-        )
-
-    attention_output, logarithm_row_totals, selection_penalty = lax.map(
-        attention_single_row, (projection_rows, segments)
-    )
-    attended_flat = attention_output.reshape(rows_here * length, rank_attn)
-    attn_total = lax.psum(contract_cols(attended_flat, w_out_side), "tensor")
+    normed_one = (plain_one * norms[0] + norms[1]).astype(BF16)
+    projected = jnp.dot(normed_one, w_project, preferred_element_type=F32).astype(BF16)
+    queries, keys, values = split_heads(projected[:, : 3 * rank_attn], rank_attn)
+    first_query = projected[:, 3 * rank_attn : 3 * rank_attn + HD]
+    first_key = projected[:, 3 * rank_attn + HD :]
+    allowed, strict = row_masks(segments[0])
+    first_raw = contract_cols(first_query, first_key) * scale
+    penalty = penalty_from(first_raw, strict).astype(BF16).astype(F32)
+    raw = jnp.einsum("hqd,hkd->hqk", queries, keys, preferred_element_type=F32) * scale
+    logits = jnp.where(allowed[None], raw - penalty[None], -1e30)
+    top = jnp.max(logits, axis=-1, keepdims=True)
+    weights = jnp.exp(logits - top)
+    total = jnp.sum(weights, axis=-1, keepdims=True)
+    probs = weights / total
+    mixed = jnp.einsum("hqk,hkd->hqd", probs.astype(BF16), values, preferred_element_type=F32)
+    attended = merge_heads(mixed).astype(BF16)
+    attn_total = tensor_total(contract_cols(attended, w_out_side).astype(BF16), 5)
     resid = tokens + attn_total
     plain_two, inverse_two = normalize(resid)
-    normed_two = (plain_two * norms[2] + norms[3]).astype(jnp.bfloat16)
-    up_pre = jnp.dot(normed_two, w_up, preferred_element_type=jnp.float32)
-    activated = jax.nn.gelu(up_pre, approximate=True).astype(jnp.bfloat16)
-    mlp_total = lax.psum(contract_cols(activated, w_down_side), "tensor")
-    output = (resid + mlp_total).astype(jnp.bfloat16).reshape(inputs.shape)
-    back_out = cotangent.reshape(rows_here * length, width)
-    d_act = jnp.dot(back_out, w_down_side, preferred_element_type=jnp.float32)
+    normed_two = (plain_two * norms[2] + norms[3]).astype(BF16)
+    up_pre = jnp.dot(normed_two, w_up, preferred_element_type=F32)
+    activated = jax.nn.gelu(up_pre, approximate=True).astype(BF16)
+    mlp_total = tensor_total(contract_cols(activated, w_down_side).astype(BF16), 6)
+    output = (resid + mlp_total).astype(BF16).reshape(inputs.shape)
+    back_out = cotangent.reshape(length, width)
+    d_act = jnp.dot(back_out, w_down_side, preferred_element_type=F32)
     grad_down_side = contract_rows(back_out, activated)
 
     def gelu_tanh(values):
         return jax.nn.gelu(values, approximate=True)
 
-    gelu_pull = jax.vjp(gelu_tanh, up_pre)[1]
-    d_up = gelu_pull(d_act)[0].astype(jnp.bfloat16)
+    d_up = jax.vjp(gelu_tanh, up_pre)[1](d_act)[0].astype(BF16)
     grad_up = contract_rows(normed_two, d_up)
-    d_two = lax.psum(contract_cols(d_up, w_up), "tensor")
+    d_two = tensor_total(contract_cols(d_up, w_up).astype(BF16), 7)
     grad_gain_two = jnp.sum(d_two * plain_two, axis=0)
     grad_bias_two = jnp.sum(d_two, axis=0)
-    d_resid = back_out.astype(jnp.float32) + norm_back(plain_two, inverse_two, d_two * norms[2])
-    d_resid_low = d_resid.astype(jnp.bfloat16)
-    d_attended = jnp.dot(d_resid_low, w_out_side, preferred_element_type=jnp.float32).astype(
-        jnp.bfloat16
-    )
-    grad_out_side = contract_rows(d_resid_low, attended_flat)
-
-    def attend_back(packed):
-        row_proj, row_seg, row_back, row_log, row_pen = packed
-        queries, keys, values = split_heads(row_proj, rank_attn)
-        back_heads = row_back.reshape(length, -1, HD).transpose(1, 0, 2)
-        raw = jnp.einsum("hqd,hkd->hqk", queries, keys, preferred_element_type=jnp.float32) * scale
-        allowed, strict = row_masks(row_seg)
-        logits = jnp.where(allowed[None], raw - row_pen.astype(jnp.float32)[None], -1e30)
-        probs = jnp.exp(logits - row_log[..., None])
-        d_probs = jnp.einsum("hqd,hkd->hqk", back_heads, values, preferred_element_type=jnp.float32)
-        inner = jnp.sum(d_probs * probs, axis=-1, keepdims=True)
-        d_logits = probs * (d_probs - inner)
-        pen_terms = -jnp.sum(d_logits, axis=0)
-        share = lax.psum_scatter(pen_terms, "tensor", scatter_dimension=0, tiled=True)
-        carried = entering(
-            jnp.sum(share, axis=0),
-            "tensor",
-            append_column_block,
-            jnp.zeros((share.shape[1],), jnp.float32),
-        )
-        later = lax.all_gather(later_sums(share) + carried[None], "tensor", axis=0, tiled=True)
-
-        def with_selection(first):
-            return first + jnp.where(strict, jax.nn.sigmoid(raw[0] - sel_shift) * later, 0.0)
-
-        def without_selection(first):
-            return first
-
-        first_head = lax.cond(tensor_index == 0, with_selection, without_selection, d_logits[0])
-        d_raw = jnp.concatenate([first_head[None], d_logits[1:]], axis=0).astype(jnp.bfloat16)
-        d_query = (
-            jnp.einsum("hqk,hkd->hqd", d_raw, keys, preferred_element_type=jnp.float32) * scale
-        )
-        d_key = (
-            jnp.einsum("hqk,hqd->hkd", d_raw, queries, preferred_element_type=jnp.float32) * scale
-        )
-        d_value = jnp.einsum(
-            "hqk,hqd->hkd",
-            probs.astype(jnp.bfloat16),
-            back_heads,
-            preferred_element_type=jnp.float32,
-        )
-        return jnp.concatenate(
-            [merge_heads(d_query), merge_heads(d_key), merge_heads(d_value)], axis=1
-        ).astype(jnp.bfloat16)
-
-    d_projected = lax.map(
-        attend_back,
-        (
-            projection_rows,
-            segments,
-            d_attended.reshape(rows_here, length, rank_attn),
-            logarithm_row_totals,
-            selection_penalty,
-        ),
-    )
-    d_projected = d_projected.reshape(rows_here * length, 3 * rank_attn)
-    d_one = lax.psum(contract_cols(d_projected, w_project), "tensor")
+    d_resid = back_out.astype(F32) + norm_back(plain_two, inverse_two, d_two * norms[2])
+    d_resid_low = d_resid.astype(BF16)
+    d_attended = jnp.dot(d_resid_low, w_out_side, preferred_element_type=F32).astype(BF16)
+    grad_out_side = contract_rows(d_resid_low, attended)
+    back_heads = d_attended.reshape(length, -1, HD).transpose(1, 0, 2)
+    d_probs = jnp.einsum("hqd,hkd->hqk", back_heads, values, preferred_element_type=F32)
+    inner = jnp.sum(d_probs * probs, axis=-1, keepdims=True)
+    d_logits = probs * (d_probs - inner)
+    later = later_sums(-jnp.sum(d_logits, axis=0))
+    first_part = jnp.where(strict, jax.nn.sigmoid(first_raw - sel_shift) * later, 0.0).astype(BF16)
+    d_raw = d_logits.astype(BF16)
+    d_query = jnp.einsum("hqk,hkd->hqd", d_raw, keys, preferred_element_type=F32) * scale
+    d_key = jnp.einsum("hqk,hqd->hkd", d_raw, queries, preferred_element_type=F32) * scale
+    d_value = jnp.einsum("hqk,hqd->hkd", probs.astype(BF16), back_heads, preferred_element_type=F32)
+    d_first = jnp.concatenate(
+        [
+            jnp.dot(first_part, first_key, preferred_element_type=F32) * scale,
+            contract_rows(first_part, first_query) * scale,
+        ],
+        axis=1,
+    )
+    d_projected = jnp.concatenate(
+        [merge_heads(d_query), merge_heads(d_key), merge_heads(d_value), d_first], axis=1
+    ).astype(BF16)
+    d_one = tensor_total(contract_cols(d_projected, w_project).astype(BF16), 8)
     grad_project = contract_rows(normed_one, d_projected)
+    first_grad = collect_first(grad_project[:, 3 * rank_attn :].astype(BF16))
+    blank = jnp.zeros((width, rank_attn - HD), F32)
+    grad_project = grad_project[:, : 3 * rank_attn] + jnp.concatenate(
+        [first_grad[:, :HD], blank, first_grad[:, HD:], blank, jnp.zeros((width, rank_attn), F32)], axis=1
+    )
     grad_gain_one = jnp.sum(d_one * plain_one, axis=0)
     grad_bias_one = jnp.sum(d_one, axis=0)
-    input_grad = (d_resid + norm_back(plain_one, inverse_one, d_one * norms[0])).reshape(
-        inputs.shape
-    )
+    input_grad = (d_resid + norm_back(plain_one, inverse_one, d_one * norms[0])).reshape(inputs.shape)
     grad_matrix = jnp.concatenate([grad_project, grad_up, grad_out_side, grad_down_side], axis=1)
-    stored_grads = jnp.take(matrix_to_blocks(grad_matrix, block), inverse, axis=0)
-    norm_grads = jnp.concatenate(
-        [grad_gain_one, grad_bias_one, grad_gain_two, grad_bias_two], axis=0
-    )
-    own_grads, own_norm_grads = (
-        lax.psum_scatter(stored_grads, "dp", scatter_dimension=0, tiled=True),
-        lax.psum_scatter(norm_grads, "dp", scatter_dimension=0, tiled=True),
-    )
+    norm_grads = jnp.concatenate([grad_gain_one, grad_bias_one, grad_gain_two, grad_bias_two], axis=0)
+    own_packed = scatter_grads(disperse(inverse, grad_matrix, n_dp, block))
+    own_grads = own_packed[:, : per_dev * block].reshape(block, per_dev, block).transpose(1, 0, 2)
+    own_norm_grads = lax.psum_scatter(norm_grads, "dp", scatter_dimension=0, tiled=True)
     new_first, new_second, new_master, new_left, new_right, left_next, right_next = soap(
         own_grads,
         masters[0],

time: 1210 us -> 643 us (0.53)
  waiting for transfers between devices: 636 us -> 0 us
  Pallas kernels: 85.7 us -> 296 us
  other arithmetic: 112 us -> 62.6 us
  blocking collectives: 73.2 us -> 34.3 us
  local copies, waits for them, and re-layouts: 212 us -> 176 us
  between operations: 16.1 us -> 2.7 us
    reduce_scatter x2 -> x0, waiting for transfers between devices: 311 us -> none  [the longest x1 266 us: body(): lax.psum_scatter(stored_grads, 'dp', scatter_dimension=0, tiled=True)]
    pallas_call x0 -> x10, Pallas kernels: none -> 210 us  [the longest x4 90.8 us: tensor_total(): pl.pallas_call(functools.partial(total_kernel, pieces), out_shape=jax.Sha...]
    psum x4 -> x0, waiting for transfers between devices: 208 us -> none  [the longest x1 68.2 us: body(): attn_total = lax.psum(contract_cols(attended_flat, w_out_side), 'tensor')]
    all_gather x2 -> x0, waiting for transfers between devices: 117 us -> none  [the longest x1 108 us: body(): lax.all_gather(masters[0].astype(jnp.bfloat16), 'dp', axis=0, tiled=True)]
    reshape x3, local copies, waits for them, and re-layouts: 48.4 us -> 9.28 us  [the longest x1 18.8 us: matrix_to_blocks(): return weight_matrix.reshape(grid_rows, block, grid_cols, block).transpos...]
    all_gather x2 -> x0, blocking collectives: 33.9 us -> none  [the longest x1 28.1 us: body(): lax.all_gather(norm_master.astype(jnp.bfloat16), 'dp', axis=0, tiled=True)]
    another operation x11 -> x7, local copies, waits for them, and re-layouts: 37.5 us -> 11.1 us
    rev x1, local copies, waits for them, and re-layouts: 9.33 us -> 34.5 us  [later_sums(): suffix = jnp.cumsum(grads[::-1], axis=0)[::-1]]
  transfers between devices with their start and end apart: 8 -> 0, of which waited for: 8 -> 0; matrix products, arithmetic and copies ran while one was open for 11% -> 0% of each run, Pallas kernels for 0% -> 0%
where the time goes in v2:
time: 643 us; the launch traced here: 631 us
  Pallas kernels  296 us (46%)
  local copies, waits for them, and re-layouts  176 us (27%)
  other arithmetic  62.6 us (10%)
  matrix products  60.1 us (9%)
  blocking collectives  34.3 us (5%)
    pallas_call x4, Pallas kernels, tensor_total(): pl.pallas_call(functools.partial(total_kernel, pieces), out_shape=jax.Sha...  90.8 us
    pallas_call x1, Pallas kernels, soap(): pl.pallas_call(functools.partial(soap_kernel, count, chunk, block), grid=...  85.8 us
    unnamed x156, local copies, waits for them, and re-layouts  52.9 us
    pallas_call x1, Pallas kernels, gather_masters(): pl.pallas_call(functools.partial(gather_kernel, n, count, block, wide, no...  47.6 us
    pallas_call x1, Pallas kernels, scatter_grads(): pl.pallas_call(functools.partial(scatter_kernel, n), out_shape=jax.ShapeD...  39.6 us
    rev x1, local copies, waits for them, and re-layouts, later_sums(): suffix = jnp.cumsum(grads[::-1], axis=0)[::-1]  34.5 us
    unnamed x1, blocking collectives  34.3 us
    slice x1, local copies, waits for them, and re-layouts, later_sums(): suffix[1:]  33.8 us

profile of v2, /device:TPU:0, one launch (start us, length us, event | category | flops | bytes accessed | tf_op | source)
XLA Modules:
  0.0 631.5 jit_solution(15474640605115176976)
XLA Ops:
  4.5 47.6 %gather_masters.1 = (bf16[768,48,48]{2,1,0:T(8,128)(2,1)S(1)}, bf16[8,16,128]{2,1,0:T(8,128)(2,1)S(1)}) custom-call(f32[96,48,48]{2,1,0:T(8,128)S(1)} %bitcast.168, f32[3,128]{1,0:T(4,128)S(1)} %bitcast.173), custom_call_target="tpu_custom_call" | custom-call | tf_op jit(solution)/shard_map/gather_masters/pallas_call | solution.py:178
  58.5 8.4 %share_first.1 = bf16[768,128]{1,0:T(8,128)(2,1)} custom-call(bf16[768,128]{1,0:T(8,128)(2,1)} %pad_maximum_fusion.3.x_ref), custom_call_target="tpu_custom_call" | custom-call | tf_op jit(solution)/shard_map/share_first/pallas_call | solution.py:450
  75.7 5.5 copy.154
  81.2 4.8 fusion.9
  89.1 5.5 copy.155
  105.6 5.4 copy.157
  113.5 10.3 %fusion.95 = (f32[3,1024]{1,0:T(4,128)}, f32[3,1024,1024]{1,2,0:T(8,128)}) fusion(f32[1024,1024]{0,1:T(8,128)} %copy.157, pred[1024,1024]{0,1:T(8,128)(4,1)S(1)} %copy.152, bf16[3,1024,64]{1,2,0:T(8,128)(2,1)S(1)} %bitcast.195, bf16[3,1024,64]{1,2,0:T(8,128)(2,1)S(1)} %bitcast.197), kind=kOutput, calls=%fused_computation.160 | convolution fusion | flops 418382848 | bytes 18624512 | tf_op jit(solution)/shard_map/sub | solution.py:732
  123.8 5.9 fusion.56
  130.5 22.9 %tensor_total.4 = f32[1024,768]{1,0:T(8,128)S(1)} custom-call(bf16[1024,768]{1,0:T(8,128)(2,1)S(1)} %convolution_convert_fusion.3.x_ref), custom_call_target="tpu_custom_call" | custom-call | tf_op jit(solution)/shard_map/tensor_total/pallas_call | solution.py:415
  168.3 22.6 %tensor_total.6 = f32[1024,768]{1,0:T(8,128)S(1)} custom-call(bf16[1024,768]{1,0:T(8,128)(2,1)S(1)} %convolution_convert_fusion.1.x_ref), custom_call_target="tpu_custom_call" | custom-call | tf_op jit(solution)/shard_map/tensor_total/pallas_call | solution.py:415
  195.1 22.6 %tensor_total.5 = f32[1024,768]{1,0:T(8,128)S(1)} custom-call(bf16[1024,768]{1,0:T(8,128)(2,1)S(1)} %convolution_convert_fusion.2.x_ref), custom_call_target="tpu_custom_call" | custom-call | tf_op jit(solution)/shard_map/tensor_total/pallas_call | solution.py:415
  222.9 5.6 multiply_reduce_fusion
  228.5 10.5 %fusion.6 = (f32[1024,1024]{0,1:T(8,128)S(1)}, bf16[3,1024,1024]{1,2,0:T(8,128)(2,1)S(1)}) fusion(f32[3,1024,1024]{1,2,0:T(8,128)} %get-tuple-element.121, f32[3,1024]{1,0:T(4,128)S(1)} %get-tuple-element.120, f32[3,1024,1024]{1,2,0:T(8,128)} %get-tuple-element.119, f32[3,1024]{1,0:T(4,128)S(1)} %copy-done.48), kind=kLoop, calls=%fused_computation.14 | loop fusion | flops 14680064 | bytes 35676160 | tf_op jit(solution)/shard_map/reduce_sum | solution.py:765
  242.3 6.6 %fusion.59 = bf16[3,1024,64]{1,2,0:T(8,128)(2,1)S(1)} fusion(bf16[3,1024,64]{1,2,0:T(8,128)(2,1)S(1)} %bitcast.205, f32[3,1024,1024]{1,2,0:T(8,128)} %get-tuple-element.119, f32[3,1024]{1,0:T(4,128)S(1)} %copy-done.48), kind=kOutput, calls=%fused_computation.103 | convolution fusion | flops 409141248 | bytes 13381632 | tf_op jit(solution)/shard_map/hqk,hqd->hkd/dot_general | solution.py:770
  251.4 34.5 %rev.4 = f32[1024,1024]{0,1:T(8,128)} reverse(f32[1024,1024]{0,1:T(8,128)} %neg.13), dimensions={0} | reverse | bytes 8388608 | tf_op jit(solution)/shard_map/rev | solution.py:543
  285.9 5.6 copy.163
  305.2 33.8 %slice.131 = f32[1023,1024]{1,0:T(8,128)} reverse(f32[1023,1024]{1,0:T(8,128)} %bitcast.177), dimensions={0} | reverse | bytes 8380416 | tf_op jit(solution)/shard_map/slice | solution.py:544
  348.3 22.6 %tensor_total.7 = f32[1024,768]{1,0:T(8,128)S(1)} custom-call(bf16[1024,768]{1,0:T(8,128)(2,1)S(1)} %convolution_convert_fusion.x_ref), custom_call_target="tpu_custom_call" | custom-call | tf_op jit(solution)/shard_map/tensor_total/pallas_call | solution.py:415
  385.4 9.1 %collect_first.1 = f32[768,128]{1,0:T(8,128)} custom-call(bf16[768,128]{1,0:T(8,128)(2,1)} %copy.194.x_ref), custom_call_target="tpu_custom_call" | custom-call | tf_op jit(solution)/shard_map/collect_first/pallas_call | solution.py:486
  412.8 7.8 %concatenate.31.g_ref = f32[768,2304]{1,0:T(8,128)} concatenate(f32[768,576]{1,0:T(8,128)S(1)} %copy-done.17, f32[768,768]{1,0:T(8,128)} %fusion.97, f32[768,192]{1,0:T(8,128)S(1)} %copy-done.18, f32[768,768]{1,0:T(8,128)} %convolution_bitcast_fusion), dimensions={1} | concatenate | bytes 14155776 | tf_op jit(solution)/shard_map/concatenate | solution.py:791
  423.6 10.7 %disperse.1.p_ref = bf16[8,48,4608]{2,1,0:T(8,128)(2,1)S(1)} custom-call(s32[768]{0:T(1024)S(1)} %select_reduce_fusion.inverse_ref, f32[768,2304]{1,0:T(8,128)S(1)} %copy-done), custom_call_target="tpu_custom_call" | custom-call | tf_op jit(solution)/shard_map/disperse/pallas_call | solution.py:242
  434.3 39.6 %scatter_grads.1 = f32[48,4608]{1,0:T(8,128)S(1)} custom-call(bf16[8,48,4608]{2,1,0:T(8,128)(2,1)S(1)} %disperse.1.p_ref), custom_call_target="tpu_custom_call" | custom-call | tf_op jit(solution)/shard_map/scatter_grads/pallas_call | solution.py:352
  490.7 85.8 %soap.1 = (f32[96,48,48]{2,1,0:T(8,128)S(1)}, f32[96,48,48]{2,1,0:T(8,128)S(1)}, f32[96,48,48]{2,1,0:T(8,128)}, f32[96,48,48]{2,1,0:T(8,128)}, f32[96,48,48]{2,1...) custom-call(f32[96,48,48]{2,1,0:T(8,128)} %bitcast.180, f32[96,48,48]{2,1,0:T(8,128)} %bitcast.169, ...), custom_call_target="tpu_custom_call" | custom-call | tf_op jit(solution)/shard_map/soap/pallas_call | solution.py:658
  594.8 34.3 %all-reduce.2 = f32[3072]{0:T(1024)S(1)} all-reduce(f32[3072]{0:T(1024)S(1)} %pad_maximum_fusion.4), channel_id=2, replica_groups=mesh['dp'=8,'tensor'=4] {'dp'}, use_global_device_ids=true, to_apply=%region_22.23.clone | all-reduce | flops 3072 | bytes 24576
  (232 shorter events, 160.8 us)
Async XLA Ops:
  2.5 53.4 %copy-start.5 = (s32[768]{0:T(1024)}, s32[768]{0:T(1024)S(1)}, u32[]{:S(2)}) copy-start(s32[768]{0:T(1024)S(1)} %multiply_add_fusion.2.slot_ref) | copy-start | bytes 9220
  4.5 51.5 %copy-start.1 = (f32[1,96,48,48]{3,2,1,0:T(8,128)}, f32[1,96,48,48]{3,2,1,0:T(8,128)S(1)}, u32[]{:S(2)}) copy-start(f32[1,96,48,48]{3,2,1,0:T(8,128)S(1)} %copy.153) | copy-start | bytes 2654212
  57.7 11.3 %copy-start.12 = (bf16[1,1024,768]{2,1,0:T(8,128)(2,1)S(1)}, bf16[1,1024,768]{2,1,0:T(8,128)(2,1)}, u32[]{:S(2)}) copy-start(bf16[1,1024,768]{2,1,0:T(8,128)(2,1)} %param.14) | copy-start | bytes 4718596
  72.7 40.8 %copy-start.27 = (bf16[1024,192]{0,1:T(8,128)(2,1)}, bf16[1024,192]{0,1:T(8,128)(2,1)S(1)}, u32[]{:S(2)}) copy-start(bf16[1024,192]{0,1:T(8,128)(2,1)S(1)} %get-tuple-element.111) | copy-start | bytes 1179652
  72.7 40.8 %copy-start.29 = (bf16[1024,192]{0,1:T(8,128)(2,1)}, bf16[1024,192]{0,1:T(8,128)(2,1)S(1)}, u32[]{:S(2)}) copy-start(bf16[1024,192]{0,1:T(8,128)(2,1)S(1)} %get-tuple-element.109) | copy-start | bytes 1179652
  75.7 5.5 copy-start.43
  123.8 6.0 copy-start.3
  129.7 23.8 %copy-start.25 = (bf16[3,1024,64]{1,2,0:T(8,128)(2,1)}, bf16[3,1024,64]{1,2,0:T(8,128)(2,1)S(1)}, u32[]{:S(2)}) copy-start(bf16[3,1024,64]{1,2,0:T(8,128)(2,1)S(1)} %fusion.56) | copy-start | bytes 1179652
  129.7 23.7 %copy-start.13 = (bf16[1,1024,768]{2,1,0:T(8,128)(2,1)S(1)}, bf16[1,1024,768]{2,1,0:T(8,128)(2,1)}, u32[]{:S(2)}) copy-start(bf16[1,1024,768]{2,1,0:T(8,128)(2,1)} %param.14) | copy-start | bytes 4718596
  163.3 29.8 %copy-start.60 = (f32[1024,768]{1,0:T(8,128)}, f32[1024,768]{1,0:T(8,128)S(1)}, u32[]{:S(2)}) copy-start(f32[1024,768]{1,0:T(8,128)S(1)} %fusion.69) | copy-start | bytes 9437188
  195.1 27.0 %slice-start = ((s8[12582912]{0:T(1024)(128)(4,1)}), s8[4194304]{0:T(1024)(128)(4,1)S(1)}, s32[]{:S(2)}) async-start(s8[12582912]{0:T(1024)(128)(4,1)} %bitcast.178), calls=%async_computation | async-start | bytes 8388608
  217.7 4.9 slice-start.2
  228.5 10.5 %copy-start.30 = (bf16[1024,192]{0,1:T(8,128)(2,1)S(1)}, bf16[1024,192]{0,1:T(8,128)(2,1)}, u32[]{:S(2)}) copy-start(bf16[1024,192]{0,1:T(8,128)(2,1)} %copy-done.29) | copy-start | bytes 1179652
  348.3 22.6 %copy-start.14 = (bf16[1,1024,768]{2,1,0:T(8,128)(2,1)S(1)}, bf16[1,1024,768]{2,1,0:T(8,128)(2,1)}, u32[]{:S(2)}) copy-start(bf16[1,1024,768]{2,1,0:T(8,128)(2,1)} %param.14) | copy-start | bytes 4718596
  348.3 22.6 %copy-start.47 = (f32[1024]{0:T(1024)S(1)}, f32[1024]{0:T(1024)}, u32[]{:S(2)}) copy-start(f32[1024]{0:T(1024)} %copy-done.46) | copy-start | bytes 12292
  477.7 5.0 copy-start.34
  587.1 5.9 copy-start.19
  590.1 4.6 copy-start.51
  590.1 4.6 copy-start.52
  590.1 4.6 copy-start.53
  590.1 39.0 %copy-start.59 = (u32[32]{0:T(128)S(1)}, u32[32]{0:T(128)}, u32[]{:S(2)}) copy-start(u32[32]{0:T(128)} %constant.88) | copy-start | bytes 388
  590.1 40.2 %copy-start.8 = (f32[384]{0:T(512)S(1)}, f32[384]{0:T(512)}, u32[]{:S(2)}) copy-start(f32[384]{0:T(512)} %param.25) | copy-start | bytes 4612
  590.2 40.2 %copy-start.57 = (f32[384]{0:T(512)S(1)}, f32[384]{0:T(512)}, u32[]{:S(2)}) copy-start(f32[384]{0:T(512)} %param.27) | copy-start | bytes 4612
  590.2 40.2 %copy-start.58 = (f32[384]{0:T(512)S(1)}, f32[384]{0:T(512)}, u32[]{:S(2)}) copy-start(f32[384]{0:T(512)} %param.26) | copy-start | bytes 4612
  (43 other events, 116.9 us)

commit v3 on v1

v3 whole, which is shorter than its diff:
```python
import functools
import math

import jax
import jax.numpy as jnp
from jax import lax
from jax.experimental import pallas as pl
from jax.experimental.pallas import tpu as pltpu
from jax.sharding import PartitionSpec as P

HD = 64
STEP = 10
F32 = jnp.float32
BF16 = jnp.bfloat16
LAYER_LIMIT = 48 * 2**20

norm_eps = 1e-05
beta_one = 0.9
beta_two = 0.95
beta_stats = 0.95
learn_rate = 0.03
norm_rate = 0.4
weight_decay = 0.01
adam_eps = 1e-08


def shift_for(length):
    return math.log(length / 8.0)


def block_slots(owner, per_dev):
    count = owner.shape[0]
    index = jnp.arange(count, dtype=jnp.int32)
    earlier = (owner[:, None] == owner[None, :]) & (index[None, :] < index[:, None])
    rank = jnp.sum(earlier.astype(jnp.int32), axis=1)
    slots = owner * per_dev + rank
    inverse = jnp.sum(jnp.where(slots[None, :] == index[:, None], index[None, :], 0), axis=1)
    return (slots, inverse)


def norm_back(plain, inverse_std, grad):
    return inverse_std * (
        grad
        - jnp.mean(grad, axis=-1, keepdims=True)
        - plain * jnp.mean(grad * plain, axis=-1, keepdims=True)
    )


def split3(v):
    hi = v.astype(BF16)
    return hi, (v - hi.astype(F32)).astype(BF16)

def prod(left, right, dims):
    lh, ll = left
    rh, rl = right
    spec = (dims, ((), ()))
    def one(a, b):
        return lax.dot_general(a, b, spec, preferred_element_type=F32)
    return one(lh, rh) + (one(lh, rl) + one(ll, rh))

NN = ((1,), (0,))
NT = ((1,), (1,))
TN = ((0,), (0,))

def soap_kernel(count, chunk, block, g_ref, m_ref, f_ref, s_ref, l_ref, r_ref, ql_ref, qr_ref,
                nf_ref, ns_ref, nm_ref, nl_ref, nr_ref, bl_ref, br_ref, a_scr, t_scr):
    step = pl.program_id(0)
    tiles = block // 8
    for c in range(chunk):
        g = g_ref[c]
        ql, qr = split3(ql_ref[c]), split3(qr_ref[c])
        gs = split3(g)
        gt = split3(g.T)
        new_left = beta_stats * l_ref[c] + (1.0 - beta_stats) * prod(gs, gs, NT)
        new_right = beta_stats * r_ref[c] + (1.0 - beta_stats) * prod(gt, gt, NT)
        nl_ref[c] = new_left
        nr_ref[c] = new_right
        half = prod(gt, ql, NN)
        rot = prod(split3(half.T), qr, NN)
        first = beta_one * f_ref[c] + (1.0 - beta_one) * rot
        second = beta_two * s_ref[c] + (1.0 - beta_two) * rot * rot
        nf_ref[c] = first
        ns_ref[c] = second
        direction = first / (1.0 - beta_one**STEP) / (
            jnp.sqrt(second / (1.0 - beta_two**STEP)) + adam_eps)
        moved = prod(split3(prod(ql, split3(direction), NN)), qr, NT)
        master = m_ref[c]
        nm_ref[c] = master - learn_rate * (moved + weight_decay * master)
        a_scr[0, step * chunk + c] = prod(split3(new_left), ql, NN)
        a_scr[1, step * chunk + c] = prod(split3(new_right), qr, NN)

    @pl.when(step == pl.num_programs(0) - 1)
    def _():
        def bring(i, _):
            for s in range(2):
                slab = a_scr[s, :, pl.ds(i, 1), :].reshape(128, block)
                t_scr[s, i] = slab.T
            return 0
        lax.fori_loop(0, block, bring, 0, unroll=4)
        sub = lax.broadcasted_iota(jnp.int32, (8, 128), 0)
        norms = [[None] * tiles, [None] * tiles]
        for kt in range(tiles):
            def one(kk, carry):
                k = kt * 8 + kk
                acc = [[jnp.zeros((8, 128), F32) for _ in range(kt, tiles)] for _ in range(2)]
                for i in range(block):
                    for s in range(2):
                        row = jnp.broadcast_to(t_scr[s, i, pl.ds(k, 1), :], (8, 128))
                        for j in range(kt, tiles):
                            acc[s][j - kt] += row * t_scr[s, i, 8 * j : 8 * j + 8, :]
                out = []
                for s in range(2):
                    here = sub == kk
                    size = jnp.sum(jnp.where(here, acc[s][0], 0.0), axis=0, keepdims=True)
                    size = jnp.broadcast_to(size, (8, 128))
                    inv = 1.0 / size
                    acc[s] = [v * inv for v in acc[s]]
                    acc[s][0] = jnp.where(sub > kk, acc[s][0], 0.0)
                    out.append(jnp.where(here, size, carry[s]))
                for i in range(block):
                    for s in range(2):
                        row = jnp.broadcast_to(t_scr[s, i, pl.ds(k, 1), :], (8, 128))
                        for j in range(kt, tiles):
                            t_scr[s, i, 8 * j : 8 * j + 8, :] -= row * acc[s][j - kt]
                return tuple(out)
            res = lax.fori_loop(0, 8, one, (jnp.ones((8, 128), F32),) * 2)
            for s in range(2):
                norms[s][kt] = lax.rsqrt(res[s])
        scale = [jnp.concatenate(norms[s], axis=0) for s in range(2)]
        def back(i, _):
            for s, ref in ((0, bl_ref), (1, br_ref)):
                done = (t_scr[s, i] * scale[s]).T
                ref[:, pl.ds(i, 1), :] = done[:count].reshape(count, 1, block)
            return 0
        lax.fori_loop(0, block, back, 0, unroll=4)

def soap(g, m, f, s, l, r, ql, qr):
    count, block = g.shape[0], g.shape[-1]
    chunk = math.gcd(count, 8)
    spec = pl.BlockSpec((chunk, block, block), lambda i: (i, 0, 0))
    whole = pl.BlockSpec((count, block, block), lambda i: (0, 0, 0))
    shape = jax.ShapeDtypeStruct(g.shape, F32)
    return pl.pallas_call(
        functools.partial(soap_kernel, count, chunk, block),
        grid=(count // chunk,),
        in_specs=[spec] * 8,
        out_specs=[spec] * 5 + [whole] * 2,
        out_shape=[shape] * 7,
        scratch_shapes=[pltpu.VMEM((2, 128, block, block), F32), pltpu.VMEM((2, block, block, 128), F32)],
        compiler_params=pltpu.CompilerParams(vmem_limit_bytes=48 * 2**20),
        name="soap",
    )(g, m, f, s, l, r, ql, qr)


MESH = pl.DeviceIdType.MESH
VM = pl.BlockSpec(memory_space=pltpu.VMEM)
MIB = 2**20


def tiles_up(value):
    return -(-value // 128) * 128


def remote(src, dst, send, recv, where):
    return pltpu.make_async_remote_copy(
        src_ref=src, dst_ref=dst, send_sem=send, recv_sem=recv, device_id=where, device_id_type=MESH
    )


def greet(devices):
    barrier = pltpu.get_barrier_semaphore()
    for device in devices:
        pl.semaphore_signal(barrier, inc=1, device_id=device, device_id_type=MESH)
    pl.semaphore_wait(barrier, len(devices))


def line_greet(dp, t, m):
    place, side = dp // 2, lax.rem(dp, 2)
    barrier = pltpu.get_barrier_semaphore()
    pl.semaphore_signal(barrier, inc=1, device_id=(place * 2 + 1 - side, t), device_id_type=MESH)

    @pl.when(place > 0)
    def _():
        pl.semaphore_signal(barrier, inc=1, device_id=(dp - 2, t), device_id_type=MESH)

    @pl.when(place < m - 1)
    def _():
        pl.semaphore_signal(barrier, inc=1, device_id=(dp + 2, t), device_id_type=MESH)

    ends = (place == 0).astype(jnp.int32) + (place == m - 1).astype(jnp.int32)
    pl.semaphore_wait(barrier, 3 - ends)


def gather_kernel(n, count, block, wide, norm_rows, m_ref, norm_ref, u_ref, nout_ref, held, send_sem, recv_sem):
    m = n // 2
    dp, t = lax.axis_index("dp"), lax.axis_index("tensor")
    place, side = dp // 2, lax.rem(dp, 2)
    pair = (place * 2 + 1 - side, t)
    for k in range(count):
        held[dp, :, k * block : (k + 1) * block] = m_ref[k].astype(BF16)
    if wide > count * block:
        held[dp, :, count * block : wide] = jnp.zeros((block, wide - count * block), BF16)
    held[dp, :, wide : wide + 128] = jnp.concatenate(
        [norm_ref[...], jnp.zeros((block - norm_rows, 128), F32)], axis=0
    ).astype(BF16)
    line_greet(dp, t, m)

    def send(source, way, where):
        return remote(held.at[source], held.at[source], send_sem.at[source, way], recv_sem.at[source], where)

    def unpack(source):
        for k in range(count):
            u_ref[source * count + k] = held[source, :, k * block : (k + 1) * block]
        nout_ref[source] = held[source, :16, wide : wide + 128]

    def spread(source, left, right):
        send(source, 2, pair).start()

        @pl.when(left)
        def _():
            send(source, 0, (dp - 2, t)).start()

        @pl.when(right)
        def _():
            send(source, 1, (dp + 2, t)).start()

    def spread_done(source, left, right):
        send(source, 2, pair).wait_send()

        @pl.when(left)
        def _():
            send(source, 0, (dp - 2, t)).wait_send()

        @pl.when(right)
        def _():
            send(source, 1, (dp + 2, t)).wait_send()

    spread(dp, place > 0, place < m - 1)
    unpack(dp)

    def one(hop, _):
        @pl.when(place - hop >= 0)
        def _():
            source = dp - 2 * hop
            send(source, 2, pair).wait_recv()
            spread(source, False, place < m - 1)

        @pl.when(place + hop < m)
        def _():
            source = dp + 2 * hop
            send(source, 2, pair).wait_recv()
            spread(source, place > 0, False)

        @pl.when(place - hop >= 0)
        def _():
            unpack(dp - 2 * hop)

        @pl.when(place + hop < m)
        def _():
            unpack(dp + 2 * hop)

        return 0

    lax.fori_loop(1, m, one, 0)

    def other(step, _):
        source = step * 2 + 1 - side
        send(source, 2, pair).wait_recv()
        unpack(source)
        return 0

    lax.fori_loop(0, m, other, 0)

    def finish(step, _):
        source = step * 2 + side
        spread_done(
            source,
            (place > 0) & (step >= place),
            (place < m - 1) & (step <= place),
        )
        return 0

    lax.fori_loop(0, m, finish, 0)


def gather_masters(masters, norm, n):
    count, block = masters.shape[0], masters.shape[-1]
    wide = tiles_up(count * block)
    norm_rows = -(-norm.shape[0] // 128)
    norm_tile = jnp.pad(norm, (0, norm_rows * 128 - norm.shape[0])).reshape(norm_rows, 128)
    blocks, norms = pl.pallas_call(
        functools.partial(gather_kernel, n, count, block, wide, norm_rows),
        out_shape=[
            jax.ShapeDtypeStruct((n * count, block, block), BF16),
            jax.ShapeDtypeStruct((n, 16, 128), BF16),
        ],
        in_specs=[VM, VM],
        out_specs=[VM, VM],
        scratch_shapes=[
            pltpu.VMEM((n, block, wide + 128), BF16),
            pltpu.SemaphoreType.DMA((n, 3)),
            pltpu.SemaphoreType.DMA((n,)),
        ],
        compiler_params=pltpu.CompilerParams(collective_id=1, has_side_effects=True, vmem_limit_bytes=10 * MIB),
        name="gather_masters",
    )(masters, norm_tile)
    return blocks, norms.reshape(n, 16 * 128)[:, : norm.shape[0]].reshape(-1)


def assemble_kernel(rows, cols, block, cuts, slot_ref, u_ref, *w_refs):
    def one(row, _):
        for first, last, w_ref in zip(cuts, cuts[1:], w_refs):
            strip = jnp.concatenate([u_ref[slot_ref[row * cols + c]] for c in range(first, last)], axis=1)
            w_ref[pl.ds(pl.multiple_of(row * block, block), block), :] = strip
        return 0

    lax.fori_loop(0, rows, one, 0)


def piece_cuts(rows, cols, parts):
    attn = rows // parts
    hidden = (cols - 4 * attn) // 2
    return (0, 3 * attn, 3 * attn + hidden, 4 * attn + hidden, cols)


def assemble(slots, blocks, rows, parts):
    block = blocks.shape[-1]
    cols = blocks.shape[0] // rows
    cuts = piece_cuts(rows, cols, parts)
    return pl.pallas_call(
        functools.partial(assemble_kernel, rows, cols, block, cuts),
        out_shape=[
            jax.ShapeDtypeStruct((rows * block, (last - first) * block), BF16)
            for first, last in zip(cuts, cuts[1:])
        ],
        in_specs=[pl.BlockSpec(memory_space=pltpu.SMEM), VM],
        out_specs=[VM] * 4,
        compiler_params=pltpu.CompilerParams(vmem_limit_bytes=4 * MIB),
        name="assemble",
    )(slots, blocks)


def disperse_kernel(rows, cols, block, cuts, n, count, wide, inverse_ref, *refs):
    g_refs, p_ref, u_scr = refs[:4], refs[4], refs[5]

    def cut(row, _):
        for first, last, g_ref in zip(cuts, cuts[1:], g_refs):
            strip = g_ref[pl.ds(pl.multiple_of(row * block, block), block), :]
            for c in range(first, last):
                u_scr[row * cols + c] = strip[:, (c - first) * block : (c - first + 1) * block]
        return 0

    lax.fori_loop(0, rows, cut, 0)

    def lay(d, _):
        for k in range(count):
            p_ref[d, :, k * block : (k + 1) * block] = u_scr[inverse_ref[d * count + k]]
        if wide > count * block:
            p_ref[d, :, count * block : wide] = jnp.zeros((block, wide - count * block), BF16)
        return 0

    lax.fori_loop(0, n, lay, 0)


def disperse(inverse, grads, n, block, parts):
    rows = grads[0].shape[0] // block
    cols = sum(grad.shape[1] for grad in grads) // block
    count = rows * cols // n
    wide = tiles_up(count * block)
    return pl.pallas_call(
        functools.partial(
            disperse_kernel, rows, cols, block, piece_cuts(rows, cols, parts), n, count, wide
        ),
        out_shape=jax.ShapeDtypeStruct((n, block, wide), BF16),
        in_specs=[pl.BlockSpec(memory_space=pltpu.SMEM)] + [VM] * 4,
        out_specs=VM,
        scratch_shapes=[pltpu.VMEM((rows * cols, block, block), BF16)],
        compiler_params=pltpu.CompilerParams(vmem_limit_bytes=16 * MIB),
        name="disperse",
    )(inverse, *grads)


BLK = 128


def plain_norm(rows):
    centered = rows - jnp.mean(rows, axis=-1, keepdims=True)
    inverse_std = lax.rsqrt(jnp.mean(centered * centered, axis=-1, keepdims=True) + norm_eps)
    return centered * inverse_std, inverse_std


def dot(left, right, dims):
    return lax.dot_general(left, right, (dims, ((), ())), preferred_element_type=F32)


class Total:
    def __init__(self, dp, t, x, near, mine, far, near_mine, near_far, sems):
        up, core = t // 2, lax.rem(t, 2)
        self.core = core
        self.beside = (dp, up * 2 + 1 - core)
        self.over = (dp, (1 - up) * 2 + core)
        self.x, self.near, self.mine, self.far = x, near, mine, far
        self.near_mine, self.near_far, self.sems = near_mine, near_far, sems
        self.blocks = sems.shape[1]
        self.size = x.shape[0] // self.blocks
        self.half = self.size // 2

    def rows(self, b, core):
        return pl.ds(pl.multiple_of(b * self.size + core * self.half, self.half), self.half)

    def part(self, b):
        return pl.ds(pl.multiple_of(b * self.half, self.half), self.half)

    def copy(self, kind, b):
        here = self.part(b)
        src, dst, where = (
            (self.x.at[self.rows(b, 1 - self.core)], self.near, self.beside),
            (self.mine.at[here], self.far, self.over),
            (self.mine.at[here], self.near_mine, self.beside),
            (self.far.at[here], self.near_far, self.beside),
        )[kind]
        return remote(src, dst.at[here], self.sems.at[2 * kind, b], self.sems.at[2 * kind + 1, b], where)

    def enter(self, b):
        self.copy(0, b).start()

    def add(self, b):
        here = self.part(b)
        self.copy(0, b).wait_recv()
        self.mine[here] = (self.x[self.rows(b, self.core)].astype(F32) + self.near[here].astype(F32)).astype(BF16)

    def cross(self, b):
        self.copy(1, b).start()
        self.copy(2, b).start()

    def relay(self, b):
        self.copy(1, b).wait_recv()
        self.copy(3, b).start()

    def arrived(self, b):
        self.copy(2, b).wait_recv()
        self.copy(3, b).wait_recv()

    def sums(self, b):
        here = self.part(b)
        own = self.mine[here].astype(F32) + self.far[here].astype(F32)
        other = self.near_mine[here].astype(F32) + self.near_far[here].astype(F32)
        low = self.core == 0
        return jnp.concatenate([jnp.where(low, own, other), jnp.where(low, other, own)], axis=0)

    def close(self, b):
        for kind in range(4):
            self.copy(kind, b).wait_send()


def layer_kernel(
    heads,
    shift,
    x_ref,
    seg_row_ref,
    seg_col_ref,
    dy_ref,
    wp_ref,
    w1_ref,
    wo_ref,
    w2_ref,
    norm_ref,
    gp_ref,
    g1_ref,
    go_ref,
    g2_ref,
    out_ref,
    da_ref,
    resid_ref,
    dres_ref,
    ng_ref,
    a_ref,
    wf_ref,
    qkv_ref,
    pen_ref,
    lse_ref,
    o_ref,
    cn_ref,
    s_ref,
    du_ref,
    dhb_ref,
    dproj_ref,
    dkv_ref,
    carry_ref,
    x1_ref,
    near1,
    mine1,
    far1,
    near_mine1,
    near_far1,
    sem1,
    x3_ref,
    near3,
    mine3,
    far3,
    near_mine3,
    near_far3,
    sem3,
    gf_ref,
    gf_near,
    gf_far,
    share_sem,
    collect_sem,
):
    dp, t = lax.axis_index("dp"), lax.axis_index("tensor")
    up, core = t // 2, lax.rem(t, 2)
    beside, over = (dp, up * 2 + 1 - core), (dp, (1 - up) * 2 + core)
    length, width = x_ref.shape
    blocks = length // BLK
    span = min(length // 2 + BLK, length)
    attn = heads * HD
    one = Total(dp, t, x1_ref, near1, mine1, far1, near_mine1, near_far1, sem1)
    three = Total(dp, t, x3_ref, near3, mine3, far3, near_mine3, near_far3, sem3)
    greet([beside, over])

    def give(where, i):
        return remote(wf_ref, wf_ref, share_sem.at[i], share_sem.at[2], where)

    @pl.when(t == 0)
    def _():
        wf_ref[:, :HD] = wp_ref[:, :HD]
        wf_ref[:, HD:] = wp_ref[:, attn : attn + HD]
        give(over, 0).start()
        give(beside, 1).start()

    def rows_of(b):
        return pl.ds(pl.multiple_of(b * BLK, BLK), BLK)

    gain_one, bias_one = norm_ref[0:1, :], norm_ref[1:2, :]
    gain_two, bias_two = norm_ref[2:3, :], norm_ref[3:4, :]
    wide = 2 * BLK

    def wide_rows(i):
        return pl.ds(pl.multiple_of(i * wide, wide), wide)

    def project(i, _):
        rows = wide_rows(i)
        plain, _ = plain_norm(x_ref[rows].astype(F32))
        a = (plain * gain_one + bias_one).astype(BF16)
        a_ref[rows] = a
        projected = dot(a, wp_ref[...], NN)
        for h in range(heads):
            qkv_ref[h, rows] = projected[:, h * HD : (h + 1) * HD].astype(BF16) * 0.125
        for h in range(heads, 3 * heads):
            qkv_ref[h, rows] = projected[:, h * HD : (h + 1) * HD].astype(BF16)
        return 0

    lax.fori_loop(0, length // wide, project, 0)

    @pl.when(t == 2)
    def _():
        give(over, 0).wait_recv()
        give(beside, 1).start()

    @pl.when((t == 1) | (t == 3))
    def _():
        give(beside, 1).wait_recv()

    def project_first(i, _):
        rows = wide_rows(i)
        projected = dot(a_ref[rows], wf_ref[...], NN)
        qkv_ref[3 * heads, rows] = projected[:, :HD].astype(BF16) * 0.125
        qkv_ref[3 * heads + 1, rows] = projected[:, HD:].astype(BF16)
        return 0

    lax.fori_loop(0, length // wide, project_first, 0)

    row_in = lax.broadcasted_iota(jnp.int32, (BLK, 1), 0)
    col_in = lax.broadcasted_iota(jnp.int32, (1, span), 1)
    square_row = lax.broadcasted_iota(jnp.int32, (BLK, BLK), 0)
    square_col = lax.broadcasted_iota(jnp.int32, (BLK, BLK), 1)
    earlier = (square_col < square_row).astype(F32).astype(BF16)
    later = (square_col > square_row).astype(F32).astype(BF16)

    def window(b):
        start = pl.multiple_of(jnp.maximum(b * BLK + BLK - span, 0), BLK)
        return start, pl.ds(start, span)

    def masks(b):
        start, keys = window(b)
        same = seg_col_ref[rows_of(b)] == seg_row_ref[:, keys]
        behind = (row_in + (b * BLK - start)) - col_in
        return same & (behind >= 0), same & (behind > 0)

    def two_part(matrix, values):
        high = values.astype(BF16)
        low = (values - high.astype(F32)).astype(BF16)
        return dot(matrix, high, NN) + dot(matrix, low, NN)

    carry_ref[...] = jnp.zeros_like(carry_ref)

    def attend(b, _):
        rows = rows_of(b)
        _, keys = window(b)
        allowed, strict = masks(b)
        first = dot(qkv_ref[3 * heads, rows], qkv_ref[3 * heads + 1, keys], NT) - shift
        soft = jnp.maximum(first, 0.0) + jnp.log1p(jnp.exp(-jnp.abs(first)))
        picks = jnp.where(strict, soft, 0.0)
        before = carry_ref[0:1, keys]
        penalty = (two_part(earlier, picks) + before).astype(BF16)
        carry_ref[0:1, keys] = before + jnp.sum(picks, axis=0, keepdims=True)
        pen_ref[rows] = penalty
        penalty = penalty.astype(F32)
        mixed = []
        for h in range(heads):
            raw = dot(qkv_ref[h, rows], qkv_ref[heads + h, keys], NT)
            logits = jnp.where(allowed, raw - penalty, -1e30)
            top = jnp.max(logits, axis=-1, keepdims=True)
            weights = jnp.exp(logits - top)
            total = jnp.sum(weights, axis=-1, keepdims=True)
            lse_ref[h, rows] = top + jnp.log(total)
            probs = (weights * (1.0 / total)).astype(BF16)
            mixed.append(dot(probs, qkv_ref[2 * heads + h, keys], NN))
        o = jnp.concatenate(mixed, axis=1).astype(BF16)
        o_ref[rows] = o
        x1_ref[rows] = dot(o, wo_ref[...], NT).astype(BF16)
        one.enter(b)

        @pl.when(b > 0)
        def _():
            one.add(b - 1)
            one.cross(b - 1)

        return 0

    lax.fori_loop(0, blocks, attend, 0)
    one.add(blocks - 1)
    one.cross(blocks - 1)

    def act_back(i, _):
        rows = wide_rows(i)
        dres_ref[rows] = dot(dy_ref[rows], w2_ref[...], NN)
        return 0

    lax.fori_loop(0, length // wide, act_back, 0)

    def mlp(b, _):
        @pl.when(b == 0)
        def _():
            one.relay(0)

        @pl.when(b < blocks - 1)
        def _():
            one.relay(b + 1)

        @pl.when(b == blocks - 2)
        def _():
            for early in (0, 1):
                three.add(early)
                three.cross(early)

        one.arrived(b)
        rows = rows_of(b)
        resid = x_ref[rows].astype(F32) + one.sums(b)
        resid_ref[rows] = resid
        plain, _ = plain_norm(resid)
        cn = (plain * gain_two + bias_two).astype(BF16)
        cn_ref[rows] = cn
        u = dot(cn, w1_ref[...], NN)
        root = math.sqrt(2.0 / math.pi)
        square = u * u
        bent = jnp.tanh(root * u * (1.0 + 0.044715 * square))
        half = 0.5 * (1.0 + bent)
        s_ref[rows] = (u * half).astype(BF16)
        slope = half + 0.5 * u * (1.0 - bent * bent) * (root * (1.0 + 3 * 0.044715 * square))
        du = (dres_ref[rows] * slope).astype(BF16)
        du_ref[rows] = du
        x3_ref[rows] = dot(du, w1_ref[...], NT).astype(BF16)
        three.enter(b)
        return 0

    lax.fori_loop(0, blocks, mlp, 0)

    def cross_back(i, _):
        three.add(blocks - 1 - i)
        three.cross(blocks - 1 - i)
        return 0

    lax.fori_loop(0, blocks - 2, cross_back, 0)
    g2_ref[...] = dot(dy_ref[...], s_ref[...], TN).astype(BF16)
    g1_ref[...] = dot(cn_ref[...], du_ref[...], TN).astype(BF16)

    for early in (0, 1):
        three.relay(early)
    three.relay(blocks - 1)
    ng_ref[...] = jnp.zeros_like(ng_ref)
    carry_ref[...] = jnp.zeros_like(carry_ref)
    dkv_ref[...] = jnp.zeros_like(dkv_ref)

    def back(i, _):
        b = blocks - 1 - i

        @pl.when(b > 2)
        def _():
            three.relay(b - 1)

        three.arrived(b)
        rows = rows_of(b)
        _, keys = window(b)
        plain, inverse_std = plain_norm(resid_ref[rows])
        d_two = three.sums(b)
        ng_ref[0:1, :] += jnp.sum(d_two * plain, axis=0, keepdims=True)
        ng_ref[1:2, :] += jnp.sum(d_two, axis=0, keepdims=True)
        dres = dy_ref[rows].astype(F32) + norm_back(plain, inverse_std, d_two * gain_two)
        dres_ref[rows] = dres
        dhb = dres.astype(BF16)
        dhb_ref[rows] = dhb
        do = dot(dhb, wo_ref[...], NN).astype(BF16)
        allowed, strict = masks(b)
        penalty = pen_ref[rows].astype(F32)
        total = None
        dq = []
        for h in range(heads):
            q, k, v = qkv_ref[h, rows], qkv_ref[heads + h, keys], qkv_ref[2 * heads + h, keys]
            do_h = do[:, h * HD : (h + 1) * HD]
            logits = jnp.where(allowed, dot(q, k, NT) - penalty, -1e30)
            probs = jnp.exp(logits - lse_ref[h, rows])
            dprobs = dot(do_h, v, NT)
            inner = jnp.sum(dprobs * probs, axis=-1, keepdims=True)
            dlogits = probs * (dprobs - inner)
            total = dlogits if total is None else total + dlogits
            draw = dlogits.astype(BF16)
            dq.append(dot(draw, k, NN) * 0.125)
            dkv_ref[h * HD : (h + 1) * HD, keys] += dot(q, draw, TN)
            dkv_ref[attn + h * HD : attn + (h + 1) * HD, keys] += dot(do_h, probs.astype(BF16), TN)
        q, k = qkv_ref[3 * heads, rows], qkv_ref[3 * heads + 1, keys]
        first = dot(q, k, NT) - shift
        picked = 1.0 / (1.0 + jnp.exp(-first))
        after = carry_ref[0:1, keys]
        suffix = two_part(later, total) + after
        carry_ref[0:1, keys] = after + jnp.sum(total, axis=0, keepdims=True)
        draw = jnp.where(strict, -picked * suffix, 0.0).astype(BF16)
        dq.append(dot(draw, k, NN) * 0.125)
        dkv_ref[2 * attn : 2 * attn + HD, keys] += dot(q, draw, TN)
        dproj_ref[rows, :attn] = jnp.concatenate(dq[:heads], axis=1).astype(BF16)
        dproj_ref[rows, 3 * attn : 3 * attn + HD] = dq[heads].astype(BF16)
        return 0

    lax.fori_loop(0, blocks, back, 0)
    turned = dkv_ref[...].T.astype(BF16)
    dproj_ref[:, attn : 3 * attn] = turned[:, : 2 * attn]
    dproj_ref[:, 3 * attn + HD : 3 * attn + 2 * HD] = turned[:, 2 * attn :]

    def collect(src, dst, where, i):
        return remote(src, dst, collect_sem.at[i], collect_sem.at[i + 2], where)

    gf_ref[...] = dot(a_ref[...], dproj_ref[:, 3 * attn :], TN).astype(BF16)

    @pl.when(core == 1)
    def _():
        collect(gf_ref, gf_near, beside, 0).start()

    @pl.when(core == 0)
    def _():
        collect(gf_ref, gf_near, beside, 0).wait_recv()
        gf_ref[...] = (gf_ref[...].astype(F32) + gf_near[...].astype(F32)).astype(BF16)

    @pl.when(t == 2)
    def _():
        collect(gf_ref, gf_far, over, 1).start()

    go_ref[...] = dot(dhb_ref[...], o_ref[...], TN).astype(BF16)
    grad = dot(a_ref[...], dproj_ref[:, : 3 * attn], TN)
    gp_ref[...] = grad.astype(BF16)

    def finish(i, _):
        rows = wide_rows(i)
        out_ref[rows] = dot(s_ref[rows], w2_ref[...], NT).astype(BF16)
        da = dot(dproj_ref[rows, : 3 * attn], wp_ref[...], NT)
        da_ref[rows] = (da + dot(dproj_ref[rows, 3 * attn :], wf_ref[...], NT)).astype(BF16)
        return 0

    lax.fori_loop(0, length // wide, finish, 0)

    @pl.when(t == 0)
    def _():
        collect(gf_ref, gf_far, over, 1).wait_recv()
        extra = gf_ref[...].astype(F32) + gf_far[...].astype(F32)
        gp_ref[:, :HD] = (gp_ref[:, :HD].astype(F32) + extra[:, :HD]).astype(BF16)
        gp_ref[:, attn : attn + HD] = (gp_ref[:, attn : attn + HD].astype(F32) + extra[:, HD:]).astype(BF16)
        give(over, 0).wait_send()

    @pl.when(core == 0)
    def _():
        give(beside, 1).wait_send()

    @pl.when(core == 1)
    def _():
        collect(gf_ref, gf_near, beside, 0).wait_send()

    @pl.when(t == 2)
    def _():
        collect(gf_ref, gf_far, over, 1).wait_send()

    def close(b, _):
        one.close(b)
        three.close(b)
        return 0

    lax.fori_loop(0, blocks, close, 0)


def layer(inputs, segments, cotangent, wp, w1, wo, w2, norms):
    length, width = inputs.shape
    attn, hidden = wo.shape[1], w1.shape[1]
    heads = attn // HD
    blocks = length // BLK
    span = min(length // 2 + BLK, length)

    def low(*shape):
        return pltpu.VMEM(shape, BF16)

    half = length // 2
    total = [low(length, width)] + [low(half, width)] * 5 + [pltpu.SemaphoreType.DMA((8, blocks))]

    def out(shape, dtype):
        return jax.ShapeDtypeStruct(shape, dtype)

    return pl.pallas_call(
        functools.partial(layer_kernel, heads, shift_for(length)),
        out_shape=[
            out(wp.shape, BF16),
            out(w1.shape, BF16),
            out(wo.shape, BF16),
            out(w2.shape, BF16),
            out((length, width), BF16),
            out((length, width), BF16),
            out((length, width), F32),
            out((length, width), F32),
            out((2, width), F32),
        ],
        in_specs=[VM] * 9,
        out_specs=[VM] * 9,
        scratch_shapes=[
            low(length, width),
            low(width, 2 * HD),
            low(3 * heads + 2, length, HD),
            low(length, span),
            pltpu.VMEM((heads, length, 1), F32),
            low(length, attn),
            low(length, width),
            low(length, hidden),
            low(length, hidden),
            low(length, width),
            low(length, 3 * attn + 2 * HD),
            pltpu.VMEM((2 * attn + HD, length), F32),
            pltpu.VMEM((8, length), F32),
        ]
        + total
        + total
        + [low(width, 2 * HD)] * 3
        + [pltpu.SemaphoreType.DMA((3,)), pltpu.SemaphoreType.DMA((4,))],
        compiler_params=pltpu.CompilerParams(
            collective_id=3, has_side_effects=True, vmem_limit_bytes=LAYER_LIMIT
        ),
        name="layer",
    )(
        inputs,
        segments.reshape(1, length),
        segments.reshape(length, 1),
        cotangent,
        wp,
        w1,
        wo,
        w2,
        norms,
    )


def settle_kernel(
    n,
    p_ref,
    out_in,
    da_in,
    resid_ref,
    dres_ref,
    x_ref,
    norm_ref,
    ng_in,
    g_ref,
    output_ref,
    grad_ref,
    ng_ref,
    xin,
    lin,
    rin,
    x_send,
    x_recv,
    l_send,
    l_recv,
    r_send,
    r_recv,
    near4,
    mine4,
    far4,
    near_mine4,
    near_far4,
    sem4,
    near2,
    mine2,
    far2,
    near_mine2,
    near_far2,
    sem2,
    norm_held,
    norm_send,
    norm_recv,
):
    m = n // 2
    dp, t = lax.axis_index("dp"), lax.axis_index("tensor")
    place, side = dp // 2, lax.rem(dp, 2)
    pair = (place * 2 + 1 - side, t)
    four = Total(dp, t, da_in, near4, mine4, far4, near_mine4, near_far4, sem4)
    two = Total(dp, t, out_in, near2, mine2, far2, near_mine2, near_far2, sem2)
    blocks = four.blocks
    peers = [lax.rem(dp + hop, n) for hop in range(1, n)]
    greet([four.beside, four.over] + [(peer, t) for peer in peers])

    def across(q):
        return remote(p_ref.at[q * 2 + 1 - side], xin.at[q], x_send.at[q], x_recv.at[q], pair)

    def rightward(q):
        return remote(lin.at[q], lin.at[q], r_send.at[q], l_recv.at[q], (dp + 2, t))

    def leftward(q):
        return remote(rin.at[q], rin.at[q], l_send.at[q], r_recv.at[q], (dp - 2, t))

    def both(hop, one):
        @pl.when(place + hop < m)
        def _():
            one(place + hop, True)

        if hop > 0:
            @pl.when(place - hop >= 0)
            def _():
                one(place - hop, False)

    def work(q, right):
        across(q).wait_recv()
        own = p_ref[q * 2 + side].astype(F32) + xin[q].astype(F32)
        if right:
            @pl.when(place > 0)
            def _():
                rightward(q).wait_recv()
                lin[q] = (own + lin[q].astype(F32)).astype(BF16)

            @pl.when(place == 0)
            def _():
                lin[q] = own.astype(BF16)

            rightward(q).start()
        else:
            @pl.when(place < m - 1)
            def _():
                leftward(q).wait_recv()
                rin[q] = (own + rin[q].astype(F32)).astype(BF16)

            @pl.when(place == m - 1)
            def _():
                rin[q] = own.astype(BF16)

            leftward(q).start()

    def keep():
        q = place
        across(q).wait_recv()
        g_ref[...] = p_ref[q * 2 + side].astype(F32) + xin[q].astype(F32)

        @pl.when(place > 0)
        def _():
            rightward(q).wait_recv()
            g_ref[...] += lin[q].astype(F32)

        @pl.when(place < m - 1)
        def _():
            leftward(q).wait_recv()
            g_ref[...] += rin[q].astype(F32)

    def norm_copy(peer):
        return remote(ng_ref, norm_held.at[dp], norm_send.at[peer], norm_recv.at[dp], (peer, t))

    def norm_from(peer):
        return remote(ng_ref, norm_held.at[peer], norm_send.at[peer], norm_recv.at[peer], (peer, t))

    for hop in reversed(range(m)):
        both(hop, lambda q, right: across(q).start())
    for b in range(blocks):
        four.enter(b)
    for b in range(blocks):
        two.enter(b)
    for b in range(blocks):
        four.add(b)
        four.cross(b)
    for b in range(blocks):
        two.add(b)
        two.cross(b)
    ng_ref[...] = jnp.zeros_like(ng_ref)
    gain = norm_ref[0:1, :]

    def rows_of(b):
        return pl.ds(b * four.size, four.size)

    def grad_block(b):
        rows = rows_of(b)
        four.arrived(b)
        d_one = four.sums(b)
        plain, inverse_std = plain_norm(x_ref[rows].astype(F32))
        ng_ref[0:1, :] += jnp.sum(d_one * plain, axis=0, keepdims=True)
        ng_ref[1:2, :] += jnp.sum(d_one, axis=0, keepdims=True)
        grad_ref[rows] = dres_ref[rows] + norm_back(plain, inverse_std, d_one * gain)

    def out_block(b):
        rows = rows_of(b)
        two.arrived(b)
        output_ref[rows] = (resid_ref[rows] + two.sums(b)).astype(BF16)

    def norms_out():
        ng_ref[2:4, :] = ng_in[...]
        for peer in peers:
            norm_copy(peer).start()

    def norms_in():
        for peer in peers:
            norm_from(peer).wait_recv()
        total = None
        for source in range(n):
            term = jnp.where(dp == source, ng_ref[...], norm_held[source])
            total = term if total is None else total + term
        for peer in peers:
            norm_copy(peer).wait_send()
        ng_ref[...] = total

    tasks = []
    for b in range(blocks):
        tasks.append(functools.partial(four.relay, b))
        if b > 0:
            tasks.append(functools.partial(grad_block, b - 1))
    tasks.append(functools.partial(grad_block, blocks - 1))
    tasks.append(norms_out)
    for b in range(blocks):
        tasks.append(functools.partial(two.relay, b))
        if b > 0:
            tasks.append(functools.partial(out_block, b - 1))
    tasks.append(functools.partial(out_block, blocks - 1))
    done = 0
    for step, hop in enumerate(reversed(range(1, m))):
        until = len(tasks) * (step + 1) // m
        while done < until:
            tasks[done]()
            done += 1
        both(hop, work)
    while done < len(tasks):
        tasks[done]()
        done += 1
    keep()
    norms_in()

    def finish(q, _):
        across(q).wait_send()

        @pl.when(q > place)
        def _():
            rightward(q).wait_send()

        @pl.when(q < place)
        def _():
            leftward(q).wait_send()

        return 0

    lax.fori_loop(0, m, finish, 0)
    for b in range(blocks):
        four.close(b)
        two.close(b)


def settle(packed, out_part, da_part, resid, dres, inputs, norms, ng):
    n, block, wide = packed.shape
    m = n // 2
    length, width = inputs.shape
    blocks = 4

    def low(*shape):
        return pltpu.VMEM(shape, BF16)

    half = length // 2
    total = [low(half, width)] * 5 + [pltpu.SemaphoreType.DMA((8, blocks))]
    return pl.pallas_call(
        functools.partial(settle_kernel, n),
        out_shape=[
            jax.ShapeDtypeStruct((block, wide), F32),
            jax.ShapeDtypeStruct((length, width), BF16),
            jax.ShapeDtypeStruct((length, width), F32),
            jax.ShapeDtypeStruct((4, width), F32),
        ],
        in_specs=[VM] * 8,
        out_specs=[VM] * 4,
        scratch_shapes=[low(m, block, wide)] * 3
        + [pltpu.SemaphoreType.DMA((m,))] * 6
        + total
        + total
        + [pltpu.VMEM((n, 4, width), F32), pltpu.SemaphoreType.DMA((n,)), pltpu.SemaphoreType.DMA((n,))],
        compiler_params=pltpu.CompilerParams(
            collective_id=2, has_side_effects=True, vmem_limit_bytes=24 * MIB
        ),
        name="settle",
    )(packed, out_part, da_part, resid, dres, inputs, norms, ng)


def norm_update(grad, master, first, second):
    new_first = beta_one * first + (1.0 - beta_one) * grad
    new_second = beta_two * second + (1.0 - beta_two) * grad * grad
    direction = (
        new_first
        / (1.0 - beta_one**STEP)
        / (jnp.sqrt(new_second / (1.0 - beta_two**STEP)) + adam_eps)
    )
    return (new_first, new_second, master - norm_rate * direction)


def body(
    inputs,
    segments,
    cotangent,
    owner,
    masters,
    first_moment,
    second_moment,
    left_stats,
    right_stats,
    left_basis,
    right_basis,
    norm_master,
    norm_first,
    norm_second,
):
    length = inputs.shape[1]
    width = inputs.shape[2]
    n_dp = lax.axis_size("dp")
    parts = lax.axis_size("tensor")
    per_dev = masters.shape[1]
    block = masters.shape[-1]
    blocks, shared_norms = gather_masters(masters[0], norm_master, n_dp)
    slots, inverse = block_slots(owner, per_dev)
    pieces = assemble(slots, blocks, width // block, parts)
    norms = shared_norms.astype(F32).reshape(4, width)
    *grads, out_part, da_part, resid, dres, norm_grads = layer(
        inputs[0], segments[0], cotangent[0], *pieces, norms
    )
    packed = disperse(inverse, grads, n_dp, block, parts)
    own_packed, output, input_grad, norm_grads = settle(
        packed, out_part, da_part, resid, dres, inputs[0], norms, norm_grads
    )
    own_grads = own_packed[:, : per_dev * block].reshape(block, per_dev, block).transpose(1, 0, 2)
    norm_per = norm_master.shape[0]
    own_norm_grads = lax.dynamic_slice_in_dim(
        norm_grads.reshape(-1), lax.axis_index("dp") * norm_per, norm_per
    )
    new_first, new_second, new_master, new_left, new_right, left_next, right_next = soap(
        own_grads,
        masters[0],
        first_moment[0],
        second_moment[0],
        left_stats[0],
        right_stats[0],
        left_basis[0],
        right_basis[0],
    )
    norm_first_new, norm_second_new, norm_new = norm_update(
        own_norm_grads, norm_master, norm_first, norm_second
    )
    return (
        output[None],
        input_grad[None],
        new_first[None],
        new_second[None],
        new_master[None],
        new_left[None],
        new_right[None],
        left_next[None],
        right_next[None],
        norm_first_new,
        norm_second_new,
        norm_new,
    )


def solution(mesh):
    in_specs = (
        P("dp", None, None),
        P("dp", None),
        P("dp", None, None),
        P(),
        P("tensor", "dp", None, None),
        P("tensor", "dp", None, None),
        P("tensor", "dp", None, None),
        P("tensor", "dp", None, None),
        P("tensor", "dp", None, None),
        P("tensor", "dp", None, None),
        P("tensor", "dp", None, None),
        P("dp"),
        P("dp"),
        P("dp"),
    )
    out_specs = (
        P("dp", None, None),
        P("dp", None, None),
        P("tensor", "dp", None, None),
        P("tensor", "dp", None, None),
        P("tensor", "dp", None, None),
        P("tensor", "dp", None, None),
        P("tensor", "dp", None, None),
        P("tensor", "dp", None, None),
        P("tensor", "dp", None, None),
        P("dp"),
        P("dp"),
        P("dp"),
    )
    return jax.shard_map(body, mesh=mesh, in_specs=in_specs, out_specs=out_specs, check_vma=False)
```

time: 1210 us -> 355 us (0.29)
  waiting for transfers between devices: 636 us -> 0 us
  Pallas kernels: 85.7 us -> 283 us
  local copies, waits for them, and re-layouts: 212 us -> 67.3 us
  other arithmetic: 112 us -> 2.81 us
  blocking collectives: 73.2 us -> 0 us
  matrix products: 63.8 us -> 0 us
  between operations: 16.1 us -> 0.86 us
    reduce_scatter x2 -> x0, waiting for transfers between devices: 311 us -> none  [the longest x1 266 us: body(): lax.psum_scatter(stored_grads, 'dp', scatter_dimension=0, tiled=True)]
    psum x4 -> x0, waiting for transfers between devices: 208 us -> none  [the longest x1 68.2 us: body(): attn_total = lax.psum(contract_cols(attended_flat, w_out_side), 'tensor')]
    pallas_call x0 -> x5, Pallas kernels: none -> 197 us  [the longest x1 81.8 us: layer(): pl.pallas_call(functools.partial(layer_kernel, heads, shift_for(length)),...]
    all_gather x2 -> x0, waiting for transfers between devices: 117 us -> none  [the longest x1 108 us: body(): lax.all_gather(masters[0].astype(jnp.bfloat16), 'dp', axis=0, tiled=True)]
    dot_general x18 -> x0, matrix products: 63.8 us -> none  [the longest x4 17.2 us: contract_cols(): lax.dot_general(left, right, (((1,), (1,)), ((), ())), preferred_element_...]
    reshape x3, local copies, waits for them, and re-layouts: 48.4 us -> 7.68 us  [the longest x2 7.67 us: body(): own_packed[:, :per_dev * block].reshape(block, per_dev, block)]
    unnamed x1 -> x0, blocking collectives: 39.3 us -> none
    another operation x11 -> x1, local copies, waits for them, and re-layouts: 37.5 us -> 1.71 us  [layer(): segments.reshape(length, 1)]
  transfers between devices with their start and end apart: 8 -> 0, of which waited for: 8 -> 0; matrix products, arithmetic and copies ran while one was open for 11% -> 0% of each run, Pallas kernels for 0% -> 0%
where the time goes in v3:
time: 355 us; the launch traced here: 354 us
  Pallas kernels  283 us (80%)
  local copies, waits for them, and re-layouts  67.3 us (19%)
    pallas_call x1, Pallas kernels, soap(): pl.pallas_call(functools.partial(soap_kernel, count, chunk, block), grid=...  85.9 us
    pallas_call x1, Pallas kernels, layer(): pl.pallas_call(functools.partial(layer_kernel, heads, shift_for(length)),...  81.8 us
    unnamed x55, local copies, waits for them, and re-layouts  57.9 us
    pallas_call x1, Pallas kernels, settle(): pl.pallas_call(functools.partial(settle_kernel, n), out_shape=[jax.ShapeD...  52.5 us
    pallas_call x1, Pallas kernels, gather_masters(): pl.pallas_call(functools.partial(gather_kernel, n, count, block, wide, no...  47.6 us
    pallas_call x1, Pallas kernels, disperse(): pl.pallas_call(functools.partial(disperse_kernel, rows, cols, block, piec...  11.2 us
    reshape x2, local copies, waits for them, and re-layouts, body(): own_packed[:, :per_dev * block].reshape(block, per_dev, block)  7.67 us

profile of v3, /device:TPU:0, one launch (start us, length us, event | category | flops | bytes accessed | tf_op | source)
XLA Modules:
  0.0 353.7 jit_solution(6059065514110770206)
XLA Ops:
  4.5 2.0 copy.56
  6.5 3.6 %copy.59 = f32[1,96,48,48]{3,2,1,0:T(8,128)} copy(f32[1,96,48,48]{1,3,2,0:T(8,128)} %param.19) | data formatting | bytes 1769472 | tf_op args[5]
  10.1 3.0 copy.60
  13.0 3.0 copy.61
  16.0 3.0 copy.62
  19.0 2.9 copy.63
  21.9 3.0 copy.64
  24.9 47.6 %gather_masters.1 = (bf16[768,48,48]{2,1,0:T(8,128)(2,1)S(1)}, bf16[8,16,128]{2,1,0:T(8,128)(2,1)S(1)}) custom-call(f32[96,48,48]{2,1,0:T(8,128)S(1)} %bitcast.27, f32[3,128]{1,0:T(4,128)S(1)} %bitcast.37), custom_call_target="tpu_custom_call" | custom-call | tf_op jit(solution)/shard_map/gather_masters/pallas_call | solution.py:291
  72.5 3.8 %assemble.1 = (bf16[768,576]{1,0:T(8,128)(2,1)S(1)}, bf16[768,768]{1,0:T(8,128)(2,1)S(1)}, bf16[768,192]{1,0:T(8,128)(2,1)S(1)}, bf16[768,768]{1,0:T(8,128)(2,1)S(1)}) custom-call(s32[768]{0:T(1024)S(1)} %multiply_add_fusion.slot_ref, bf16[768,48,48]{2,1,0:T(8,128)(2,1)S(1)} %get-tuple-element.38.u_ref), custom_call_target="tpu_custom_call" | custom-call | tf_op jit(solution)/shard_map/assemble/pallas_call | solution.py:330
  81.5 81.8 %layer.1 = (bf16[768,576]{1,0:T(8,128)(2,1)S(1)}, bf16[768,768]{1,0:T(8,128)(2,1)S(1)}, bf16[768,192]{1,0:T(8,128)(2,1)S(1)}, bf16[768,768]{1,0:T(8,128)(2,1)S(1...) custom-call(bf16[1024,768]{1,0:T(8,128)(2,1)} %bitcast.29, ...), custom_call_target="tpu_custom_call" | custom-call | tf_op jit(solution)/shard_map/layer/pallas_call | solution.py:824
  163.4 11.2 %disperse.1.p_ref = bf16[8,48,4608]{2,1,0:T(8,128)(2,1)S(1)} custom-call(s32[768]{0:T(1024)S(1)} %select_reduce_fusion.inverse_ref, bf16[768,576]{1,0:T(8,128)(2,1)S(1)} %get-tuple-element.44.refs_0_, bf16[768,768]{1,0:T(8,128)(2,1)S(1)} %get-tuple-element.45.refs_1_, bf16[768,192]{1,0:T(8,128)(2,1)S(1)} %get-tuple-element.46.refs_2_, ...), custom_call_target="tpu_custom_call" | custom-call | tf_op jit(solution)/shard_map/disperse/pallas_call | solution.py:370
  174.6 1.9 copy-done.3
  177.9 52.5 %settle.1 = (f32[48,4608]{1,0:T(8,128)S(1)}, bf16[1024,768]{1,0:T(8,128)(2,1)S(1)}, f32[1024,768]{1,0:T(8,128)S(1)}, f32[4,768]{1,0:T(4,128)S(1)}) custom-call(bf16[8,48,4608]{2,1,0:T(8,128)(2,1)S(1)} %disperse.1.p_ref, bf16[1024,768]{1,0:T(8,128)(2,1)S(1)} %copy-done.7, bf16[1024,768]{1,0:T(8,128)(2,1)S(1)} %copy-done.8, f32[1024,768]{1,0:T(8,128)S(1)} %copy-done.2, ...), custom_call_target="tpu_custom_call" | custom-call | tf_op jit(solution)/shard_map/settle/pallas_call | solution.py:1093
  233.2 3.1 reshape.46
  236.4 4.5 %copy.75 = f32[48,96,48]{2,0,1:T(8,128)} copy(f32[48,96,48]{2,1,0:T(8,128)} %reshape.46) | data formatting | bytes 1769472 | tf_op jit(solution)/shard_map/reshape | solution.py:1159
  240.9 85.9 %soap.1 = (f32[96,48,48]{2,1,0:T(8,128)S(1)}, f32[96,48,48]{2,1,0:T(8,128)S(1)}, f32[96,48,48]{2,1,0:T(8,128)}, f32[96,48,48]{2,1,0:T(8,128)}, f32[96,48,48]{2,1...) custom-call(f32[96,48,48]{2,1,0:T(8,128)} %bitcast.44, f32[96,48,48]{2,1,0:T(8,128)} %bitcast.28, ...), custom_call_target="tpu_custom_call" | custom-call | tf_op jit(solution)/shard_map/soap/pallas_call | solution.py:143
  329.6 2.8 copy.65
  332.4 2.8 copy.66
  335.3 2.8 copy.67
  338.1 2.8 copy.68
  340.9 2.8 copy.69
  343.8 2.8 copy.70
  346.6 2.8 copy.71
  349.4 2.7 copy.79
  (47 shorter events, 17.8 us)
Async XLA Ops:
  6.5 18.4 %copy-start = (f32[1,96,48,48]{3,2,1,0:T(8,128)}, f32[1,96,48,48]{3,2,1,0:T(8,128)S(1)}, u32[]{:S(2)}) copy-start(f32[1,96,48,48]{3,2,1,0:T(8,128)S(1)} %copy.56) | copy-start | bytes 2654212
  21.9 3.0 copy-start.16
  72.4 6.8 %copy-start.15 = (s32[1,1024]{1,0:T(1,128)S(1)}, s32[1,1024]{1,0:T(1,128)}, u32[]{:S(2)}) copy-start(s32[1,1024]{1,0:T(1,128)} %seg_row_ref.1) | copy-start | bytes 12292
  76.3 1.0 copy-start.10
  77.3 1.0 copy-start.11
  78.3 0.9 copy-start.12
  79.3 1.0 copy-start.6
  80.3 1.2 copy-start.13
  163.4 11.2 %copy-start.1 = (bf16[1,1024,768]{2,1,0:T(8,128)(2,1)S(1)}, bf16[1,1024,768]{2,1,0:T(8,128)(2,1)}, u32[]{:S(2)}) copy-start(bf16[1,1024,768]{2,1,0:T(8,128)(2,1)} %param.14) | copy-start | bytes 4718596
  163.4 11.2 %copy-start.2 = (f32[1024,768]{1,0:T(8,128)S(1)}, f32[1024,768]{1,0:T(8,128)}, u32[]{:S(2)}) copy-start(f32[1024,768]{1,0:T(8,128)} %get-tuple-element.50.resid_ref) | copy-start | bytes 9437188
  163.4 11.2 %copy-start.7 = (bf16[1024,768]{1,0:T(8,128)(2,1)S(1)}, bf16[1024,768]{1,0:T(8,128)(2,1)}, u32[]{:S(2)}) copy-start(bf16[1024,768]{1,0:T(8,128)(2,1)} %get-tuple-element.48.out_in) | copy-start | bytes 4718596
  174.6 1.9 copy-start.3
  176.5 1.4 copy-start.8
  177.9 54.6 %copy-start.17 = (f32[384]{0:T(512)S(1)}, f32[384]{0:T(512)}, u32[]{:S(2)}) copy-start(f32[384]{0:T(512)} %param.27) | copy-start | bytes 4612
  177.9 54.6 %copy-start.18 = (f32[384]{0:T(512)S(1)}, f32[384]{0:T(512)}, u32[]{:S(2)}) copy-start(f32[384]{0:T(512)} %param.26) | copy-start | bytes 4612
  230.5 1.2 copy-start.9
  231.6 0.9 copy-start.14
  326.8 1.4 copy-start.4
  328.2 1.4 copy-start.5

commit v4 on v3

--- a/solution.py
+++ b/solution.py
@@ -44,112 +44,6 @@
         - jnp.mean(grad, axis=-1, keepdims=True)
         - plain * jnp.mean(grad * plain, axis=-1, keepdims=True)
     )
-
-
-def split3(v):
-    hi = v.astype(BF16)
-    return hi, (v - hi.astype(F32)).astype(BF16)
-
-def prod(left, right, dims):
-    lh, ll = left
-    rh, rl = right
-    spec = (dims, ((), ()))
-    def one(a, b):
-        return lax.dot_general(a, b, spec, preferred_element_type=F32)
-    return one(lh, rh) + (one(lh, rl) + one(ll, rh))
-
-NN = ((1,), (0,))
-NT = ((1,), (1,))
-TN = ((0,), (0,))
-
-def soap_kernel(count, chunk, block, g_ref, m_ref, f_ref, s_ref, l_ref, r_ref, ql_ref, qr_ref,
-                nf_ref, ns_ref, nm_ref, nl_ref, nr_ref, bl_ref, br_ref, a_scr, t_scr):
-    step = pl.program_id(0)
-    tiles = block // 8
-    for c in range(chunk):
-        g = g_ref[c]
-        ql, qr = split3(ql_ref[c]), split3(qr_ref[c])
-        gs = split3(g)
-        gt = split3(g.T)
-        new_left = beta_stats * l_ref[c] + (1.0 - beta_stats) * prod(gs, gs, NT)
-        new_right = beta_stats * r_ref[c] + (1.0 - beta_stats) * prod(gt, gt, NT)
-        nl_ref[c] = new_left
-        nr_ref[c] = new_right
-        half = prod(gt, ql, NN)
-        rot = prod(split3(half.T), qr, NN)
-        first = beta_one * f_ref[c] + (1.0 - beta_one) * rot
-        second = beta_two * s_ref[c] + (1.0 - beta_two) * rot * rot
-        nf_ref[c] = first
-        ns_ref[c] = second
-        direction = first / (1.0 - beta_one**STEP) / (
-            jnp.sqrt(second / (1.0 - beta_two**STEP)) + adam_eps)
-        moved = prod(split3(prod(ql, split3(direction), NN)), qr, NT)
-        master = m_ref[c]
-        nm_ref[c] = master - learn_rate * (moved + weight_decay * master)
-        a_scr[0, step * chunk + c] = prod(split3(new_left), ql, NN)
-        a_scr[1, step * chunk + c] = prod(split3(new_right), qr, NN)
-
-    @pl.when(step == pl.num_programs(0) - 1)
-    def _():
-        def bring(i, _):
-            for s in range(2):
-                slab = a_scr[s, :, pl.ds(i, 1), :].reshape(128, block)
-                t_scr[s, i] = slab.T
-            return 0
-        lax.fori_loop(0, block, bring, 0, unroll=4)
-        sub = lax.broadcasted_iota(jnp.int32, (8, 128), 0)
-        norms = [[None] * tiles, [None] * tiles]
-        for kt in range(tiles):
-            def one(kk, carry):
-                k = kt * 8 + kk
-                acc = [[jnp.zeros((8, 128), F32) for _ in range(kt, tiles)] for _ in range(2)]
-                for i in range(block):
-                    for s in range(2):
-                        row = jnp.broadcast_to(t_scr[s, i, pl.ds(k, 1), :], (8, 128))
-                        for j in range(kt, tiles):
-                            acc[s][j - kt] += row * t_scr[s, i, 8 * j : 8 * j + 8, :]
-                out = []
-                for s in range(2):
-                    here = sub == kk
-                    size = jnp.sum(jnp.where(here, acc[s][0], 0.0), axis=0, keepdims=True)
-                    size = jnp.broadcast_to(size, (8, 128))
-                    inv = 1.0 / size
-                    acc[s] = [v * inv for v in acc[s]]
-                    acc[s][0] = jnp.where(sub > kk, acc[s][0], 0.0)
-                    out.append(jnp.where(here, size, carry[s]))
-                for i in range(block):
-                    for s in range(2):
-                        row = jnp.broadcast_to(t_scr[s, i, pl.ds(k, 1), :], (8, 128))
-                        for j in range(kt, tiles):
-                            t_scr[s, i, 8 * j : 8 * j + 8, :] -= row * acc[s][j - kt]
-                return tuple(out)
-            res = lax.fori_loop(0, 8, one, (jnp.ones((8, 128), F32),) * 2)
-            for s in range(2):
-                norms[s][kt] = lax.rsqrt(res[s])
-        scale = [jnp.concatenate(norms[s], axis=0) for s in range(2)]
-        def back(i, _):
-            for s, ref in ((0, bl_ref), (1, br_ref)):
-                done = (t_scr[s, i] * scale[s]).T
-                ref[:, pl.ds(i, 1), :] = done[:count].reshape(count, 1, block)
-            return 0
-        lax.fori_loop(0, block, back, 0, unroll=4)
-
-def soap(g, m, f, s, l, r, ql, qr):
-    count, block = g.shape[0], g.shape[-1]
-    chunk = math.gcd(count, 8)
-    spec = pl.BlockSpec((chunk, block, block), lambda i: (i, 0, 0))
-    whole = pl.BlockSpec((count, block, block), lambda i: (0, 0, 0))
-    shape = jax.ShapeDtypeStruct(g.shape, F32)
-    return pl.pallas_call(
-        functools.partial(soap_kernel, count, chunk, block),
-        grid=(count // chunk,),
-        in_specs=[spec] * 8,
-        out_specs=[spec] * 5 + [whole] * 2,
-        out_shape=[shape] * 7,
-        scratch_shapes=[pltpu.VMEM((2, 128, block, block), F32), pltpu.VMEM((2, block, block, 128), F32)],
-        compiler_params=pltpu.CompilerParams(vmem_limit_bytes=48 * 2**20),
-        name="soap",
-    )(g, m, f, s, l, r, ql, qr)
 
 
 MESH = pl.DeviceIdType.MESH
@@ -305,6 +199,274 @@
         name="gather_masters",
     )(masters, norm_tile)
     return blocks, norms.reshape(n, 16 * 128)[:, : norm.shape[0]].reshape(-1)
+
+
+NN = ((1,), (0,))
+NT = ((1,), (1,))
+TN = ((0,), (0,))
+
+
+def lane_prod(n, lanes, left_row, right_tile, put, group=4):
+    tiles = n // 8
+
+    def some(step, _):
+        base = step * group
+
+        def one(k, acc):
+            rights = [right_tile(k, j) for j in range(tiles)]
+            out = []
+            for r in range(group):
+                row = jnp.broadcast_to(left_row(base + r, k), (8, lanes))
+                out.append(tuple(acc[r][j] + row * rights[j] for j in range(tiles)))
+            return tuple(out)
+
+        zero = tuple(tuple(jnp.zeros((8, lanes), F32) for _ in range(tiles)) for _ in range(group))
+        acc = lax.fori_loop(0, n, one, zero, unroll=8)
+        for r in range(group):
+            for j in range(tiles):
+                put(base + r, j, acc[r][j])
+        return 0
+
+    lax.fori_loop(0, n // group, some, 0)
+
+
+def lane_gram(n, lanes, row, tile, put, put_turned):
+    tiles = n // 8
+    for first in range(tiles):
+        columns = range(first, tiles)
+
+        def some(step, _):
+            base = first * 8 + step * 4
+
+            def one(k, acc):
+                rights = [tile(k, j) for j in columns]
+                out = []
+                for r in range(4):
+                    left = jnp.broadcast_to(row(base + r, k), (8, lanes))
+                    out.append(tuple(a + left * right for a, right in zip(acc[r], rights)))
+                return tuple(out)
+
+            zero = tuple(tuple(jnp.zeros((8, lanes), F32) for _ in columns) for _ in range(4))
+            acc = lax.fori_loop(0, n, one, zero, unroll=8)
+            for r in range(4):
+                for j in columns:
+                    put(base + r, j, acc[r][j - first])
+                    if j > first:
+                        put_turned(base + r, j, acc[r][j - first])
+            return 0
+
+        lax.fori_loop(0, 2, some, 0)
+
+
+def soap_kernel(
+    n,
+    count,
+    packed_ref,
+    m_ref,
+    f_ref,
+    s_ref,
+    l_ref,
+    r_ref,
+    ql_ref,
+    qr_ref,
+    nf_out,
+    ns_out,
+    nm_out,
+    nl_out,
+    nr_out,
+    bl_out,
+    br_out,
+    nf_ref,
+    ns_ref,
+    nm_ref,
+    nl_ref,
+    nr_ref,
+    basis_ref,
+    u_scr,
+    g_ref,
+    gt_ref,
+    qt_ref,
+    h_ref,
+    d_ref,
+    sems,
+):
+    tiles = n // 8
+
+    def at(ref):
+        def row(i, k):
+            return ref[pl.ds(i * n + k, 1), :]
+
+        return row
+
+    def at_turned(ref):
+        def row(i, k):
+            return ref[pl.ds(k * n + i, 1), :]
+
+        return row
+
+    def tile(ref):
+        def one(k, j):
+            return ref[pl.ds(pl.multiple_of(k * n + 8 * j, 8), 8), :]
+
+        return one
+
+    def turned(i, j):
+        return pl.ds(8 * j * n + i, 8, stride=n)
+
+    def turn_into(dst, src):
+        def one(k, _):
+            for j in range(tiles):
+                dst[here(k, j), :] = src[turned(k, j), :]
+            return 0
+
+        lax.fori_loop(0, n, one, 0, unroll=4)
+
+    def here(i, j):
+        return pl.ds(pl.multiple_of(i * n + 8 * j, 8), 8)
+
+    def send(place, src, dst):
+        return pltpu.make_async_copy(src, dst, sems.at[place])
+
+    for c in range(count):
+        u_scr[c] = packed_ref[:, c * n : (c + 1) * n]
+
+    def turn(i, _):
+        slab = u_scr[:, pl.ds(i, 1), :].reshape(count, n)
+        g_ref[pl.ds(pl.multiple_of(i * n, 8), n), :] = slab.T
+        return 0
+
+    lax.fori_loop(0, n, turn, 0, unroll=4)
+
+    turn_into(gt_ref, g_ref)
+    turn_into(qt_ref, qr_ref)
+
+    def blend(dst, old):
+        def put(i, j, value):
+            where = here(i, j)
+            dst[where, :] = beta_stats * old[where, :] + (1.0 - beta_stats) * value
+
+        def put_turned(i, j, value):
+            where = turned(i, j)
+            dst[where, :] = beta_stats * old[where, :] + (1.0 - beta_stats) * value
+
+        return put, put_turned
+
+    def store(ref, base=0):
+        def put(i, j, value):
+            ref[pl.ds(pl.multiple_of(base + i * n + 8 * j, 8), 8), :] = value
+
+        return put
+
+    lane_gram(n, count, at_turned(gt_ref), tile(gt_ref), *blend(nl_ref, l_ref))
+    send(3, nl_ref, nl_out).start()
+    lane_gram(n, count, at_turned(g_ref), tile(g_ref), *blend(nr_ref, r_ref))
+    send(4, nr_ref, nr_out).start()
+    lane_prod(n, count, at(nl_ref), tile(ql_ref), store(basis_ref))
+    lane_prod(n, count, at(nr_ref), tile(qr_ref), store(basis_ref, n * n))
+
+    sub = lax.broadcasted_iota(jnp.int32, (8, count), 0)
+    for panel in range(tiles):
+        def side(s, _):
+            base = pl.multiple_of(s * n * n, 8)
+
+            def spot(i, j):
+                return pl.ds(pl.multiple_of(base + i * n + 8 * j, 8), 8)
+
+            rows = [basis_ref[spot(i, panel), :] for i in range(n)]
+            sizes = jnp.ones((8, count), F32)
+            for k in range(8):
+                heads = [jnp.broadcast_to(row[k : k + 1], (8, count)) for row in rows]
+                terms = [head * row for head, row in zip(heads, rows)]
+                while len(terms) > 1:
+                    terms = [sum(terms[p : p + 2][1:], terms[p]) for p in range(0, len(terms), 2)]
+                size = jnp.broadcast_to(terms[0][k : k + 1], (8, count))
+                sizes = jnp.where(sub == k, size, sizes)
+                factor = jnp.where(sub > k, terms[0] * (1.0 / size), 0.0)
+                rows = [row - head * factor for head, row in zip(heads, rows)]
+            scale = lax.rsqrt(sizes)
+            for i in range(n):
+                basis_ref[spot(i, panel), :] = rows[i] * scale
+            for start in range(panel + 1, tiles, 3):
+                columns = range(start, min(start + 3, tiles))
+
+                def heads_of(i):
+                    return [
+                        jnp.broadcast_to(basis_ref[pl.ds(base + i * n + 8 * panel + k, 1), :], (8, count))
+                        for k in range(8)
+                    ]
+
+                def project(i, acc):
+                    heads = heads_of(i)
+                    values = [basis_ref[spot(i, j), :] for j in columns]
+                    return tuple(
+                        tuple(a + head * value for a, value in zip(acc[k], values))
+                        for k, head in enumerate(heads)
+                    )
+
+                zero = tuple(tuple(jnp.zeros((8, count), F32) for _ in columns) for _ in range(8))
+                parts = lax.fori_loop(0, n, project, zero, unroll=4)
+
+                def take(i, _):
+                    heads = heads_of(i)
+                    for c, j in enumerate(columns):
+                        value = basis_ref[spot(i, j), :]
+                        for k in range(8):
+                            value = value - heads[k] * parts[k][c]
+                        basis_ref[spot(i, j), :] = value
+                    return 0
+
+                lax.fori_loop(0, n, take, 0, unroll=4)
+            return 0
+
+        lax.fori_loop(0, 2, side, 0)
+    left_basis, right_basis = basis_ref.at[: n * n], basis_ref.at[n * n :]
+    send(5, left_basis, bl_out).start()
+    send(6, right_basis, br_out).start()
+
+    def put_moments(i, j, rot):
+        first = beta_one * f_ref[here(i, j), :] + (1.0 - beta_one) * rot
+        second = beta_two * s_ref[here(i, j), :] + (1.0 - beta_two) * rot * rot
+        nf_ref[here(i, j), :] = first
+        ns_ref[here(i, j), :] = second
+        d_ref[here(i, j), :] = first / (1.0 - beta_one**STEP) / (
+            jnp.sqrt(second / (1.0 - beta_two**STEP)) + adam_eps
+        )
+
+    def put_master(i, j, moved):
+        master = m_ref[here(i, j), :]
+        nm_ref[here(i, j), :] = master - learn_rate * (moved + weight_decay * master)
+
+    lane_prod(n, count, at_turned(ql_ref), tile(g_ref), store(h_ref))
+    lane_prod(n, count, at(h_ref), tile(qr_ref), put_moments)
+    send(0, nf_ref, nf_out).start()
+    send(1, ns_ref, ns_out).start()
+    lane_prod(n, count, at(ql_ref), tile(d_ref), store(h_ref))
+    lane_prod(n, count, at(h_ref), tile(qt_ref), put_master)
+    send(2, nm_ref, nm_out).start()
+    sources = (nf_ref, ns_ref, nm_ref, nl_ref, nr_ref, left_basis, right_basis)
+    targets = (nf_out, ns_out, nm_out, nl_out, nr_out, bl_out, br_out)
+    for place, (src, dst) in enumerate(zip(sources, targets)):
+        send(place, src, dst).wait()
+
+
+def soap(packed, *state):
+    count, n = state[0].shape[0], state[0].shape[-1]
+    flat = [item.transpose(1, 2, 0).reshape(n * n, count) for item in state]
+    shape = jax.ShapeDtypeStruct((n * n, count), F32)
+    room = pltpu.VMEM((n * n, count), F32)
+    outs = pl.pallas_call(
+        functools.partial(soap_kernel, n, count),
+        out_shape=[shape] * 7,
+        in_specs=[VM] * 8,
+        out_specs=[pl.BlockSpec(memory_space=pl.ANY)] * 7,
+        scratch_shapes=[room] * 5
+        + [pltpu.VMEM((2 * n * n, count), F32), pltpu.VMEM((count, n, n), F32)]
+        + [room] * 5
+        + [pltpu.SemaphoreType.DMA((7,))],
+        compiler_params=pltpu.CompilerParams(vmem_limit_bytes=24 * MIB),
+        name="soap",
+    )(packed, *flat)
+    return [item.reshape(n, n, count).transpose(2, 0, 1) for item in outs]
 
 
 def assemble_kernel(rows, cols, block, cuts, slot_ref, u_ref, *w_refs):
@@ -1156,13 +1318,12 @@
     own_packed, output, input_grad, norm_grads = settle(
         packed, out_part, da_part, resid, dres, inputs[0], norms, norm_grads
     )
-    own_grads = own_packed[:, : per_dev * block].reshape(block, per_dev, block).transpose(1, 0, 2)
     norm_per = norm_master.shape[0]
     own_norm_grads = lax.dynamic_slice_in_dim(
         norm_grads.reshape(-1), lax.axis_index("dp") * norm_per, norm_per
     )
     new_first, new_second, new_master, new_left, new_right, left_next, right_next = soap(
-        own_grads,
+        own_packed,
         masters[0],
         first_moment[0],
         second_moment[0],

time: 355 us -> 264 us (0.74)
  local copies, waits for them, and re-layouts: 67.3 us -> 11.9 us
  Pallas kernels: 283 us -> 248 us
    unnamed x55 -> x44, local copies, waits for them, and re-layouts: 57.9 us -> 11.7 us
    pallas_call x1, Pallas kernels: 85.9 us -> 51.2 us  [soap(): pl.pallas_call(functools.partial(soap_kernel, n, count), out_shape=[shape...]
    reshape x2 -> x0, local copies, waits for them, and re-layouts: 7.67 us -> none  [body(): own_packed[:, :per_dev * block].reshape(block, per_dev, block)]
where the time goes in v4:
time: 264 us; the launch traced here: 263 us
  Pallas kernels  248 us (94%)
  local copies, waits for them, and re-layouts  11.9 us (5%)
    pallas_call x1, Pallas kernels, layer(): pl.pallas_call(functools.partial(layer_kernel, heads, shift_for(length)),...  81.9 us
    pallas_call x1, Pallas kernels, settle(): pl.pallas_call(functools.partial(settle_kernel, n), out_shape=[jax.ShapeD...  52.6 us
    pallas_call x1, Pallas kernels, soap(): pl.pallas_call(functools.partial(soap_kernel, n, count), out_shape=[shape...  51.2 us
    pallas_call x1, Pallas kernels, gather_masters(): pl.pallas_call(functools.partial(gather_kernel, n, count, block, wide, no...  47.6 us
    unnamed x44, local copies, waits for them, and re-layouts  11.7 us
    pallas_call x1, Pallas kernels, disperse(): pl.pallas_call(functools.partial(disperse_kernel, rows, cols, block, piec...  11.2 us

profile of v4, /device:TPU:0, one launch (start us, length us, event | category | flops | bytes accessed | tf_op | source)
XLA Modules:
  0.0 262.5 jit_solution(1838403711513438876)
XLA Ops:
  0.7 2.0 copy.31
  2.6 0.0 copy-start.17
  2.7 47.6 %gather_masters.1 = (bf16[768,48,48]{2,1,0:T(8,128)(2,1)S(1)}, bf16[8,16,128]{2,1,0:T(8,128)(2,1)S(1)}) custom-call(f32[96,48,48]{2,1,0:T(8,128)S(1)} %bitcast.80, f32[3,128]{1,0:T(4,128)S(1)} %bitcast.94), custom_call_target="tpu_custom_call" | custom-call | tf_op jit(solution)/shard_map/gather_masters/pallas_call | solution.py:185
  50.2 0.4 convert_reduce_fusion
  50.6 0.0 copy-start.15
  50.6 3.8 %assemble.1 = (bf16[768,576]{1,0:T(8,128)(2,1)S(1)}, bf16[768,768]{1,0:T(8,128)(2,1)S(1)}, bf16[768,192]{1,0:T(8,128)(2,1)S(1)}, bf16[768,768]{1,0:T(8,128)(2,1)S(1)}) custom-call(s32[768]{0:T(1024)S(1)} %multiply_add_fusion.slot_ref, bf16[768,48,48]{2,1,0:T(8,128)(2,1)S(1)} %get-tuple-element.38.u_ref), custom_call_target="tpu_custom_call" | custom-call | tf_op jit(solution)/shard_map/assemble/pallas_call | solution.py:492
  54.5 1.0 copy-done.13
  55.5 1.0 copy-done.14
  56.5 0.2 copy.32.seg_col_ref
  56.7 81.9 %layer.1 = (bf16[768,576]{1,0:T(8,128)(2,1)S(1)}, bf16[768,768]{1,0:T(8,128)(2,1)S(1)}, bf16[768,192]{1,0:T(8,128)(2,1)S(1)}, bf16[768,768]{1,0:T(8,128)(2,1)S(1...) custom-call(bf16[1024,768]{1,0:T(8,128)(2,1)} %bitcast.81, ...), custom_call_target="tpu_custom_call" | custom-call | tf_op jit(solution)/shard_map/layer/pallas_call | solution.py:986
  138.7 0.3 select_reduce_fusion.inverse_ref
  139.0 0.0 copy-start
  139.0 11.2 %disperse.1.p_ref = bf16[8,48,4608]{2,1,0:T(8,128)(2,1)S(1)} custom-call(s32[768]{0:T(1024)S(1)} %select_reduce_fusion.inverse_ref, bf16[768,576]{1,0:T(8,128)(2,1)S(1)} %get-tuple-element.44.refs_0_, bf16[768,768]{1,0:T(8,128)(2,1)S(1)} %get-tuple-element.45.refs_1_, bf16[768,192]{1,0:T(8,128)(2,1)S(1)} %get-tuple-element.46.refs_2_, ...), custom_call_target="tpu_custom_call" | custom-call | tf_op jit(solution)/shard_map/disperse/pallas_call | solution.py:532
  150.3 1.9 copy-done.3
  152.1 1.4 copy-done.5
  153.6 0.0 copy-start.10
  153.6 0.0 copy-start.11
  153.6 52.6 %settle.1 = (f32[48,4608]{1,0:T(8,128)S(1)}, bf16[1024,768]{1,0:T(8,128)(2,1)S(1)}, f32[1024,768]{1,0:T(8,128)S(1)}, f32[4,768]{1,0:T(4,128)S(1)}) custom-call(bf16[8,48,4608]{2,1,0:T(8,128)(2,1)S(1)} %disperse.1.p_ref, bf16[1024,768]{1,0:T(8,128)(2,1)S(1)} %copy-done.4, bf16[1024,768]{1,0:T(8,128)(2,1)S(1)} %copy-done.5, f32[1024,768]{1,0:T(8,128)S(1)} %copy-done.2, ...), custom_call_target="tpu_custom_call" | custom-call | tf_op jit(solution)/shard_map/settle/pallas_call | solution.py:1255
  206.2 0.0 copy-start.6
  206.2 0.0 copy-start.18
  206.3 51.2 %soap.1 = (f32[2304,96]{1,0:T(8,128)}, f32[2304,96]{1,0:T(8,128)}, f32[2304,96]{1,0:T(8,128)}, f32[2304,96]{1,0:T(8,128)}, f32[2304,96]{1,0:T(8,128)}, /*index=5*/f32[2304,96]{1,0:T(8,128)}, f32[2304,96]{1,0:T(8,128)}) custom-call(f32[48,4608]{1,0:T(8,128)S(1)} %get-tuple-element.55.packed_ref, f32[2304,96]{1,0:T(8,128)S(1)} %bitcast.83, ...), custom_call_target="tpu_custom_call" | custom-call | tf_op jit(solution)/shard_map/soap/pallas_call | solution.py:457
  257.5 0.7 multiply_subtract_fusion
  258.2 2.7 %copy.40 = bf16[1,1024,768]{2,1,0:T(8,128)(2,1)} copy(bf16[1,1024,768]{2,1,0:T(8,128)(2,1)} %bitcast.85) | data formatting | bytes 3145728
  260.8 1.7 copy.41
  (34 shorter events, 0.1 us)
Async XLA Ops:
  0.6 2.0 copy-start.16
  2.6 47.6 %copy-start.17 = (s32[768]{0:T(1024)S(1)}, s32[768]{0:T(1024)}, u32[]{:S(2)}) copy-start(s32[768]{0:T(1024)} %param.17) | copy-start | bytes 9220
  50.6 5.9 %copy-start.15 = (s32[1,1024]{1,0:T(1,128)S(1)}, s32[1,1024]{1,0:T(1,128)}, u32[]{:S(2)}) copy-start(s32[1,1024]{1,0:T(1,128)} %seg_row_ref.1) | copy-start | bytes 12292
  54.4 1.0 copy-start.13
  55.5 1.0 copy-start.14
  139.0 11.2 %copy-start = (bf16[1,1024,768]{2,1,0:T(8,128)(2,1)S(1)}, bf16[1,1024,768]{2,1,0:T(8,128)(2,1)}, u32[]{:S(2)}) copy-start(bf16[1,1024,768]{2,1,0:T(8,128)(2,1)} %param.14) | copy-start | bytes 4718596
  139.0 11.2 %copy-start.2 = (f32[1024,768]{1,0:T(8,128)S(1)}, f32[1024,768]{1,0:T(8,128)}, u32[]{:S(2)}) copy-start(f32[1024,768]{1,0:T(8,128)} %get-tuple-element.50.resid_ref) | copy-start | bytes 9437188
  139.0 11.2 %copy-start.4 = (bf16[1024,768]{1,0:T(8,128)(2,1)S(1)}, bf16[1024,768]{1,0:T(8,128)(2,1)}, u32[]{:S(2)}) copy-start(bf16[1024,768]{1,0:T(8,128)(2,1)} %get-tuple-element.48.out_in) | copy-start | bytes 4718596
  150.2 1.9 copy-start.3
  152.1 1.4 copy-start.5
  153.5 52.6 %copy-start.1 = (f32[1,96,48,48]{1,3,2,0:T(8,128)S(1)}, f32[1,96,48,48]{1,3,2,0:T(8,128)}, u32[]{:S(2)}) copy-start(f32[1,96,48,48]{1,3,2,0:T(8,128)} %param.18) | copy-start | bytes 2654212
  153.5 52.6 %copy-start.7 = (f32[1,96,48,48]{1,3,2,0:T(8,128)S(1)}, f32[1,96,48,48]{1,3,2,0:T(8,128)}, u32[]{:S(2)}) copy-start(f32[1,96,48,48]{1,3,2,0:T(8,128)} %param.19) | copy-start | bytes 2654212
  153.5 52.6 %copy-start.8 = (f32[1,96,48,48]{1,3,2,0:T(8,128)S(1)}, f32[1,96,48,48]{1,3,2,0:T(8,128)}, u32[]{:S(2)}) copy-start(f32[1,96,48,48]{1,3,2,0:T(8,128)} %param.20) | copy-start | bytes 2654212
  153.5 52.7 %copy-start.9 = (f32[1,96,48,48]{1,3,2,0:T(8,128)S(1)}, f32[1,96,48,48]{1,3,2,0:T(8,128)}, u32[]{:S(2)}) copy-start(f32[1,96,48,48]{1,3,2,0:T(8,128)} %param.21) | copy-start | bytes 2654212
  153.6 52.7 %copy-start.10 = (f32[1,96,48,48]{1,3,2,0:T(8,128)S(1)}, f32[1,96,48,48]{1,3,2,0:T(8,128)}, u32[]{:S(2)}) copy-start(f32[1,96,48,48]{1,3,2,0:T(8,128)} %param.22) | copy-start | bytes 2654212
  153.6 52.7 %copy-start.11 = (f32[1,96,48,48]{1,3,2,0:T(8,128)S(1)}, f32[1,96,48,48]{1,3,2,0:T(8,128)}, u32[]{:S(2)}) copy-start(f32[1,96,48,48]{1,3,2,0:T(8,128)} %param.23) | copy-start | bytes 2654212
  153.6 52.7 %copy-start.12 = (f32[1,96,48,48]{1,3,2,0:T(8,128)S(1)}, f32[1,96,48,48]{1,3,2,0:T(8,128)}, u32[]{:S(2)}) copy-start(f32[1,96,48,48]{1,3,2,0:T(8,128)} %param.24) | copy-start | bytes 2654212
  206.2 51.3 %copy-start.6 = (bf16[1024,768]{1,0:T(8,128)(2,1)}, bf16[1024,768]{1,0:T(8,128)(2,1)S(1)}, u32[]{:S(2)}) copy-start(bf16[1024,768]{1,0:T(8,128)(2,1)S(1)} %get-tuple-element.53) | copy-start | bytes 4718596
  206.2 51.3 %copy-start.18 = (f32[384]{0:T(512)S(1)}, f32[384]{0:T(512)}, u32[]{:S(2)}) copy-start(f32[384]{0:T(512)} %param.27) | copy-start | bytes 4612
  206.3 51.3 %copy-start.19 = (f32[384]{0:T(512)S(1)}, f32[384]{0:T(512)}, u32[]{:S(2)}) copy-start(f32[384]{0:T(512)} %param.26) | copy-start | bytes 4612

commit v5 on v4

--- a/solution.py
+++ b/solution.py
@@ -12,7 +12,7 @@
 STEP = 10
 F32 = jnp.float32
 BF16 = jnp.bfloat16
-LAYER_LIMIT = 48 * 2**20
+LAYER_LIMIT = 33 * 2**20
 
 norm_eps = 1e-05
 beta_one = 0.9
@@ -262,6 +262,8 @@
     n,
     count,
     packed_ref,
+    y_ref,
+    dx_ref,
     m_ref,
     f_ref,
     s_ref,
@@ -276,6 +278,8 @@
     nr_out,
     bl_out,
     br_out,
+    y_out,
+    dx_out,
     nf_ref,
     ns_ref,
     nm_ref,
@@ -327,6 +331,8 @@
     def send(place, src, dst):
         return pltpu.make_async_copy(src, dst, sems.at[place])
 
+    send(7, y_ref, y_out).start()
+    send(8, dx_ref, dx_out).start()
     for c in range(count):
         u_scr[c] = packed_ref[:, c * n : (c + 1) * n]
 
@@ -443,30 +449,30 @@
     lane_prod(n, count, at(ql_ref), tile(d_ref), store(h_ref))
     lane_prod(n, count, at(h_ref), tile(qt_ref), put_master)
     send(2, nm_ref, nm_out).start()
-    sources = (nf_ref, ns_ref, nm_ref, nl_ref, nr_ref, left_basis, right_basis)
-    targets = (nf_out, ns_out, nm_out, nl_out, nr_out, bl_out, br_out)
+    sources = (nf_ref, ns_ref, nm_ref, nl_ref, nr_ref, left_basis, right_basis, y_ref, dx_ref)
+    targets = (nf_out, ns_out, nm_out, nl_out, nr_out, bl_out, br_out, y_out, dx_out)
     for place, (src, dst) in enumerate(zip(sources, targets)):
         send(place, src, dst).wait()
 
 
-def soap(packed, *state):
+def soap(packed, output, input_grad, *state):
     count, n = state[0].shape[0], state[0].shape[-1]
     flat = [item.transpose(1, 2, 0).reshape(n * n, count) for item in state]
     shape = jax.ShapeDtypeStruct((n * n, count), F32)
     room = pltpu.VMEM((n * n, count), F32)
     outs = pl.pallas_call(
         functools.partial(soap_kernel, n, count),
-        out_shape=[shape] * 7,
-        in_specs=[VM] * 8,
-        out_specs=[pl.BlockSpec(memory_space=pl.ANY)] * 7,
+        out_shape=[shape] * 7 + [jax.ShapeDtypeStruct(item.shape, item.dtype) for item in (output, input_grad)],
+        in_specs=[VM] * 10,
+        out_specs=[pl.BlockSpec(memory_space=pl.ANY)] * 9,
         scratch_shapes=[room] * 5
         + [pltpu.VMEM((2 * n * n, count), F32), pltpu.VMEM((count, n, n), F32)]
         + [room] * 5
-        + [pltpu.SemaphoreType.DMA((7,))],
+        + [pltpu.SemaphoreType.DMA((9,))],
         compiler_params=pltpu.CompilerParams(vmem_limit_bytes=24 * MIB),
         name="soap",
-    )(packed, *flat)
-    return [item.reshape(n, n, count).transpose(2, 0, 1) for item in outs]
+    )(packed, output, input_grad, *flat)
+    return [item.reshape(n, n, count).transpose(2, 0, 1) for item in outs[:7]] + list(outs[7:])
 
 
 def assemble_kernel(rows, cols, block, cuts, slot_ref, u_ref, *w_refs):
@@ -514,9 +520,12 @@
 
     lax.fori_loop(0, rows, cut, 0)
 
+    some = math.gcd(count, 8)
+
     def lay(d, _):
-        for k in range(count):
-            p_ref[d, :, k * block : (k + 1) * block] = u_scr[inverse_ref[d * count + k]]
+        for k in range(0, count, some):
+            strip = [u_scr[inverse_ref[d * count + k + e]] for e in range(some)]
+            p_ref[d, :, k * block : (k + some) * block] = jnp.concatenate(strip, axis=1)
         if wide > count * block:
             p_ref[d, :, count * block : wide] = jnp.zeros((block, wide - count * block), BF16)
         return 0
@@ -558,7 +567,7 @@
 class Total:
     def __init__(self, dp, t, x, near, mine, far, near_mine, near_far, sems):
         up, core = t // 2, lax.rem(t, 2)
-        self.core = core
+        self.up, self.core = up, core
         self.beside = (dp, up * 2 + 1 - core)
         self.over = (dp, (1 - up) * 2 + core)
         self.x, self.near, self.mine, self.far = x, near, mine, far
@@ -613,6 +622,61 @@
     def close(self, b):
         for kind in range(4):
             self.copy(kind, b).wait_send()
+
+
+class Packs:
+    def __init__(self, total, own, beside, over, far, sems):
+        self.beside, self.over = total.beside, total.over
+        self.up, self.core = total.up, total.core
+        self.own, self.from_beside, self.from_over, self.from_far, self.sems = own, beside, over, far, sems
+
+    def copy(self, kind, b):
+        src, dst, where = (
+            (self.own, self.from_beside, self.beside),
+            (self.own, self.from_over, self.over),
+            (self.from_over, self.from_far, self.beside),
+        )[kind]
+        return remote(src.at[b], dst.at[b], self.sems.at[2 * kind, b], self.sems.at[2 * kind + 1, b], where)
+
+    def send(self, b):
+        self.copy(1, b).start()
+        self.copy(0, b).start()
+
+    def relay(self, b):
+        self.copy(1, b).wait_recv()
+        self.copy(2, b).start()
+
+    def arrived(self, b):
+        self.copy(0, b).wait_recv()
+        self.copy(2, b).wait_recv()
+
+    def close(self, b):
+        for kind in range(3):
+            self.copy(kind, b).wait_send()
+
+    def lay(self, b, dst, rows):
+        tall = rows.size
+        pairs = ((self.up, self.own, self.from_beside), (1 - self.up, self.from_over, self.from_far))
+        for up, same, other in pairs:
+            for core, ref in ((self.core, same), (1 - self.core, other)):
+                dst[rows, pl.ds(pl.multiple_of((up * 2 + core) * 128, 128), 128)] = ref[b, :tall]
+            first, second = same[b, tall:], other[b, tall:]
+            low = self.core == 0
+            zero = jnp.where(low, first.astype(F32), second.astype(F32)).astype(BF16)
+            one = jnp.where(low, second.astype(F32), first.astype(F32)).astype(BF16)
+            tail = jnp.concatenate(
+                [
+                    jnp.concatenate([zero[:, :HD], one[:, :HD]], axis=1),
+                    jnp.concatenate([zero[:, HD:], one[:, HD:]], axis=1),
+                ],
+                axis=0,
+            )
+            dst[rows, pl.ds(pl.multiple_of(512 + up * 128, 128), 128)] = tail
+
+    def pack(self, b, value):
+        tall = value.shape[0]
+        self.own[b, :tall] = value[:, :128]
+        self.own[b, tall:] = jnp.concatenate([value[: tall // 2, 128:], value[tall // 2 :, 128:]], axis=1)
 
 
 def layer_kernel(
@@ -632,7 +696,8 @@
     go_ref,
     g2_ref,
     out_ref,
-    da_ref,
+    dproj_ref,
+    wf_out,
     resid_ref,
     dres_ref,
     ng_ref,
@@ -640,22 +705,32 @@
     wf_ref,
     qkv_ref,
     pen_ref,
+    sig_ref,
     lse_ref,
     o_ref,
     cn_ref,
     s_ref,
     du_ref,
     dhb_ref,
-    dproj_ref,
     dkv_ref,
     carry_ref,
-    x1_ref,
-    near1,
-    mine1,
-    far1,
-    near_mine1,
-    near_far1,
-    sem1,
+    raw_scr,
+    back_scr,
+    probs_scr,
+    draw_scr,
+    pick_scr,
+    o_own,
+    o_beside,
+    o_over,
+    o_far,
+    o_sem,
+    o_all,
+    wo_own,
+    wo_beside,
+    wo_over,
+    wo_far,
+    wo_sem,
+    wo_all,
     x3_ref,
     near3,
     mine3,
@@ -676,8 +751,9 @@
     blocks = length // BLK
     span = min(length // 2 + BLK, length)
     attn = heads * HD
-    one = Total(dp, t, x1_ref, near1, mine1, far1, near_mine1, near_far1, sem1)
     three = Total(dp, t, x3_ref, near3, mine3, far3, near_mine3, near_far3, sem3)
+    one = Packs(three, o_own, o_beside, o_over, o_far, o_sem)
+    outer = Packs(three, wo_own, wo_beside, wo_over, wo_far, wo_sem)
     greet([beside, over])
 
     def give(where, i):
@@ -689,6 +765,9 @@
         wf_ref[:, HD:] = wp_ref[:, attn : attn + HD]
         give(over, 0).start()
         give(beside, 1).start()
+
+    outer.pack(0, wo_ref[...])
+    outer.send(0)
 
     def rows_of(b):
         return pl.ds(pl.multiple_of(b * BLK, BLK), BLK)
@@ -731,68 +810,94 @@
         return 0
 
     lax.fori_loop(0, length // wide, project_first, 0)
-
-    row_in = lax.broadcasted_iota(jnp.int32, (BLK, 1), 0)
-    col_in = lax.broadcasted_iota(jnp.int32, (1, span), 1)
-    square_row = lax.broadcasted_iota(jnp.int32, (BLK, BLK), 0)
-    square_col = lax.broadcasted_iota(jnp.int32, (BLK, BLK), 1)
+    wf_out[...] = wf_ref[...]
+
+    square_row = lax.broadcasted_iota(jnp.int32, (BLK, 2 * BLK), 0)
+    square_col = lax.rem(lax.broadcasted_iota(jnp.int32, (BLK, 2 * BLK), 1), BLK)
     earlier = (square_col < square_row).astype(F32).astype(BF16)
     later = (square_col > square_row).astype(F32).astype(BF16)
-
-    def window(b):
-        start = pl.multiple_of(jnp.maximum(b * BLK + BLK - span, 0), BLK)
-        return start, pl.ds(start, span)
-
-    def masks(b):
-        start, keys = window(b)
-        same = seg_col_ref[rows_of(b)] == seg_row_ref[:, keys]
-        behind = (row_in + (b * BLK - start)) - col_in
-        return same & (behind >= 0), same & (behind > 0)
-
-    def two_part(matrix, values):
+    few = 32
+
+    def every_block(one, backward):
+        low = span // BLK - 1
+
+        def early():
+            for b in range(low)[:: -1 if backward else 1]:
+                one(b, 0, (b + 1) * BLK)
+
+        def rest():
+            def step(i, _):
+                b = blocks - 1 - i if backward else low + i
+                one(b, pl.multiple_of((b - low) * BLK, BLK), span)
+                return 0
+
+            lax.fori_loop(0, blocks - low, step, 0)
+
+        for part in (rest, early) if backward else (early, rest):
+            part()
+
+    def by_rows(b, one):
+        def step(i, _):
+            base = pl.multiple_of(i * few, few)
+            one(pl.ds(base, few), pl.ds(pl.multiple_of(b * BLK + base, few), few), base)
+            return 0
+
+        lax.fori_loop(0, BLK // few, step, 0, unroll=True)
+
+    def two_part(values, part, keys):
         high = values.astype(BF16)
-        low = (values - high.astype(F32)).astype(BF16)
-        return dot(matrix, high, NN) + dot(matrix, low, NN)
+        pick_scr[part, :keys] = high
+        pick_scr[pl.ds(pl.multiple_of(part.start + BLK, few), few), :keys] = (
+            values - high.astype(F32)
+        ).astype(BF16)
+
+    def behind(base, keys):
+        row = lax.broadcasted_iota(jnp.int32, (few, keys), 0) + (base + keys - BLK)
+        return row - lax.broadcasted_iota(jnp.int32, (few, keys), 1)
 
     carry_ref[...] = jnp.zeros_like(carry_ref)
 
-    def attend(b, _):
-        rows = rows_of(b)
-        _, keys = window(b)
-        allowed, strict = masks(b)
-        first = dot(qkv_ref[3 * heads, rows], qkv_ref[3 * heads + 1, keys], NT) - shift
-        soft = jnp.maximum(first, 0.0) + jnp.log1p(jnp.exp(-jnp.abs(first)))
-        picks = jnp.where(strict, soft, 0.0)
-        before = carry_ref[0:1, keys]
-        penalty = (two_part(earlier, picks) + before).astype(BF16)
-        carry_ref[0:1, keys] = before + jnp.sum(picks, axis=0, keepdims=True)
-        pen_ref[rows] = penalty
-        penalty = penalty.astype(F32)
-        mixed = []
+    def attend(b, start, keys):
+        rows, window = rows_of(b), pl.ds(start, keys)
+        raw_scr[heads, :, :keys] = dot(qkv_ref[3 * heads, rows], qkv_ref[3 * heads + 1, window], NT)
         for h in range(heads):
-            raw = dot(qkv_ref[h, rows], qkv_ref[heads + h, keys], NT)
-            logits = jnp.where(allowed, raw - penalty, -1e30)
-            top = jnp.max(logits, axis=-1, keepdims=True)
-            weights = jnp.exp(logits - top)
-            total = jnp.sum(weights, axis=-1, keepdims=True)
-            lse_ref[h, rows] = top + jnp.log(total)
-            probs = (weights * (1.0 / total)).astype(BF16)
-            mixed.append(dot(probs, qkv_ref[2 * heads + h, keys], NN))
+            raw_scr[h, :, :keys] = dot(qkv_ref[h, rows], qkv_ref[heads + h, window], NT)
+        seg_row = seg_row_ref[:, window]
+
+        def pick(part, whole, base):
+            first = raw_scr[heads, part, :keys] - shift
+            small = jnp.exp(-jnp.abs(first))
+            soft = jnp.maximum(first, 0.0) + jnp.log(1.0 + small)
+            strict = (seg_col_ref[whole] == seg_row) & (behind(base, keys) > 0)
+            two_part(jnp.where(strict, soft, 0.0), part, keys)
+            share = jnp.where(first >= 0.0, 1.0, small) / (1.0 + small)
+            sig_ref[whole, :keys] = jnp.where(strict, share, 0.0).astype(BF16)
+
+        by_rows(b, pick)
+        raw_scr[heads, :, :keys] = dot(earlier, pick_scr[:, :keys], NN)
+        before = carry_ref[0:1, window]
+        last = [pick_scr[end - few : end, :keys].astype(F32)[few - 1 :] for end in (BLK, 2 * BLK)]
+        carry_ref[0:1, window] = before + raw_scr[heads, BLK - 1 : BLK, :keys] + (last[0] + last[1])
+
+        def soften(part, whole, base):
+            allowed = (seg_col_ref[whole] == seg_row) & (behind(base, keys) >= 0)
+            penalty = jnp.where(allowed, raw_scr[heads, part, :keys] + before, 1e30).astype(BF16)
+            pen_ref[whole, :keys] = penalty
+            penalty = penalty.astype(F32)
+            for h in range(heads):
+                logits = raw_scr[h, part, :keys] - penalty
+                top = jnp.max(logits, axis=-1, keepdims=True)
+                weights = jnp.exp(logits - top)
+                total = jnp.sum(weights, axis=-1, keepdims=True)
+                lse_ref[whole, h : h + 1] = top + jnp.log(total)
+                probs_scr[h, part, :keys] = (weights * (1.0 / total)).astype(BF16)
+
+        by_rows(b, soften)
+        mixed = [dot(probs_scr[h, :, :keys], qkv_ref[2 * heads + h, window], NN) for h in range(heads)]
         o = jnp.concatenate(mixed, axis=1).astype(BF16)
         o_ref[rows] = o
-        x1_ref[rows] = dot(o, wo_ref[...], NT).astype(BF16)
-        one.enter(b)
-
-        @pl.when(b > 0)
-        def _():
-            one.add(b - 1)
-            one.cross(b - 1)
-
-        return 0
-
-    lax.fori_loop(0, blocks, attend, 0)
-    one.add(blocks - 1)
-    one.cross(blocks - 1)
+        one.pack(b, o)
+        one.send(b)
 
     def act_back(i, _):
         rows = wide_rows(i)
@@ -800,25 +905,13 @@
         return 0
 
     lax.fori_loop(0, length // wide, act_back, 0)
-
-    def mlp(b, _):
-        @pl.when(b == 0)
-        def _():
-            one.relay(0)
-
-        @pl.when(b < blocks - 1)
-        def _():
-            one.relay(b + 1)
-
-        @pl.when(b == blocks - 2)
-        def _():
-            for early in (0, 1):
-                three.add(early)
-                three.cross(early)
-
+    outer.relay(0)
+
+    def mlp(b):
         one.arrived(b)
         rows = rows_of(b)
-        resid = x_ref[rows].astype(F32) + one.sums(b)
+        one.lay(b, o_all, pl.ds(0, BLK))
+        resid = x_ref[rows].astype(F32) + dot(o_all[...], wo_all[...], NT)
         resid_ref[rows] = resid
         plain, _ = plain_norm(resid)
         cn = (plain * gain_two + bias_two).astype(BF16)
@@ -834,36 +927,79 @@
         du_ref[rows] = du
         x3_ref[rows] = dot(du, w1_ref[...], NT).astype(BF16)
         three.enter(b)
+
+    lag, turned_from = 3, blocks - 3
+
+    def mlp_and_send(b):
+        mlp(b)
+
+        def before():
+            three.add(b - 1)
+            three.cross(b - 1)
+
+        if isinstance(b, int):
+            if 0 < b <= turned_from:
+                before()
+        else:
+            pl.when((b > 0) & (b <= turned_from))(before)
+
+    def forward(b, start, keys):
+        attend(b, start, keys)
+        if isinstance(b, int):
+            if b == lag - 1:
+                outer.arrived(0)
+                outer.lay(0, wo_all, pl.ds(0, width))
+            if b >= lag - 1:
+                one.relay(b - lag + 1)
+            if b >= lag:
+                mlp_and_send(b - lag)
+        else:
+            one.relay(b - lag + 1)
+            mlp_and_send(b - lag)
+
+    every_block(forward, False)
+
+    def forward_last(i, _):
+        b = blocks - lag + i
+
+        @pl.when(i < lag - 1)
+        def _():
+            one.relay(b + 1)
+
+        mlp_and_send(b)
         return 0
 
-    lax.fori_loop(0, blocks, mlp, 0)
-
-    def cross_back(i, _):
-        three.add(blocks - 1 - i)
-        three.cross(blocks - 1 - i)
-        return 0
-
-    lax.fori_loop(0, blocks - 2, cross_back, 0)
+    lax.fori_loop(0, lag, forward_last, 0)
+    for b in reversed(range(turned_from, blocks)):
+        three.add(b)
+        three.cross(b)
     g2_ref[...] = dot(dy_ref[...], s_ref[...], TN).astype(BF16)
     g1_ref[...] = dot(cn_ref[...], du_ref[...], TN).astype(BF16)
 
-    for early in (0, 1):
+    def mlp_out(i, _):
+        rows = wide_rows(i)
+        out_ref[rows] = dot(s_ref[rows], w2_ref[...], NT).astype(BF16)
+        return 0
+
+    lax.fori_loop(0, length // wide, mlp_out, 0)
+
+    for early in range(turned_from):
         three.relay(early)
     three.relay(blocks - 1)
     ng_ref[...] = jnp.zeros_like(ng_ref)
     carry_ref[...] = jnp.zeros_like(carry_ref)
     dkv_ref[...] = jnp.zeros_like(dkv_ref)
 
-    def back(i, _):
-        b = blocks - 1 - i
-
-        @pl.when(b > 2)
-        def _():
+    def back(b, start, keys):
+        def ahead():
             three.relay(b - 1)
 
+        if not isinstance(b, int):
+            pl.when(b > turned_from)(ahead)
+        elif b > turned_from:
+            ahead()
         three.arrived(b)
-        rows = rows_of(b)
-        _, keys = window(b)
+        rows, window = rows_of(b), pl.ds(start, keys)
         plain, inverse_std = plain_norm(resid_ref[rows])
         d_two = three.sums(b)
         ng_ref[0:1, :] += jnp.sum(d_two * plain, axis=0, keepdims=True)
@@ -873,40 +1009,49 @@
         dhb = dres.astype(BF16)
         dhb_ref[rows] = dhb
         do = dot(dhb, wo_ref[...], NN).astype(BF16)
-        allowed, strict = masks(b)
-        penalty = pen_ref[rows].astype(F32)
-        total = None
+        do = [do[:, h * HD : (h + 1) * HD] for h in range(heads)]
+        for h in range(heads):
+            raw_scr[h, :, :keys] = dot(qkv_ref[h, rows], qkv_ref[heads + h, window], NT)
+            back_scr[h, :, :keys] = dot(do[h], qkv_ref[2 * heads + h, window], NT)
+
+        def harden(part, whole, base):
+            penalty = pen_ref[whole, :keys].astype(F32)
+            total = None
+            for h in range(heads):
+                probs = jnp.exp(raw_scr[h, part, :keys] - penalty - lse_ref[whole, h : h + 1])
+                dprobs = back_scr[h, part, :keys]
+                inner = jnp.sum(dprobs * probs, axis=-1, keepdims=True)
+                dlogits = probs * (dprobs - inner)
+                probs_scr[h, part, :keys] = probs.astype(BF16)
+                draw_scr[h, part, :keys] = dlogits.astype(BF16)
+                total = dlogits if total is None else total + dlogits
+            two_part(total, part, keys)
+
+        by_rows(b, harden)
+        raw_scr[heads, :, :keys] = dot(later, pick_scr[:, :keys], NN)
+        after = carry_ref[0:1, window]
+        top = [pick_scr[start_ : start_ + few, :keys].astype(F32)[:1] for start_ in (0, BLK)]
+        carry_ref[0:1, window] = after + raw_scr[heads, 0:1, :keys] + (top[0] + top[1])
+
+        def select(part, whole, base):
+            suffix = raw_scr[heads, part, :keys] + after
+            draw_scr[heads, part, :keys] = (sig_ref[whole, :keys].astype(F32) * -suffix).astype(BF16)
+
+        by_rows(b, select)
         dq = []
         for h in range(heads):
-            q, k, v = qkv_ref[h, rows], qkv_ref[heads + h, keys], qkv_ref[2 * heads + h, keys]
-            do_h = do[:, h * HD : (h + 1) * HD]
-            logits = jnp.where(allowed, dot(q, k, NT) - penalty, -1e30)
-            probs = jnp.exp(logits - lse_ref[h, rows])
-            dprobs = dot(do_h, v, NT)
-            inner = jnp.sum(dprobs * probs, axis=-1, keepdims=True)
-            dlogits = probs * (dprobs - inner)
-            total = dlogits if total is None else total + dlogits
-            draw = dlogits.astype(BF16)
-            dq.append(dot(draw, k, NN) * 0.125)
-            dkv_ref[h * HD : (h + 1) * HD, keys] += dot(q, draw, TN)
-            dkv_ref[attn + h * HD : attn + (h + 1) * HD, keys] += dot(do_h, probs.astype(BF16), TN)
-        q, k = qkv_ref[3 * heads, rows], qkv_ref[3 * heads + 1, keys]
-        first = dot(q, k, NT) - shift
-        picked = 1.0 / (1.0 + jnp.exp(-first))
-        after = carry_ref[0:1, keys]
-        suffix = two_part(later, total) + after
-        carry_ref[0:1, keys] = after + jnp.sum(total, axis=0, keepdims=True)
-        draw = jnp.where(strict, -picked * suffix, 0.0).astype(BF16)
-        dq.append(dot(draw, k, NN) * 0.125)
-        dkv_ref[2 * attn : 2 * attn + HD, keys] += dot(q, draw, TN)
+            draw = draw_scr[h, :, :keys]
+            dq.append(dot(draw, qkv_ref[heads + h, window], NN) * 0.125)
+            dkv_ref[h * HD : (h + 1) * HD, window] += dot(qkv_ref[h, rows], draw, TN)
+            dkv_ref[attn + h * HD : attn + (h + 1) * HD, window] += dot(do[h], probs_scr[h, :, :keys], TN)
+        draw = draw_scr[heads, :, :keys]
+        dq.append(dot(draw, qkv_ref[3 * heads + 1, window], NN) * 0.125)
+        dkv_ref[2 * attn : 2 * attn + HD, window] += dot(qkv_ref[3 * heads, rows], draw, TN)
         dproj_ref[rows, :attn] = jnp.concatenate(dq[:heads], axis=1).astype(BF16)
         dproj_ref[rows, 3 * attn : 3 * attn + HD] = dq[heads].astype(BF16)
-        return 0
-
-    lax.fori_loop(0, blocks, back, 0)
-    turned = dkv_ref[...].T.astype(BF16)
-    dproj_ref[:, attn : 3 * attn] = turned[:, : 2 * attn]
-    dproj_ref[:, 3 * attn + HD : 3 * attn + 2 * HD] = turned[:, 2 * attn :]
+
+    every_block(back, True)
+    dproj_ref[:, 3 * attn + HD : 3 * attn + 2 * HD] = dkv_ref[2 * attn :].T.astype(BF16)
 
     def collect(src, dst, where, i):
         return remote(src, dst, collect_sem.at[i], collect_sem.at[i + 2], where)
@@ -926,18 +1071,10 @@
     def _():
         collect(gf_ref, gf_far, over, 1).start()
 
+    dproj_ref[:, attn : 3 * attn] = dkv_ref[: 2 * attn].T.astype(BF16)
     go_ref[...] = dot(dhb_ref[...], o_ref[...], TN).astype(BF16)
     grad = dot(a_ref[...], dproj_ref[:, : 3 * attn], TN)
     gp_ref[...] = grad.astype(BF16)
-
-    def finish(i, _):
-        rows = wide_rows(i)
-        out_ref[rows] = dot(s_ref[rows], w2_ref[...], NT).astype(BF16)
-        da = dot(dproj_ref[rows, : 3 * attn], wp_ref[...], NT)
-        da_ref[rows] = (da + dot(dproj_ref[rows, 3 * attn :], wf_ref[...], NT)).astype(BF16)
-        return 0
-
-    lax.fori_loop(0, length // wide, finish, 0)
 
     @pl.when(t == 0)
     def _():
@@ -965,6 +1102,7 @@
         return 0
 
     lax.fori_loop(0, blocks, close, 0)
+    outer.close(0)
 
 
 def layer(inputs, segments, cotangent, wp, w1, wo, w2, norms):
@@ -991,29 +1129,38 @@
             out(wo.shape, BF16),
             out(w2.shape, BF16),
             out((length, width), BF16),
-            out((length, width), BF16),
+            out((length, 3 * attn + 2 * HD), BF16),
+            out((width, 2 * HD), BF16),
             out((length, width), F32),
             out((length, width), F32),
             out((2, width), F32),
         ],
         in_specs=[VM] * 9,
-        out_specs=[VM] * 9,
+        out_specs=[VM] * 10,
         scratch_shapes=[
             low(length, width),
             low(width, 2 * HD),
             low(3 * heads + 2, length, HD),
             low(length, span),
-            pltpu.VMEM((heads, length, 1), F32),
+            low(length, span),
+            pltpu.VMEM((length, 8), F32),
             low(length, attn),
             low(length, width),
             low(length, hidden),
             low(length, hidden),
             low(length, width),
-            low(length, 3 * attn + 2 * HD),
             pltpu.VMEM((2 * attn + HD, length), F32),
             pltpu.VMEM((8, length), F32),
+            pltpu.VMEM((heads + 1, BLK, span), F32),
+            pltpu.VMEM((heads, BLK, span), F32),
+            low(heads, BLK, span),
+            low(heads + 1, BLK, span),
+            low(2 * BLK, span),
         ]
-        + total
+        + [low(blocks, attn, BLK)] * 4
+        + [pltpu.SemaphoreType.DMA((6, blocks)), low(BLK, width)]
+        + [low(1, width + width // 2, BLK)] * 4
+        + [pltpu.SemaphoreType.DMA((6, 1)), low(width, width)]
         + total
         + [low(width, 2 * HD)] * 3
         + [pltpu.SemaphoreType.DMA((3,)), pltpu.SemaphoreType.DMA((4,))],
@@ -1038,7 +1185,9 @@
     n,
     p_ref,
     out_in,
-    da_in,
+    dproj_ref,
+    wp_ref,
+    wf_ref,
     resid_ref,
     dres_ref,
     x_ref,
@@ -1072,12 +1221,13 @@
     norm_held,
     norm_send,
     norm_recv,
+    da_scr,
 ):
     m = n // 2
     dp, t = lax.axis_index("dp"), lax.axis_index("tensor")
     place, side = dp // 2, lax.rem(dp, 2)
     pair = (place * 2 + 1 - side, t)
-    four = Total(dp, t, da_in, near4, mine4, far4, near_mine4, near_far4, sem4)
+    four = Total(dp, t, da_scr, near4, mine4, far4, near_mine4, near_far4, sem4)
     two = Total(dp, t, out_in, near2, mine2, far2, near_mine2, near_far2, sem2)
     blocks = four.blocks
     peers = [lax.rem(dp + hop, n) for hop in range(1, n)]
@@ -1151,7 +1301,11 @@
 
     for hop in reversed(range(m)):
         both(hop, lambda q, right: across(q).start())
+    cut = wp_ref.shape[1]
     for b in range(blocks):
+        rows = pl.ds(b * four.size, four.size)
+        da = dot(dproj_ref[rows, :cut], wp_ref[...], NT)
+        da_scr[rows] = (da + dot(dproj_ref[rows, cut:], wf_ref[...], NT)).astype(BF16)
         four.enter(b)
     for b in range(blocks):
         two.enter(b)
@@ -1241,7 +1395,7 @@
         two.close(b)
 
 
-def settle(packed, out_part, da_part, resid, dres, inputs, norms, ng):
+def settle(packed, out_part, dproj, wp, wf, resid, dres, inputs, norms, ng):
     n, block, wide = packed.shape
     m = n // 2
     length, width = inputs.shape
@@ -1260,18 +1414,19 @@
             jax.ShapeDtypeStruct((length, width), F32),
             jax.ShapeDtypeStruct((4, width), F32),
         ],
-        in_specs=[VM] * 8,
+        in_specs=[VM] * 10,
         out_specs=[VM] * 4,
         scratch_shapes=[low(m, block, wide)] * 3
         + [pltpu.SemaphoreType.DMA((m,))] * 6
         + total
         + total
-        + [pltpu.VMEM((n, 4, width), F32), pltpu.SemaphoreType.DMA((n,)), pltpu.SemaphoreType.DMA((n,))],
+        + [pltpu.VMEM((n, 4, width), F32), pltpu.SemaphoreType.DMA((n,)), pltpu.SemaphoreType.DMA((n,))]
+        + [low(length, width)],
         compiler_params=pltpu.CompilerParams(
             collective_id=2, has_side_effects=True, vmem_limit_bytes=24 * MIB
         ),
         name="settle",
-    )(packed, out_part, da_part, resid, dres, inputs, norms, ng)
+    )(packed, out_part, dproj, wp, wf, resid, dres, inputs, norms, ng)
 
 
 def norm_update(grad, master, first, second):
@@ -1311,19 +1466,21 @@
     slots, inverse = block_slots(owner, per_dev)
     pieces = assemble(slots, blocks, width // block, parts)
     norms = shared_norms.astype(F32).reshape(4, width)
-    *grads, out_part, da_part, resid, dres, norm_grads = layer(
+    *grads, out_part, dproj, w_first, resid, dres, norm_grads = layer(
         inputs[0], segments[0], cotangent[0], *pieces, norms
     )
     packed = disperse(inverse, grads, n_dp, block, parts)
     own_packed, output, input_grad, norm_grads = settle(
-        packed, out_part, da_part, resid, dres, inputs[0], norms, norm_grads
+        packed, out_part, dproj, pieces[0], w_first, resid, dres, inputs[0], norms, norm_grads
     )
     norm_per = norm_master.shape[0]
     own_norm_grads = lax.dynamic_slice_in_dim(
         norm_grads.reshape(-1), lax.axis_index("dp") * norm_per, norm_per
     )
-    new_first, new_second, new_master, new_left, new_right, left_next, right_next = soap(
+    *updated, output, input_grad = soap(
         own_packed,
+        output,
+        input_grad,
         masters[0],
         first_moment[0],
         second_moment[0],
@@ -1338,13 +1495,7 @@
     return (
         output[None],
         input_grad[None],
-        new_first[None],
-        new_second[None],
-        new_master[None],
-        new_left[None],
-        new_right[None],
-        left_next[None],
-        right_next[None],
+        *[item[None] for item in updated],
         norm_first_new,
         norm_second_new,
         norm_new,

time: 264 us -> 244 us (0.924)
  Pallas kernels: 248 us -> 230 us
  local copies, waits for them, and re-layouts: 11.9 us -> 8.28 us
    pallas_call x1, Pallas kernels: 81.9 us -> 65.9 us  [layer(): pl.pallas_call(functools.partial(layer_kernel, heads, shift_for(length)),...]
    unnamed x44 -> x38, local copies, waits for them, and re-layouts: 11.7 us -> 8.03 us
where the time goes in v5:
time: 244 us; the launch traced here: 241 us
  Pallas kernels  230 us (94%)
  local copies, waits for them, and re-layouts  8.28 us (3%)
    pallas_call x1, Pallas kernels, layer(): pl.pallas_call(functools.partial(layer_kernel, heads, shift_for(length)),...  65.9 us
    pallas_call x1, Pallas kernels, settle(): pl.pallas_call(functools.partial(settle_kernel, n), out_shape=[jax.ShapeD...  52.4 us
    pallas_call x1, Pallas kernels, soap(): pl.pallas_call(functools.partial(soap_kernel, n, count), out_shape=[shape...  51.3 us
    pallas_call x1, Pallas kernels, gather_masters(): pl.pallas_call(functools.partial(gather_kernel, n, count, block, wide, no...  47.6 us
    pallas_call x1, Pallas kernels, disperse(): pl.pallas_call(functools.partial(disperse_kernel, rows, cols, block, piec...  9.11 us
    unnamed x38, local copies, waits for them, and re-layouts  8.03 us

profile of v5, /device:TPU:0, one launch (start us, length us, event | category | flops | bytes accessed | tf_op | source)
XLA Modules:
  0.0 241.0 jit_solution(1295453090795935424)
XLA Ops:
  0.7 2.0 copy.31
  2.6 0.0 copy-start.15
  2.7 47.6 %gather_masters.1 = (bf16[768,48,48]{2,1,0:T(8,128)(2,1)S(1)}, bf16[8,16,128]{2,1,0:T(8,128)(2,1)S(1)}) custom-call(f32[96,48,48]{2,1,0:T(8,128)S(1)} %bitcast.80, f32[3,128]{1,0:T(4,128)S(1)} %bitcast.93), custom_call_target="tpu_custom_call" | custom-call | tf_op jit(solution)/shard_map/gather_masters/pallas_call | solution.py:185
  50.2 0.4 convert_reduce_fusion
  50.6 0.0 copy-start.13
  50.6 3.8 %assemble.1 = (bf16[768,576]{1,0:T(8,128)(2,1)S(1)}, bf16[768,768]{1,0:T(8,128)(2,1)S(1)}, bf16[768,192]{1,0:T(8,128)(2,1)S(1)}, bf16[768,768]{1,0:T(8,128)(2,1)S(1)}) custom-call(s32[768]{0:T(1024)S(1)} %multiply_add_fusion.slot_ref, bf16[768,48,48]{2,1,0:T(8,128)(2,1)S(1)} %get-tuple-element.41.u_ref), custom_call_target="tpu_custom_call" | custom-call | tf_op jit(solution)/shard_map/assemble/pallas_call | solution.py:498
  54.5 0.0 copy-start.3
  54.5 1.0 copy-done.3
  55.5 1.0 copy-done.5
  56.5 0.2 copy.32.seg_col_ref
  56.8 0.0 copy-start.2
  56.8 1.4 copy-done.2
  58.2 1.3 copy-done.4
  59.5 1.3 copy-done.6
  60.7 65.9 %layer.1 = (bf16[768,576]{1,0:T(8,128)(2,1)S(1)}, bf16[768,768]{1,0:T(8,128)(2,1)S(1)}, bf16[768,192]{1,0:T(8,128)(2,1)S(1)}, bf16[768,768]{1,0:T(8,128)(2,1)S(1...) custom-call(bf16[1024,768]{1,0:T(8,128)(2,1)S(1)} %bitcast.81, ...), custom_call_target="tpu_custom_call" | custom-call | tf_op jit(solution)/shard_map/layer/pallas_call | solution.py:1124
  126.7 0.3 select_reduce_fusion.inverse_ref
  127.0 9.1 %disperse.1.p_ref = bf16[8,48,4608]{2,1,0:T(8,128)(2,1)S(1)} custom-call(s32[768]{0:T(1024)S(1)} %select_reduce_fusion.inverse_ref, bf16[768,576]{1,0:T(8,128)(2,1)S(1)} %get-tuple-element.47.refs_0_, bf16[768,768]{1,0:T(8,128)(2,1)S(1)} %get-tuple-element.48.refs_1_, bf16[768,192]{1,0:T(8,128)(2,1)S(1)} %get-tuple-element.49.refs_2_, ...), custom_call_target="tpu_custom_call" | custom-call | tf_op jit(solution)/shard_map/disperse/pallas_call | solution.py:541
  136.1 0.0 copy-start.7
  136.1 0.0 copy-start.8
  136.2 0.0 copy-start.11
  136.2 0.0 copy-start.12
  136.2 52.4 %settle.1 = (f32[48,4608]{1,0:T(8,128)S(1)}, bf16[1024,768]{1,0:T(8,128)(2,1)S(1)}, f32[1024,768]{1,0:T(8,128)S(1)}, f32[4,768]{1,0:T(4,128)S(1)}) custom-call(bf16[8,48,4608]{2,1,0:T(8,128)(2,1)S(1)} %disperse.1.p_ref, bf16[1024,768]{1,0:T(8,128)(2,1)S(1)} %get-tuple-element.51.out_in, bf16[1024,704]{1,0:T(8,128)(2,1)S(1)} %get-tuple-element.52.dproj_ref, ...), custom_call_target="tpu_custom_call" | custom-call | tf_op jit(solution)/shard_map/settle/pallas_call | solution.py:1409
  188.7 51.3 %soap.1 = (f32[2304,96]{1,0:T(8,128)}, f32[2304,96]{1,0:T(8,128)}, f32[2304,96]{1,0:T(8,128)}, f32[2304,96]{1,0:T(8,128)}, f32[2304,96]{1,0:T(8,128)}, /*index=5...) custom-call(f32[48,4608]{1,0:T(8,128)S(1)} %get-tuple-element.57.packed_ref, ...), custom_call_target="tpu_custom_call" | custom-call | tf_op jit(solution)/shard_map/soap/pallas_call | solution.py:463
  240.1 0.7 multiply_subtract_fusion
  (28 shorter events, 0.1 us)
Async XLA Ops:
  0.6 2.0 copy-start.14
  2.6 47.6 %copy-start.15 = (s32[768]{0:T(1024)S(1)}, s32[768]{0:T(1024)}, u32[]{:S(2)}) copy-start(s32[768]{0:T(1024)} %param.17) | copy-start | bytes 9220
  50.6 5.9 %copy-start.13 = (s32[1,1024]{1,0:T(1,128)S(1)}, s32[1,1024]{1,0:T(1,128)}, u32[]{:S(2)}) copy-start(s32[1,1024]{1,0:T(1,128)} %seg_row_ref.1) | copy-start | bytes 12292
  50.6 6.1 %copy-start = (bf16[1,1024,768]{2,1,0:T(8,128)(2,1)S(1)}, bf16[1,1024,768]{2,1,0:T(8,128)(2,1)}, u32[]{:S(2)}) copy-start(bf16[1,1024,768]{2,1,0:T(8,128)(2,1)} %param.14) | copy-start | bytes 4718596
  54.5 1.0 copy-start.3
  55.5 1.0 copy-start.5
  56.8 1.4 copy-start.2
  58.2 1.3 copy-start.4
  59.5 1.3 copy-start.6
  136.1 52.5 %copy-start.1 = (f32[1,96,48,48]{1,3,2,0:T(8,128)S(1)}, f32[1,96,48,48]{1,3,2,0:T(8,128)}, u32[]{:S(2)}) copy-start(f32[1,96,48,48]{1,3,2,0:T(8,128)} %param.18) | copy-start | bytes 2654212
  136.1 52.5 %copy-start.7 = (f32[1,96,48,48]{1,3,2,0:T(8,128)S(1)}, f32[1,96,48,48]{1,3,2,0:T(8,128)}, u32[]{:S(2)}) copy-start(f32[1,96,48,48]{1,3,2,0:T(8,128)} %param.19) | copy-start | bytes 2654212
  136.1 52.5 %copy-start.8 = (f32[1,96,48,48]{1,3,2,0:T(8,128)S(1)}, f32[1,96,48,48]{1,3,2,0:T(8,128)}, u32[]{:S(2)}) copy-start(f32[1,96,48,48]{1,3,2,0:T(8,128)} %param.20) | copy-start | bytes 2654212
  136.1 52.5 %copy-start.9 = (f32[1,96,48,48]{1,3,2,0:T(8,128)S(1)}, f32[1,96,48,48]{1,3,2,0:T(8,128)}, u32[]{:S(2)}) copy-start(f32[1,96,48,48]{1,3,2,0:T(8,128)} %param.21) | copy-start | bytes 2654212
  136.1 52.5 %copy-start.10 = (f32[1,96,48,48]{1,3,2,0:T(8,128)S(1)}, f32[1,96,48,48]{1,3,2,0:T(8,128)}, u32[]{:S(2)}) copy-start(f32[1,96,48,48]{1,3,2,0:T(8,128)} %param.22) | copy-start | bytes 2654212
  136.2 52.5 %copy-start.11 = (f32[1,96,48,48]{1,3,2,0:T(8,128)S(1)}, f32[1,96,48,48]{1,3,2,0:T(8,128)}, u32[]{:S(2)}) copy-start(f32[1,96,48,48]{1,3,2,0:T(8,128)} %param.23) | copy-start | bytes 2654212
  136.2 52.5 %copy-start.12 = (f32[1,96,48,48]{1,3,2,0:T(8,128)S(1)}, f32[1,96,48,48]{1,3,2,0:T(8,128)}, u32[]{:S(2)}) copy-start(f32[1,96,48,48]{1,3,2,0:T(8,128)} %param.24) | copy-start | bytes 2654212
  188.7 51.3 %copy-start.16 = (f32[384]{0:T(512)S(1)}, f32[384]{0:T(512)}, u32[]{:S(2)}) copy-start(f32[384]{0:T(512)} %param.27) | copy-start | bytes 4612
  188.7 51.3 %copy-start.17 = (f32[384]{0:T(512)S(1)}, f32[384]{0:T(512)}, u32[]{:S(2)}) copy-start(f32[384]{0:T(512)} %param.26) | copy-start | bytes 4612

commit v6 on v5

--- a/solution.py
+++ b/solution.py
@@ -12,7 +12,9 @@
 STEP = 10
 F32 = jnp.float32
 BF16 = jnp.bfloat16
-LAYER_LIMIT = 33 * 2**20
+LAYER_LIMIT = 35 * 2**20
+GATHER_LIMIT = 35 * 2**20
+SETTLE_LIMIT = 31 * 2**20
 
 norm_eps = 1e-05
 beta_one = 0.9
@@ -46,6 +48,12 @@
     )
 
 
+def piece_cuts(rows, cols, parts):
+    attn = rows // parts
+    hidden = (cols - 4 * attn) // 2
+    return (0, 3 * attn, 3 * attn + hidden, 4 * attn + hidden, cols)
+
+
 MESH = pl.DeviceIdType.MESH
 VM = pl.BlockSpec(memory_space=pltpu.VMEM)
 MIB = 2**20
@@ -85,7 +93,10 @@
     pl.semaphore_wait(barrier, 3 - ends)
 
 
-def gather_kernel(n, count, block, wide, norm_rows, m_ref, norm_ref, u_ref, nout_ref, held, send_sem, recv_sem):
+def gather_kernel(
+    n, count, block, wide, norm_rows, norm_per, rows, cuts, slot_ref, m_ref, norm_ref, *refs
+):
+    w_refs, (nout_ref, u_ref, held, send_sem, recv_sem) = refs[:4], refs[4:]
     m = n // 2
     dp, t = lax.axis_index("dp"), lax.axis_index("tensor")
     place, side = dp // 2, lax.rem(dp, 2)
@@ -105,7 +116,6 @@
     def unpack(source):
         for k in range(count):
             u_ref[source * count + k] = held[source, :, k * block : (k + 1) * block]
-        nout_ref[source] = held[source, :16, wide : wide + 128]
 
     def spread(source, left, right):
         send(source, 2, pair).start()
@@ -164,6 +174,25 @@
         return 0
 
     lax.fori_loop(0, m, other, 0)
+
+    def strip(row, _):
+        for first, last, w_ref in zip(cuts, cuts[1:], w_refs):
+            w_ref[pl.ds(pl.multiple_of(row * block, block), block), :] = jnp.concatenate(
+                [u_ref[slot_ref[row * cuts[-1] + c]] for c in range(first, last)], axis=1
+            )
+        return 0
+
+    lax.fori_loop(0, rows, strip, 0)
+
+    line = nout_ref.shape[1]
+    for source in range(n):
+        values = held[source, :16, wide : wide + 128].astype(F32)
+        for r in range(norm_rows):
+            spot = source * norm_per + r * 128
+            size = min(128, norm_per - r * 128)
+            nout_ref[spot // line : spot // line + 1, spot % line : spot % line + size] = values[
+                r : r + 1, :size
+            ]
 
     def finish(step, _):
         source = step * 2 + side
@@ -177,28 +206,34 @@
     lax.fori_loop(0, m, finish, 0)
 
 
-def gather_masters(masters, norm, n):
+def gather_masters(slots, masters, norm, n, rows, parts):
     count, block = masters.shape[0], masters.shape[-1]
     wide = tiles_up(count * block)
     norm_rows = -(-norm.shape[0] // 128)
     norm_tile = jnp.pad(norm, (0, norm_rows * 128 - norm.shape[0])).reshape(norm_rows, 128)
-    blocks, norms = pl.pallas_call(
-        functools.partial(gather_kernel, n, count, block, wide, norm_rows),
+    cuts = piece_cuts(rows, n * count // rows, parts)
+    *pieces, norms = pl.pallas_call(
+        functools.partial(gather_kernel, n, count, block, wide, norm_rows, norm.shape[0], rows, cuts),
         out_shape=[
-            jax.ShapeDtypeStruct((n * count, block, block), BF16),
-            jax.ShapeDtypeStruct((n, 16, 128), BF16),
-        ],
-        in_specs=[VM, VM],
-        out_specs=[VM, VM],
+            jax.ShapeDtypeStruct((rows * block, (last - first) * block), BF16)
+            for first, last in zip(cuts, cuts[1:])
+        ]
+        + [jax.ShapeDtypeStruct((4, n * norm.shape[0] // 4), F32)],
+        in_specs=[pl.BlockSpec(memory_space=pltpu.SMEM), VM, VM],
+        out_specs=[VM] * 5,
         scratch_shapes=[
+            pltpu.VMEM((n * count, block, block), BF16),
             pltpu.VMEM((n, block, wide + 128), BF16),
             pltpu.SemaphoreType.DMA((n, 3)),
             pltpu.SemaphoreType.DMA((n,)),
         ],
-        compiler_params=pltpu.CompilerParams(collective_id=1, has_side_effects=True, vmem_limit_bytes=10 * MIB),
+        compiler_params=pltpu.CompilerParams(
+            collective_id=1, has_side_effects=True, vmem_limit_bytes=GATHER_LIMIT
+        ),
         name="gather_masters",
-    )(masters, norm_tile)
-    return blocks, norms.reshape(n, 16 * 128)[:, : norm.shape[0]].reshape(-1)
+        cost_estimate=pl.CostEstimate(flops=0, bytes_accessed=163200000, transcendentals=0),
+    )(slots, masters, norm_tile)
+    return pieces, norms
 
 
 NN = ((1,), (0,))
@@ -469,86 +504,10 @@
         + [pltpu.VMEM((2 * n * n, count), F32), pltpu.VMEM((count, n, n), F32)]
         + [room] * 5
         + [pltpu.SemaphoreType.DMA((9,))],
-        compiler_params=pltpu.CompilerParams(vmem_limit_bytes=24 * MIB),
+        compiler_params=pltpu.CompilerParams(vmem_limit_bytes=31 * MIB),
         name="soap",
     )(packed, output, input_grad, *flat)
     return [item.reshape(n, n, count).transpose(2, 0, 1) for item in outs[:7]] + list(outs[7:])
-
-
-def assemble_kernel(rows, cols, block, cuts, slot_ref, u_ref, *w_refs):
-    def one(row, _):
-        for first, last, w_ref in zip(cuts, cuts[1:], w_refs):
-            strip = jnp.concatenate([u_ref[slot_ref[row * cols + c]] for c in range(first, last)], axis=1)
-            w_ref[pl.ds(pl.multiple_of(row * block, block), block), :] = strip
-        return 0
-
-    lax.fori_loop(0, rows, one, 0)
-
-
-def piece_cuts(rows, cols, parts):
-    attn = rows // parts
-    hidden = (cols - 4 * attn) // 2
-    return (0, 3 * attn, 3 * attn + hidden, 4 * attn + hidden, cols)
-
-
-def assemble(slots, blocks, rows, parts):
-    block = blocks.shape[-1]
-    cols = blocks.shape[0] // rows
-    cuts = piece_cuts(rows, cols, parts)
-    return pl.pallas_call(
-        functools.partial(assemble_kernel, rows, cols, block, cuts),
-        out_shape=[
-            jax.ShapeDtypeStruct((rows * block, (last - first) * block), BF16)
-            for first, last in zip(cuts, cuts[1:])
-        ],
-        in_specs=[pl.BlockSpec(memory_space=pltpu.SMEM), VM],
-        out_specs=[VM] * 4,
-        compiler_params=pltpu.CompilerParams(vmem_limit_bytes=4 * MIB),
-        name="assemble",
-    )(slots, blocks)
-
-
-def disperse_kernel(rows, cols, block, cuts, n, count, wide, inverse_ref, *refs):
-    g_refs, p_ref, u_scr = refs[:4], refs[4], refs[5]
-
-    def cut(row, _):
-        for first, last, g_ref in zip(cuts, cuts[1:], g_refs):
-            strip = g_ref[pl.ds(pl.multiple_of(row * block, block), block), :]
-            for c in range(first, last):
-                u_scr[row * cols + c] = strip[:, (c - first) * block : (c - first + 1) * block]
-        return 0
-
-    lax.fori_loop(0, rows, cut, 0)
-
-    some = math.gcd(count, 8)
-
-    def lay(d, _):
-        for k in range(0, count, some):
-            strip = [u_scr[inverse_ref[d * count + k + e]] for e in range(some)]
-            p_ref[d, :, k * block : (k + some) * block] = jnp.concatenate(strip, axis=1)
-        if wide > count * block:
-            p_ref[d, :, count * block : wide] = jnp.zeros((block, wide - count * block), BF16)
-        return 0
-
-    lax.fori_loop(0, n, lay, 0)
-
-
-def disperse(inverse, grads, n, block, parts):
-    rows = grads[0].shape[0] // block
-    cols = sum(grad.shape[1] for grad in grads) // block
-    count = rows * cols // n
-    wide = tiles_up(count * block)
-    return pl.pallas_call(
-        functools.partial(
-            disperse_kernel, rows, cols, block, piece_cuts(rows, cols, parts), n, count, wide
-        ),
-        out_shape=jax.ShapeDtypeStruct((n, block, wide), BF16),
-        in_specs=[pl.BlockSpec(memory_space=pltpu.SMEM)] + [VM] * 4,
-        out_specs=VM,
-        scratch_shapes=[pltpu.VMEM((rows * cols, block, block), BF16)],
-        compiler_params=pltpu.CompilerParams(vmem_limit_bytes=16 * MIB),
-        name="disperse",
-    )(inverse, *grads)
 
 
 BLK = 128
@@ -682,24 +641,21 @@
 def layer_kernel(
     heads,
     shift,
+    cuts,
     x_ref,
-    seg_row_ref,
-    seg_col_ref,
+    seg_in,
     dy_ref,
     wp_ref,
     w1_ref,
     wo_ref,
     w2_ref,
     norm_ref,
-    gp_ref,
-    g1_ref,
-    go_ref,
-    g2_ref,
+    mat_ref,
     out_ref,
     dproj_ref,
     wf_out,
+    dhb_ref,
     resid_ref,
-    dres_ref,
     ng_ref,
     a_ref,
     wf_ref,
@@ -711,7 +667,6 @@
     cn_ref,
     s_ref,
     du_ref,
-    dhb_ref,
     dkv_ref,
     carry_ref,
     raw_scr,
@@ -743,6 +698,8 @@
     gf_far,
     share_sem,
     collect_sem,
+    seg_row_ref,
+    seg_col_ref,
 ):
     dp, t = lax.axis_index("dp"), lax.axis_index("tensor")
     up, core = t // 2, lax.rem(t, 2)
@@ -755,6 +712,11 @@
     one = Packs(three, o_own, o_beside, o_over, o_far, o_sem)
     outer = Packs(three, wo_own, wo_beside, wo_over, wo_far, wo_sem)
     greet([beside, over])
+    seg_row_ref[...] = seg_in[...].astype(F32)
+    by_block = jnp.concatenate([seg_row_ref[:, b * BLK : (b + 1) * BLK] for b in range(blocks)], axis=0)
+    turned_seg = by_block.T
+    for b in range(blocks):
+        seg_col_ref[b * BLK : (b + 1) * BLK] = turned_seg[:, b : b + 1]
 
     def give(where, i):
         return remote(wf_ref, wf_ref, share_sem.at[i], share_sem.at[2], where)
@@ -899,12 +861,6 @@
         one.pack(b, o)
         one.send(b)
 
-    def act_back(i, _):
-        rows = wide_rows(i)
-        dres_ref[rows] = dot(dy_ref[rows], w2_ref[...], NN)
-        return 0
-
-    lax.fori_loop(0, length // wide, act_back, 0)
     outer.relay(0)
 
     def mlp(b):
@@ -923,7 +879,7 @@
         half = 0.5 * (1.0 + bent)
         s_ref[rows] = (u * half).astype(BF16)
         slope = half + 0.5 * u * (1.0 - bent * bent) * (root * (1.0 + 3 * 0.044715 * square))
-        du = (dres_ref[rows] * slope).astype(BF16)
+        du = (dot(dy_ref[rows], w2_ref[...], NN) * slope).astype(BF16)
         du_ref[rows] = du
         x3_ref[rows] = dot(du, w1_ref[...], NT).astype(BF16)
         three.enter(b)
@@ -973,8 +929,6 @@
     for b in reversed(range(turned_from, blocks)):
         three.add(b)
         three.cross(b)
-    g2_ref[...] = dot(dy_ref[...], s_ref[...], TN).astype(BF16)
-    g1_ref[...] = dot(cn_ref[...], du_ref[...], TN).astype(BF16)
 
     def mlp_out(i, _):
         rows = wide_rows(i)
@@ -982,6 +936,9 @@
         return 0
 
     lax.fori_loop(0, length // wide, mlp_out, 0)
+    mat_ref[:, cuts[3] : cuts[4]] = dot(dy_ref[...], s_ref[...], TN).astype(BF16)
+    mat_ref[:, cuts[1] : cuts[2]] = dot(cn_ref[...], du_ref[...], TN).astype(BF16)
+    mat_ref[:, cuts[4] :] = jnp.zeros((width, mat_ref.shape[1] - cuts[4]), BF16)
 
     for early in range(turned_from):
         three.relay(early)
@@ -1005,7 +962,6 @@
         ng_ref[0:1, :] += jnp.sum(d_two * plain, axis=0, keepdims=True)
         ng_ref[1:2, :] += jnp.sum(d_two, axis=0, keepdims=True)
         dres = dy_ref[rows].astype(F32) + norm_back(plain, inverse_std, d_two * gain_two)
-        dres_ref[rows] = dres
         dhb = dres.astype(BF16)
         dhb_ref[rows] = dhb
         do = dot(dhb, wo_ref[...], NN).astype(BF16)
@@ -1072,16 +1028,16 @@
         collect(gf_ref, gf_far, over, 1).start()
 
     dproj_ref[:, attn : 3 * attn] = dkv_ref[: 2 * attn].T.astype(BF16)
-    go_ref[...] = dot(dhb_ref[...], o_ref[...], TN).astype(BF16)
+    mat_ref[:, cuts[2] : cuts[3]] = dot(dhb_ref[...], o_ref[...], TN).astype(BF16)
     grad = dot(a_ref[...], dproj_ref[:, : 3 * attn], TN)
-    gp_ref[...] = grad.astype(BF16)
+    mat_ref[:, : cuts[1]] = grad.astype(BF16)
 
     @pl.when(t == 0)
     def _():
         collect(gf_ref, gf_far, over, 1).wait_recv()
         extra = gf_ref[...].astype(F32) + gf_far[...].astype(F32)
-        gp_ref[:, :HD] = (gp_ref[:, :HD].astype(F32) + extra[:, :HD]).astype(BF16)
-        gp_ref[:, attn : attn + HD] = (gp_ref[:, attn : attn + HD].astype(F32) + extra[:, HD:]).astype(BF16)
+        mat_ref[:, :HD] = (mat_ref[:, :HD].astype(F32) + extra[:, :HD]).astype(BF16)
+        mat_ref[:, attn : attn + HD] = (mat_ref[:, attn : attn + HD].astype(F32) + extra[:, HD:]).astype(BF16)
         give(over, 0).wait_send()
 
     @pl.when(core == 0)
@@ -1105,10 +1061,12 @@
     outer.close(0)
 
 
-def layer(inputs, segments, cotangent, wp, w1, wo, w2, norms):
+def layer(inputs, segments, cotangent, wp, w1, wo, w2, norms, block):
     length, width = inputs.shape
     attn, hidden = wo.shape[1], w1.shape[1]
     heads = attn // HD
+    rows, cols = width // block, 4 * attn // block + 2 * (hidden // block)
+    cuts = piece_cuts(rows, cols, width // attn)
     blocks = length // BLK
     span = min(length // 2 + BLK, length)
 
@@ -1122,21 +1080,18 @@
         return jax.ShapeDtypeStruct(shape, dtype)
 
     return pl.pallas_call(
-        functools.partial(layer_kernel, heads, shift_for(length)),
+        functools.partial(layer_kernel, heads, shift_for(length), [cut * block for cut in cuts]),
         out_shape=[
-            out(wp.shape, BF16),
-            out(w1.shape, BF16),
-            out(wo.shape, BF16),
-            out(w2.shape, BF16),
+            out((width, cols * block + 128), BF16),
             out((length, width), BF16),
             out((length, 3 * attn + 2 * HD), BF16),
             out((width, 2 * HD), BF16),
-            out((length, width), F32),
+            out((length, width), BF16),
             out((length, width), F32),
             out((2, width), F32),
         ],
-        in_specs=[VM] * 9,
-        out_specs=[VM] * 10,
+        in_specs=[VM] * 8,
+        out_specs=[VM] * 7,
         scratch_shapes=[
             low(length, width),
             low(width, 2 * HD),
@@ -1148,7 +1103,6 @@
             low(length, width),
             low(length, hidden),
             low(length, hidden),
-            low(length, width),
             pltpu.VMEM((2 * attn + HD, length), F32),
             pltpu.VMEM((8, length), F32),
             pltpu.VMEM((heads + 1, BLK, span), F32),
@@ -1163,15 +1117,16 @@
         + [pltpu.SemaphoreType.DMA((6, 1)), low(width, width)]
         + total
         + [low(width, 2 * HD)] * 3
-        + [pltpu.SemaphoreType.DMA((3,)), pltpu.SemaphoreType.DMA((4,))],
+        + [pltpu.SemaphoreType.DMA((3,)), pltpu.SemaphoreType.DMA((4,))]
+        + [pltpu.VMEM((1, length), F32), pltpu.VMEM((length, 1), F32)],
         compiler_params=pltpu.CompilerParams(
             collective_id=3, has_side_effects=True, vmem_limit_bytes=LAYER_LIMIT
         ),
         name="layer",
+        cost_estimate=pl.CostEstimate(flops=0, bytes_accessed=221000000, transcendentals=0),
     )(
         inputs,
         segments.reshape(1, length),
-        segments.reshape(length, 1),
         cotangent,
         wp,
         w1,
@@ -1183,13 +1138,15 @@
 
 def settle_kernel(
     n,
-    p_ref,
+    count,
+    inverse_ref,
+    mat_ref,
     out_in,
     dproj_ref,
     wp_ref,
     wf_ref,
+    dhb_ref,
     resid_ref,
-    dres_ref,
     x_ref,
     norm_ref,
     ng_in,
@@ -1197,6 +1154,8 @@
     output_ref,
     grad_ref,
     ng_ref,
+    p_ref,
+    u_scr,
     xin,
     lin,
     rin,
@@ -1231,6 +1190,16 @@
     two = Total(dp, t, out_in, near2, mine2, far2, near_mine2, near_far2, sem2)
     blocks = four.blocks
     peers = [lax.rem(dp + hop, n) for hop in range(1, n)]
+    size, wide = p_ref.shape[1:]
+    cols = (mat_ref.shape[1] - 128) // size
+
+    def chop(row, _):
+        whole_row = mat_ref[pl.ds(pl.multiple_of(row * size, size), size), :]
+        for c in range(cols):
+            u_scr[row * cols + c] = whole_row[:, c * size : (c + 1) * size]
+        return 0
+
+    lax.fori_loop(0, mat_ref.shape[0] // size, chop, 0)
     greet([four.beside, four.over] + [(peer, t) for peer in peers])
 
     def across(q):
@@ -1253,6 +1222,7 @@
                 one(place - hop, False)
 
     def work(q, right):
+        lay(q * 2 + side)
         across(q).wait_recv()
         own = p_ref[q * 2 + side].astype(F32) + xin[q].astype(F32)
         if right:
@@ -1280,6 +1250,7 @@
 
     def keep():
         q = place
+        lay(q * 2 + side)
         across(q).wait_recv()
         g_ref[...] = p_ref[q * 2 + side].astype(F32) + xin[q].astype(F32)
 
@@ -1299,22 +1270,52 @@
     def norm_from(peer):
         return remote(ng_ref, norm_held.at[peer], norm_send.at[peer], norm_recv.at[peer], (peer, t))
 
-    for hop in reversed(range(m)):
-        both(hop, lambda q, right: across(q).start())
+    some = math.gcd(count, 8)
+    room = tiles_up(some * size) // 128
+
+    def strip(base):
+        return jnp.concatenate([u_scr[inverse_ref[base + e]] for e in range(some)], axis=1)
+
+    def lay(d):
+        if some * size == room * 128:
+            def one(g, _):
+                place = pl.ds(pl.multiple_of(g * room * 128, 128), room * 128)
+                p_ref[d, :, place] = strip(d * count + g * some)
+                return 0
+
+            lax.fori_loop(0, count // some, one, 0, unroll=3)
+        else:
+            parts = [strip(d * count + g * some)[:, : some * size] for g in range(count // some)]
+            if wide > count * size:
+                parts.append(jnp.zeros((size, wide - count * size), BF16))
+            p_ref[d] = jnp.concatenate(parts, axis=1)
+
+    def give(q, right):
+        lay(q * 2 + 1 - side)
+        across(q).start()
+
     cut = wp_ref.shape[1]
-    for b in range(blocks):
+
+    def project_back(b):
         rows = pl.ds(b * four.size, four.size)
         da = dot(dproj_ref[rows, :cut], wp_ref[...], NT)
         da_scr[rows] = (da + dot(dproj_ref[rows, cut:], wf_ref[...], NT)).astype(BF16)
         four.enter(b)
-    for b in range(blocks):
-        two.enter(b)
-    for b in range(blocks):
-        four.add(b)
-        four.cross(b)
+
+    for step, hop in enumerate(reversed(range(m))):
+        both(hop, give)
+        if step == 0:
+            for b in range(blocks):
+                project_back(b)
+        if step == 1:
+            for b in range(blocks):
+                four.add(b)
+                four.cross(b)
+                two.enter(b)
     for b in range(blocks):
         two.add(b)
         two.cross(b)
+
     ng_ref[...] = jnp.zeros_like(ng_ref)
     gain = norm_ref[0:1, :]
 
@@ -1328,7 +1329,7 @@
         plain, inverse_std = plain_norm(x_ref[rows].astype(F32))
         ng_ref[0:1, :] += jnp.sum(d_one * plain, axis=0, keepdims=True)
         ng_ref[1:2, :] += jnp.sum(d_one, axis=0, keepdims=True)
-        grad_ref[rows] = dres_ref[rows] + norm_back(plain, inverse_std, d_one * gain)
+        grad_ref[rows] = dhb_ref[rows].astype(F32) + norm_back(plain, inverse_std, d_one * gain)
 
     def out_block(b):
         rows = rows_of(b)
@@ -1365,7 +1366,7 @@
     tasks.append(functools.partial(out_block, blocks - 1))
     done = 0
     for step, hop in enumerate(reversed(range(1, m))):
-        until = len(tasks) * (step + 1) // m
+        until = min((1, 10, 18, len(tasks))[min(step, 3)], len(tasks))
         while done < until:
             tasks[done]()
             done += 1
@@ -1395,11 +1396,12 @@
         two.close(b)
 
 
-def settle(packed, out_part, dproj, wp, wf, resid, dres, inputs, norms, ng):
-    n, block, wide = packed.shape
+def settle(inverse, matrix, block, out_part, dproj, wp, wf, dhb, resid, inputs, norms, ng, n):
+    count = matrix.shape[0] // block * ((matrix.shape[1] - 128) // block) // n
+    wide = tiles_up(count * block)
     m = n // 2
     length, width = inputs.shape
-    blocks = 4
+    blocks = 8
 
     def low(*shape):
         return pltpu.VMEM(shape, BF16)
@@ -1407,26 +1409,28 @@
     half = length // 2
     total = [low(half, width)] * 5 + [pltpu.SemaphoreType.DMA((8, blocks))]
     return pl.pallas_call(
-        functools.partial(settle_kernel, n),
+        functools.partial(settle_kernel, n, count),
         out_shape=[
             jax.ShapeDtypeStruct((block, wide), F32),
             jax.ShapeDtypeStruct((length, width), BF16),
             jax.ShapeDtypeStruct((length, width), F32),
             jax.ShapeDtypeStruct((4, width), F32),
         ],
-        in_specs=[VM] * 10,
+        in_specs=[pl.BlockSpec(memory_space=pltpu.SMEM)] + [VM] * 10,
         out_specs=[VM] * 4,
-        scratch_shapes=[low(m, block, wide)] * 3
+        scratch_shapes=[low(n, block, wide), low(n * count, block, block)]
+        + [low(m, block, wide)] * 3
         + [pltpu.SemaphoreType.DMA((m,))] * 6
         + total
         + total
         + [pltpu.VMEM((n, 4, width), F32), pltpu.SemaphoreType.DMA((n,)), pltpu.SemaphoreType.DMA((n,))]
         + [low(length, width)],
         compiler_params=pltpu.CompilerParams(
-            collective_id=2, has_side_effects=True, vmem_limit_bytes=24 * MIB
+            collective_id=2, has_side_effects=True, vmem_limit_bytes=SETTLE_LIMIT
         ),
         name="settle",
-    )(packed, out_part, dproj, wp, wf, resid, dres, inputs, norms, ng)
+        cost_estimate=pl.CostEstimate(flops=0, bytes_accessed=187000000, transcendentals=0),
+    )(inverse, matrix, out_part, dproj, wp, wf, dhb, resid, inputs, norms, ng)
 
 
 def norm_update(grad, master, first, second):
@@ -1462,20 +1466,27 @@
     parts = lax.axis_size("tensor")
     per_dev = masters.shape[1]
     block = masters.shape[-1]
-    blocks, shared_norms = gather_masters(masters[0], norm_master, n_dp)
-    slots, inverse = block_slots(owner, per_dev)
-    pieces = assemble(slots, blocks, width // block, parts)
-    norms = shared_norms.astype(F32).reshape(4, width)
-    *grads, out_part, dproj, w_first, resid, dres, norm_grads = layer(
-        inputs[0], segments[0], cotangent[0], *pieces, norms
+    slots, inverse = lax.optimization_barrier(block_slots(owner, per_dev))
+    pieces, norms = gather_masters(
+        slots, masters[0], norm_master, n_dp, width // block, parts
     )
-    packed = disperse(inverse, grads, n_dp, block, parts)
+    grad_matrix, out_part, dproj, w_first, dhb, resid, norm_grads = layer(
+        inputs[0], segments[0], cotangent[0], *pieces, norms, block
+    )
     own_packed, output, input_grad, norm_grads = settle(
-        packed, out_part, dproj, pieces[0], w_first, resid, dres, inputs[0], norms, norm_grads
-    )
-    norm_per = norm_master.shape[0]
-    own_norm_grads = lax.dynamic_slice_in_dim(
-        norm_grads.reshape(-1), lax.axis_index("dp") * norm_per, norm_per
+        inverse,
+        grad_matrix,
+        block,
+        out_part,
+        dproj,
+        pieces[0],
+        w_first,
+        dhb,
+        resid,
+        inputs[0],
+        norms,
+        norm_grads,
+        n_dp,
     )
     *updated, output, input_grad = soap(
         own_packed,
@@ -1488,6 +1499,11 @@
         right_stats[0],
         left_basis[0],
         right_basis[0],
+    )
+    norm_grads, output = lax.optimization_barrier((norm_grads, output))
+    norm_per = norm_master.shape[0]
+    own_norm_grads = lax.dynamic_slice_in_dim(
+        norm_grads.reshape(-1), lax.axis_index("dp") * norm_per, norm_per
     )
     norm_first_new, norm_second_new, norm_new = norm_update(
         own_norm_grads, norm_master, norm_first, norm_second

time: 244 us -> 237 us (0.971)
  local copies, waits for them, and re-layouts: 8.28 us -> 3.47 us
  Pallas kernels: 230 us -> 226 us
    pallas_call x4 -> x2, Pallas kernels: 131 us -> 124 us  [the longest x1 65.1 us: layer(): pl.pallas_call(functools.partial(layer_kernel, heads, shift_for(length),...]
    unnamed x38 -> x27, local copies, waits for them, and re-layouts: 8.03 us -> 3.46 us
    pallas_call x1, Pallas kernels: 47.6 us -> 51.4 us  [gather_masters(): pl.pallas_call(functools.partial(gather_kernel, n, count, block, wide, no...]
where the time goes in v6:
time: 237 us; the launch traced here: 234 us
  Pallas kernels  226 us (95%)
  local copies, waits for them, and re-layouts  3.47 us (1%)
  other arithmetic  2.81 us (1%)
    pallas_call x1, Pallas kernels, layer(): pl.pallas_call(functools.partial(layer_kernel, heads, shift_for(length),...  65.1 us
    pallas_call x1, Pallas kernels, settle(): pl.pallas_call(functools.partial(settle_kernel, n, count), out_shape=[jax...  58.7 us
    pallas_call x1, Pallas kernels, gather_masters(): pl.pallas_call(functools.partial(gather_kernel, n, count, block, wide, no...  51.4 us
    pallas_call x1, Pallas kernels, soap(): pl.pallas_call(functools.partial(soap_kernel, n, count), out_shape=[shape...  51.2 us

profile of v6, /device:TPU:0, one launch (start us, length us, event | category | flops | bytes accessed | tf_op | source)
XLA Modules:
  0.0 233.9 jit_solution(6711932871663225936)
XLA Ops:
  0.6 1.1 convert_reduce_fusion
  1.8 0.7 multiply_add_fusion.slot_ref
  2.5 0.3 select_reduce_fusion.inverse_ref
  2.8 0.0 copy-start.9
  2.8 2.0 copy.28
  4.8 0.0 copy-start
  4.8 0.0 copy-start.10
  4.8 51.4 %gather_masters.1 = (bf16[768,576]{1,0:T(8,128)(2,1)S(1)}, bf16[768,768]{1,0:T(8,128)(2,1)S(1)}, bf16[768,192]{1,0:T(8,128)(2,1)S(1)}, bf16[768,768]{1,0:T(8,128)(2,1)S(1)}, f32[4,768]{1,0:T(4,128)S(1)}) custom-call(s32[768]{0:T(1024)S(1)} %multiply_add_fusion.slot_ref, f32[96,48,48]{2,1,0:T(8,128)S(1)} %bitcast.75, f32[3,128]{1,0:T(4,128)S(1)} %bitcast.86), custom_call_target="tpu_custom_call" | custom-call | bytes 163200000 | tf_op jit(solution)/shard_map/gather_masters/pallas_call | solution.py:215
  56.2 0.0 copy-start.2
  56.2 1.4 copy-done.2
  57.6 65.1 %layer.1 = (bf16[768,2432]{1,0:T(8,128)(2,1)S(1)}, bf16[1024,768]{1,0:T(8,128)(2,1)S(1)}, bf16[1024,704]{1,0:T(8,128)(2,1)S(1)}, bf16[768,128]{1,0:T(8,128)(2,1)...) custom-call(bf16[1024,768]{1,0:T(8,128)(2,1)S(1)} %bitcast.76, ...), custom_call_target="tpu_custom_call" | custom-call | bytes 221000000 | tf_op jit(solution)/shard_map/layer/pallas_call | solution.py:1082
  122.8 0.0 copy-start.1
  122.8 0.0 copy-start.3
  122.8 0.0 copy-start.4
  122.8 0.0 copy-start.5
  122.8 0.0 copy-start.6
  122.9 0.0 copy-start.7
  122.9 0.0 copy-start.8
  122.9 58.7 %settle.1 = (f32[48,4608]{1,0:T(8,128)S(1)}, bf16[1024,768]{1,0:T(8,128)(2,1)S(1)}, f32[1024,768]{1,0:T(8,128)S(1)}, f32[4,768]{1,0:T(4,128)S(1)}) custom-call(s32[768]{0:T(1024)S(1)} %select_reduce_fusion.inverse_ref, bf16[768,2432]{1,0:T(8,128)(2,1)S(1)} %get-tuple-element.48.mat_ref, bf16[1024,768]{1,0:T(8,128)(2,1)S(1)} %get-tuple-element.49.out_in, ...), custom_call_target="tpu_custom_call" | custom-call | bytes 187000000 | tf_op jit(solution)/shard_map/settle/pallas_call | solution.py:1411
  181.7 0.0 copy-start.11
  181.7 0.0 copy-start.12
  181.7 51.2 %soap.1 = (f32[2304,96]{1,0:T(8,128)}, f32[2304,96]{1,0:T(8,128)}, f32[2304,96]{1,0:T(8,128)}, f32[2304,96]{1,0:T(8,128)}, f32[2304,96]{1,0:T(8,128)}, /*index=5...) custom-call(f32[48,4608]{1,0:T(8,128)S(1)} %get-tuple-element.56.packed_ref, ...), custom_call_target="tpu_custom_call" | custom-call | tf_op jit(solution)/shard_map/soap/pallas_call | solution.py:498
  232.9 0.0 copy-done.11
  232.9 0.7 multiply_subtract_fusion
  (12 shorter events, 0.0 us)
Async XLA Ops:
  2.8 2.0 copy-start.9
  4.8 51.4 %copy-start = (bf16[1,1024,768]{2,1,0:T(8,128)(2,1)S(1)}, bf16[1,1024,768]{2,1,0:T(8,128)(2,1)}, u32[]{:S(2)}) copy-start(bf16[1,1024,768]{2,1,0:T(8,128)(2,1)} %param.14) | copy-start | bytes 4718596
  4.8 51.4 %copy-start.10 = (s32[1,1024]{1,0:T(1,128)S(1)}, s32[1,1024]{1,0:T(1,128)}, u32[]{:S(2)}) copy-start(s32[1,1024]{1,0:T(1,128)} %seg_in.1) | copy-start | bytes 12292
  56.2 1.4 copy-start.2
  122.8 58.8 %copy-start.1 = (f32[1,96,48,48]{1,3,2,0:T(8,128)S(1)}, f32[1,96,48,48]{1,3,2,0:T(8,128)}, u32[]{:S(2)}) copy-start(f32[1,96,48,48]{1,3,2,0:T(8,128)} %param.18) | copy-start | bytes 2654212
  122.8 58.8 %copy-start.3 = (f32[1,96,48,48]{1,3,2,0:T(8,128)S(1)}, f32[1,96,48,48]{1,3,2,0:T(8,128)}, u32[]{:S(2)}) copy-start(f32[1,96,48,48]{1,3,2,0:T(8,128)} %param.19) | copy-start | bytes 2654212
  122.8 58.8 %copy-start.4 = (f32[1,96,48,48]{1,3,2,0:T(8,128)S(1)}, f32[1,96,48,48]{1,3,2,0:T(8,128)}, u32[]{:S(2)}) copy-start(f32[1,96,48,48]{1,3,2,0:T(8,128)} %param.20) | copy-start | bytes 2654212
  122.8 58.8 %copy-start.5 = (f32[1,96,48,48]{1,3,2,0:T(8,128)S(1)}, f32[1,96,48,48]{1,3,2,0:T(8,128)}, u32[]{:S(2)}) copy-start(f32[1,96,48,48]{1,3,2,0:T(8,128)} %param.21) | copy-start | bytes 2654212
  122.8 58.8 %copy-start.6 = (f32[1,96,48,48]{1,3,2,0:T(8,128)S(1)}, f32[1,96,48,48]{1,3,2,0:T(8,128)}, u32[]{:S(2)}) copy-start(f32[1,96,48,48]{1,3,2,0:T(8,128)} %param.22) | copy-start | bytes 2654212
  122.9 58.8 %copy-start.7 = (f32[1,96,48,48]{1,3,2,0:T(8,128)S(1)}, f32[1,96,48,48]{1,3,2,0:T(8,128)}, u32[]{:S(2)}) copy-start(f32[1,96,48,48]{1,3,2,0:T(8,128)} %param.23) | copy-start | bytes 2654212
  122.9 58.8 %copy-start.8 = (f32[1,96,48,48]{1,3,2,0:T(8,128)S(1)}, f32[1,96,48,48]{1,3,2,0:T(8,128)}, u32[]{:S(2)}) copy-start(f32[1,96,48,48]{1,3,2,0:T(8,128)} %param.24) | copy-start | bytes 2654212
  181.7 51.2 %copy-start.11 = (f32[384]{0:T(512)S(1)}, f32[384]{0:T(512)}, u32[]{:S(2)}) copy-start(f32[384]{0:T(512)} %param.27) | copy-start | bytes 4612
  181.7 51.2 %copy-start.12 = (f32[384]{0:T(512)S(1)}, f32[384]{0:T(512)}, u32[]{:S(2)}) copy-start(f32[384]{0:T(512)} %param.26) | copy-start | bytes 4612

commit v7 on v6

--- a/solution.py
+++ b/solution.py
@@ -96,7 +96,7 @@
 def gather_kernel(
     n, count, block, wide, norm_rows, norm_per, rows, cuts, slot_ref, m_ref, norm_ref, *refs
 ):
-    w_refs, (nout_ref, u_ref, held, send_sem, recv_sem) = refs[:4], refs[4:]
+    w_refs, (nout_ref, u_ref, held, send_sem, recv_sem, side_send, side_recv) = refs[:4], refs[4:]
     m = n // 2
     dp, t = lax.axis_index("dp"), lax.axis_index("tensor")
     place, side = dp // 2, lax.rem(dp, 2)
@@ -110,57 +110,94 @@
     ).astype(BF16)
     line_greet(dp, t, m)
 
-    def send(source, way, where):
-        return remote(held.at[source], held.at[source], send_sem.at[source, way], recv_sem.at[source], where)
+    total = wide + 128
+    less = total // 128 // 6 * 128
+
+    middle = less + (total - less) // 256 * 128
+    parts = ((less, middle), (middle, total))
+
+    def send(source, way, where, part):
+        first, last = parts[part]
+        columns = held.at[source, :, first:last]
+        return remote(columns, columns, send_sem.at[source, way, part], recv_sem.at[source, part], where)
+
+    def side_send_to(source, way, where):
+        part = held.at[source, :, :less]
+        return remote(part, part, side_send.at[source, way], side_recv.at[source], where)
+
+    def side_spread(source, left, right):
+        @pl.when(left)
+        def _():
+            side_send_to(source, 0, (dp - 2, t)).start()
+
+        @pl.when(right)
+        def _():
+            side_send_to(source, 1, (dp + 2, t)).start()
 
     def unpack(source):
         for k in range(count):
             u_ref[source * count + k] = held[source, :, k * block : (k + 1) * block]
 
-    def spread(source, left, right):
-        send(source, 2, pair).start()
-
+    def spread(source, left, right, part):
         @pl.when(left)
         def _():
-            send(source, 0, (dp - 2, t)).start()
+            send(source, 0, (dp - 2, t), part).start()
 
         @pl.when(right)
         def _():
-            send(source, 1, (dp + 2, t)).start()
+            send(source, 1, (dp + 2, t), part).start()
+
+        send(source, 2, pair, part).start()
 
     def spread_done(source, left, right):
-        send(source, 2, pair).wait_send()
-
-        @pl.when(left)
-        def _():
-            send(source, 0, (dp - 2, t)).wait_send()
-
-        @pl.when(right)
-        def _():
-            send(source, 1, (dp + 2, t)).wait_send()
-
-    spread(dp, place > 0, place < m - 1)
+        for part in (0, 1):
+            send(source, 2, pair, part).wait_send()
+
+            @pl.when(left)
+            def _():
+                send(source, 0, (dp - 2, t), part).wait_send()
+
+            @pl.when(right)
+            def _():
+                send(source, 1, (dp + 2, t), part).wait_send()
+
+    side_send_to(dp, 2, pair).start()
+    side_spread(dp, place > 0, place < m - 1)
+    for part in (0, 1):
+        spread(dp, place > 0, place < m - 1, part)
+    beside = place * 2 + 1 - side
+    side_send_to(beside, 2, pair).wait_recv()
+    side_spread(beside, place > 0, place < m - 1)
     unpack(dp)
 
     def one(hop, _):
+        for part in (0, 1):
+            @pl.when(place - hop >= 0)
+            def _():
+                source = dp - 2 * hop
+                send(source, 2, pair, part).wait_recv()
+                spread(source, False, place < m - 1, part)
+
+            @pl.when(place + hop < m)
+            def _():
+                source = dp + 2 * hop
+                send(source, 2, pair, part).wait_recv()
+                spread(source, place > 0, False, part)
+
         @pl.when(place - hop >= 0)
         def _():
-            source = dp - 2 * hop
-            send(source, 2, pair).wait_recv()
-            spread(source, False, place < m - 1)
+            for s in (0, 1):
+                both = (place - hop) * 2 + s
+                side_send_to(both, 2, pair).wait_recv()
+                side_spread(both, False, place < m - 1)
+            unpack(dp - 2 * hop)
 
         @pl.when(place + hop < m)
         def _():
-            source = dp + 2 * hop
-            send(source, 2, pair).wait_recv()
-            spread(source, place > 0, False)
-
-        @pl.when(place - hop >= 0)
-        def _():
-            unpack(dp - 2 * hop)
-
-        @pl.when(place + hop < m)
-        def _():
+            for s in (0, 1):
+                both = (place + hop) * 2 + s
+                side_send_to(both, 2, pair).wait_recv()
+                side_spread(both, place > 0, False)
             unpack(dp + 2 * hop)
 
         return 0
@@ -169,7 +206,8 @@
 
     def other(step, _):
         source = step * 2 + 1 - side
-        send(source, 2, pair).wait_recv()
+        for part in (0, 1):
+            send(source, 2, pair, part).wait_recv()
         unpack(source)
         return 0
 
@@ -201,9 +239,21 @@
             (place > 0) & (step >= place),
             (place < m - 1) & (step <= place),
         )
+        for s in (0, 1):
+            both = step * 2 + s
+
+            @pl.when((place > 0) & (step >= place))
+            def _():
+                side_send_to(both, 0, (dp - 2, t)).wait_send()
+
+            @pl.when((place < m - 1) & (step <= place))
+            def _():
+                side_send_to(both, 1, (dp + 2, t)).wait_send()
+
         return 0
 
     lax.fori_loop(0, m, finish, 0)
+    side_send_to(dp, 2, pair).wait_send()
 
 
 def gather_masters(slots, masters, norm, n, rows, parts):
@@ -224,6 +274,8 @@
         scratch_shapes=[
             pltpu.VMEM((n * count, block, block), BF16),
             pltpu.VMEM((n, block, wide + 128), BF16),
+            pltpu.SemaphoreType.DMA((n, 3, 2)),
+            pltpu.SemaphoreType.DMA((n, 2)),
             pltpu.SemaphoreType.DMA((n, 3)),
             pltpu.SemaphoreType.DMA((n,)),
         ],
@@ -1202,14 +1254,24 @@
     lax.fori_loop(0, mat_ref.shape[0] // size, chop, 0)
     greet([four.beside, four.over] + [(peer, t) for peer in peers])
 
-    def across(q):
-        return remote(p_ref.at[q * 2 + 1 - side], xin.at[q], x_send.at[q], x_recv.at[q], pair)
-
-    def rightward(q):
-        return remote(lin.at[q], lin.at[q], r_send.at[q], l_recv.at[q], (dp + 2, t))
-
-    def leftward(q):
-        return remote(rin.at[q], rin.at[q], l_send.at[q], r_recv.at[q], (dp - 2, t))
+    middle = wide // 256 * 128
+    parts = ((0, middle), (middle, wide))
+
+    def piece(ref, part):
+        first, last = parts[part]
+        return ref.at[:, first:last]
+
+    def across(q, part):
+        src, dst = p_ref.at[q * 2 + 1 - side], xin.at[q]
+        return remote(piece(src, part), piece(dst, part), x_send.at[q, part], x_recv.at[q, part], pair)
+
+    def rightward(q, part):
+        ref = piece(lin.at[q], part)
+        return remote(ref, ref, r_send.at[q, part], l_recv.at[q, part], (dp + 2, t))
+
+    def leftward(q, part):
+        ref = piece(rin.at[q], part)
+        return remote(ref, ref, l_send.at[q, part], r_recv.at[q, part], (dp - 2, t))
 
     def both(hop, one):
         @pl.when(place + hop < m)
@@ -1223,46 +1285,40 @@
 
     def work(q, right):
         lay(q * 2 + side)
-        across(q).wait_recv()
-        own = p_ref[q * 2 + side].astype(F32) + xin[q].astype(F32)
-        if right:
-            @pl.when(place > 0)
+        for part in (0, 1):
+            first, last = parts[part]
+            across(q, part).wait_recv()
+            own = p_ref[q * 2 + side, :, first:last].astype(F32) + xin[q, :, first:last].astype(F32)
+            line, pass_on, is_end = (lin, rightward, place == 0) if right else (rin, leftward, place == m - 1)
+
+            @pl.when(jnp.logical_not(is_end))
             def _():
-                rightward(q).wait_recv()
-                lin[q] = (own + lin[q].astype(F32)).astype(BF16)
-
-            @pl.when(place == 0)
+                pass_on(q, part).wait_recv()
+                line[q, :, first:last] = (own + line[q, :, first:last].astype(F32)).astype(BF16)
+
+            @pl.when(is_end)
             def _():
-                lin[q] = own.astype(BF16)
-
-            rightward(q).start()
-        else:
-            @pl.when(place < m - 1)
-            def _():
-                leftward(q).wait_recv()
-                rin[q] = (own + rin[q].astype(F32)).astype(BF16)
-
-            @pl.when(place == m - 1)
-            def _():
-                rin[q] = own.astype(BF16)
-
-            leftward(q).start()
+                line[q, :, first:last] = own.astype(BF16)
+
+            pass_on(q, part).start()
 
     def keep():
         q = place
         lay(q * 2 + side)
-        across(q).wait_recv()
-        g_ref[...] = p_ref[q * 2 + side].astype(F32) + xin[q].astype(F32)
-
-        @pl.when(place > 0)
-        def _():
-            rightward(q).wait_recv()
-            g_ref[...] += lin[q].astype(F32)
-
-        @pl.when(place < m - 1)
-        def _():
-            leftward(q).wait_recv()
-            g_ref[...] += rin[q].astype(F32)
+        for part in (0, 1):
+            first, last = parts[part]
+            across(q, part).wait_recv()
+            g_ref[:, first:last] = p_ref[q * 2 + side, :, first:last].astype(F32) + xin[q, :, first:last].astype(F32)
+
+            @pl.when(place > 0)
+            def _():
+                rightward(q, part).wait_recv()
+                g_ref[:, first:last] += lin[q, :, first:last].astype(F32)
+
+            @pl.when(place < m - 1)
+            def _():
+                leftward(q, part).wait_recv()
+                g_ref[:, first:last] += rin[q, :, first:last].astype(F32)
 
     def norm_copy(peer):
         return remote(ng_ref, norm_held.at[dp], norm_send.at[peer], norm_recv.at[dp], (peer, t))
@@ -1292,7 +1348,8 @@
 
     def give(q, right):
         lay(q * 2 + 1 - side)
-        across(q).start()
+        across(q, 0).start()
+        across(q, 1).start()
 
     cut = wp_ref.shape[1]
 
@@ -1378,15 +1435,16 @@
     norms_in()
 
     def finish(q, _):
-        across(q).wait_send()
-
-        @pl.when(q > place)
-        def _():
-            rightward(q).wait_send()
-
-        @pl.when(q < place)
-        def _():
-            leftward(q).wait_send()
+        for part in (0, 1):
+            across(q, part).wait_send()
+
+            @pl.when(q > place)
+            def _():
+                rightward(q, part).wait_send()
+
+            @pl.when(q < place)
+            def _():
+                leftward(q, part).wait_send()
 
         return 0
 
@@ -1420,7 +1478,7 @@
         out_specs=[VM] * 4,
         scratch_shapes=[low(n, block, wide), low(n * count, block, block)]
         + [low(m, block, wide)] * 3
-        + [pltpu.SemaphoreType.DMA((m,))] * 6
+        + [pltpu.SemaphoreType.DMA((m, 2))] * 6
         + total
         + total
         + [pltpu.VMEM((n, 4, width), F32), pltpu.SemaphoreType.DMA((n,)), pltpu.SemaphoreType.DMA((n,))]

time: 237 us -> 232 us (0.979)
  Pallas kernels: 226 us -> 222 us
    pallas_call x1, Pallas kernels: 51.4 us -> 48.1 us  [gather_masters(): pl.pallas_call(functools.partial(gather_kernel, n, count, block, wide, no...]
where the time goes in v7:
time: 232 us; the launch traced here: 229 us
  Pallas kernels  222 us (96%)
  local copies, waits for them, and re-layouts  3.47 us (1%)
  other arithmetic  2.81 us (1%)
    pallas_call x1, Pallas kernels, layer(): pl.pallas_call(functools.partial(layer_kernel, heads, shift_for(length),...  65.1 us
    pallas_call x1, Pallas kernels, settle(): pl.pallas_call(functools.partial(settle_kernel, n, count), out_shape=[jax...  57.1 us
    pallas_call x1, Pallas kernels, soap(): pl.pallas_call(functools.partial(soap_kernel, n, count), out_shape=[shape...  51.2 us
    pallas_call x1, Pallas kernels, gather_masters(): pl.pallas_call(functools.partial(gather_kernel, n, count, block, wide, no...  48.1 us

profile of v7, /device:TPU:0, one launch (start us, length us, event | category | flops | bytes accessed | tf_op | source)
XLA Modules:
  0.0 229.0 jit_solution(13419787780257020638)
XLA Ops:
  0.6 1.1 convert_reduce_fusion
  1.8 0.7 multiply_add_fusion.slot_ref
  2.5 0.3 select_reduce_fusion.inverse_ref
  2.8 0.0 copy-start.9
  2.8 2.0 copy.28
  4.8 0.0 copy-start
  4.8 0.0 copy-start.10
  4.8 0.0 copy-done.9
  4.8 48.1 %gather_masters.1 = (bf16[768,576]{1,0:T(8,128)(2,1)S(1)}, bf16[768,768]{1,0:T(8,128)(2,1)S(1)}, bf16[768,192]{1,0:T(8,128)(2,1)S(1)}, bf16[768,768]{1,0:T(8,128)(2,1)S(1)}, f32[4,768]{1,0:T(4,128)S(1)}) custom-call(s32[768]{0:T(1024)S(1)} %multiply_add_fusion.slot_ref, f32[96,48,48]{2,1,0:T(8,128)S(1)} %bitcast.75, f32[3,128]{1,0:T(4,128)S(1)} %bitcast.86), custom_call_target="tpu_custom_call" | custom-call | bytes 163200000 | tf_op jit(solution)/shard_map/gather_masters/pallas_call | solution.py:265
  52.9 0.0 copy-start.2
  52.9 1.4 copy-done.2
  54.3 65.1 %layer.1 = (bf16[768,2432]{1,0:T(8,128)(2,1)S(1)}, bf16[1024,768]{1,0:T(8,128)(2,1)S(1)}, bf16[1024,704]{1,0:T(8,128)(2,1)S(1)}, bf16[768,128]{1,0:T(8,128)(2,1)...) custom-call(bf16[1024,768]{1,0:T(8,128)(2,1)S(1)} %bitcast.76, ...), custom_call_target="tpu_custom_call" | custom-call | bytes 221000000 | tf_op jit(solution)/shard_map/layer/pallas_call | solution.py:1134
  119.5 0.0 copy-start.1
  119.5 0.0 copy-start.3
  119.5 0.0 copy-start.4
  119.5 0.0 copy-start.5
  119.5 0.0 copy-start.6
  119.5 0.0 copy-start.7
  119.5 0.0 copy-start.8
  119.6 57.1 %settle.1 = (f32[48,4608]{1,0:T(8,128)S(1)}, bf16[1024,768]{1,0:T(8,128)(2,1)S(1)}, f32[1024,768]{1,0:T(8,128)S(1)}, f32[4,768]{1,0:T(4,128)S(1)}) custom-call(s32[768]{0:T(1024)S(1)} %select_reduce_fusion.inverse_ref, bf16[768,2432]{1,0:T(8,128)(2,1)S(1)} %get-tuple-element.48.mat_ref, bf16[1024,768]{1,0:T(8,128)(2,1)S(1)} %get-tuple-element.49.out_in, ...), custom_call_target="tpu_custom_call" | custom-call | bytes 187000000 | tf_op jit(solution)/shard_map/settle/pallas_call | solution.py:1469
  176.8 0.0 copy-start.11
  176.8 0.0 copy-start.12
  176.8 51.2 %soap.1 = (f32[2304,96]{1,0:T(8,128)}, f32[2304,96]{1,0:T(8,128)}, f32[2304,96]{1,0:T(8,128)}, f32[2304,96]{1,0:T(8,128)}, f32[2304,96]{1,0:T(8,128)}, /*index=5...) custom-call(f32[48,4608]{1,0:T(8,128)S(1)} %get-tuple-element.56.packed_ref, ...), custom_call_target="tpu_custom_call" | custom-call | tf_op jit(solution)/shard_map/soap/pallas_call | solution.py:550
  228.0 0.7 multiply_subtract_fusion
  (12 shorter events, 0.0 us)
Async XLA Ops:
  2.8 2.0 copy-start.9
  4.8 48.1 %copy-start = (bf16[1,1024,768]{2,1,0:T(8,128)(2,1)S(1)}, bf16[1,1024,768]{2,1,0:T(8,128)(2,1)}, u32[]{:S(2)}) copy-start(bf16[1,1024,768]{2,1,0:T(8,128)(2,1)} %param.14) | copy-start | bytes 4718596
  4.8 48.1 %copy-start.10 = (s32[1,1024]{1,0:T(1,128)S(1)}, s32[1,1024]{1,0:T(1,128)}, u32[]{:S(2)}) copy-start(s32[1,1024]{1,0:T(1,128)} %seg_in.1) | copy-start | bytes 12292
  52.9 1.4 copy-start.2
  119.5 57.2 %copy-start.1 = (f32[1,96,48,48]{1,3,2,0:T(8,128)S(1)}, f32[1,96,48,48]{1,3,2,0:T(8,128)}, u32[]{:S(2)}) copy-start(f32[1,96,48,48]{1,3,2,0:T(8,128)} %param.18) | copy-start | bytes 2654212
  119.5 57.2 %copy-start.3 = (f32[1,96,48,48]{1,3,2,0:T(8,128)S(1)}, f32[1,96,48,48]{1,3,2,0:T(8,128)}, u32[]{:S(2)}) copy-start(f32[1,96,48,48]{1,3,2,0:T(8,128)} %param.19) | copy-start | bytes 2654212
  119.5 57.2 %copy-start.4 = (f32[1,96,48,48]{1,3,2,0:T(8,128)S(1)}, f32[1,96,48,48]{1,3,2,0:T(8,128)}, u32[]{:S(2)}) copy-start(f32[1,96,48,48]{1,3,2,0:T(8,128)} %param.20) | copy-start | bytes 2654212
  119.5 57.2 %copy-start.5 = (f32[1,96,48,48]{1,3,2,0:T(8,128)S(1)}, f32[1,96,48,48]{1,3,2,0:T(8,128)}, u32[]{:S(2)}) copy-start(f32[1,96,48,48]{1,3,2,0:T(8,128)} %param.21) | copy-start | bytes 2654212
  119.5 57.2 %copy-start.6 = (f32[1,96,48,48]{1,3,2,0:T(8,128)S(1)}, f32[1,96,48,48]{1,3,2,0:T(8,128)}, u32[]{:S(2)}) copy-start(f32[1,96,48,48]{1,3,2,0:T(8,128)} %param.22) | copy-start | bytes 2654212
  119.5 57.2 %copy-start.7 = (f32[1,96,48,48]{1,3,2,0:T(8,128)S(1)}, f32[1,96,48,48]{1,3,2,0:T(8,128)}, u32[]{:S(2)}) copy-start(f32[1,96,48,48]{1,3,2,0:T(8,128)} %param.23) | copy-start | bytes 2654212
  119.5 57.2 %copy-start.8 = (f32[1,96,48,48]{1,3,2,0:T(8,128)S(1)}, f32[1,96,48,48]{1,3,2,0:T(8,128)}, u32[]{:S(2)}) copy-start(f32[1,96,48,48]{1,3,2,0:T(8,128)} %param.24) | copy-start | bytes 2654212
  176.8 51.2 %copy-start.11 = (f32[384]{0:T(512)S(1)}, f32[384]{0:T(512)}, u32[]{:S(2)}) copy-start(f32[384]{0:T(512)} %param.27) | copy-start | bytes 4612
  176.8 51.2 %copy-start.12 = (f32[384]{0:T(512)S(1)}, f32[384]{0:T(512)}, u32[]{:S(2)}) copy-start(f32[384]{0:T(512)} %param.26) | copy-start | bytes 4612

commit v8 on v7

--- a/solution.py
+++ b/solution.py
@@ -30,12 +30,12 @@
     return math.log(length / 8.0)
 
 
-def block_slots(owner, per_dev):
+def block_slots(owner):
     count = owner.shape[0]
     index = jnp.arange(count, dtype=jnp.int32)
     earlier = (owner[:, None] == owner[None, :]) & (index[None, :] < index[:, None])
-    rank = jnp.sum(earlier.astype(jnp.int32), axis=1)
-    slots = owner * per_dev + rank
+    lower = owner[None, :] < owner[:, None]
+    slots = jnp.sum((earlier | lower).astype(jnp.int32), axis=1)
     inverse = jnp.sum(jnp.where(slots[None, :] == index[:, None], index[None, :], 0), axis=1)
     return (slots, inverse)
 
@@ -220,7 +220,7 @@
             )
         return 0
 
-    lax.fori_loop(0, rows, strip, 0)
+    lax.fori_loop(0, rows, strip, 0, unroll=2)
 
     line = nout_ref.shape[1]
     for source in range(n):
@@ -1251,7 +1251,7 @@
             u_scr[row * cols + c] = whole_row[:, c * size : (c + 1) * size]
         return 0
 
-    lax.fori_loop(0, mat_ref.shape[0] // size, chop, 0)
+    lax.fori_loop(0, mat_ref.shape[0] // size, chop, 0, unroll=2)
     greet([four.beside, four.over] + [(peer, t) for peer in peers])
 
     middle = wide // 256 * 128
@@ -1339,7 +1339,7 @@
                 p_ref[d, :, place] = strip(d * count + g * some)
                 return 0
 
-            lax.fori_loop(0, count // some, one, 0, unroll=3)
+            lax.fori_loop(0, count // some, one, 0, unroll=6)
         else:
             parts = [strip(d * count + g * some)[:, : some * size] for g in range(count // some)]
             if wide > count * size:
@@ -1522,9 +1522,8 @@
     width = inputs.shape[2]
     n_dp = lax.axis_size("dp")
     parts = lax.axis_size("tensor")
-    per_dev = masters.shape[1]
     block = masters.shape[-1]
-    slots, inverse = lax.optimization_barrier(block_slots(owner, per_dev))
+    slots, inverse = lax.optimization_barrier(block_slots(owner))
     pieces, norms = gather_masters(
         slots, masters[0], norm_master, n_dp, width // block, parts
     )

time: 232 us -> 231 us (level)
  no operation moved by 1% of the time
where the time goes in v8:
time: 231 us; the launch traced here: 227 us
  Pallas kernels  220 us (95%)
  local copies, waits for them, and re-layouts  3.47 us (2%)
    pallas_call x1, Pallas kernels, layer(): pl.pallas_call(functools.partial(layer_kernel, heads, shift_for(length),...  64.8 us
    pallas_call x1, Pallas kernels, settle(): pl.pallas_call(functools.partial(settle_kernel, n, count), out_shape=[jax...  56.6 us
    pallas_call x1, Pallas kernels, soap(): pl.pallas_call(functools.partial(soap_kernel, n, count), out_shape=[shape...  51.2 us
    pallas_call x1, Pallas kernels, gather_masters(): pl.pallas_call(functools.partial(gather_kernel, n, count, block, wide, no...  47.5 us

profile of v8, /device:TPU:0, one launch (start us, length us, event | category | flops | bytes accessed | tf_op | source)
XLA Modules:
  0.0 226.9 jit_solution(4546361464096411584)
XLA Ops:
  0.6 1.3 convert_reduce_fusion.slot_ref
  1.9 0.3 select_reduce_fusion.inverse_ref
  2.3 0.0 copy-start.9
  2.3 2.0 copy.28
  4.3 0.0 copy-start
  4.3 0.0 copy-start.10
  4.3 0.0 copy-done.9
  4.3 47.5 %gather_masters.1 = (bf16[768,576]{1,0:T(8,128)(2,1)S(1)}, bf16[768,768]{1,0:T(8,128)(2,1)S(1)}, bf16[768,192]{1,0:T(8,128)(2,1)S(1)}, bf16[768,768]{1,0:T(8,128)(2,1)S(1)}, f32[4,768]{1,0:T(4,128)S(1)}) custom-call(s32[768]{0:T(1024)S(1)} %convert_reduce_fusion.slot_ref, f32[96,48,48]{2,1,0:T(8,128)S(1)} %bitcast.75, f32[3,128]{1,0:T(4,128)S(1)} %bitcast.86), custom_call_target="tpu_custom_call" | custom-call | bytes 163200000 | tf_op jit(solution)/shard_map/gather_masters/pallas_call | solution.py:265
  51.8 0.0 copy-done
  51.8 0.0 copy-start.2
  51.8 1.4 copy-done.2
  53.2 64.8 %layer.1 = (bf16[768,2432]{1,0:T(8,128)(2,1)S(1)}, bf16[1024,768]{1,0:T(8,128)(2,1)S(1)}, bf16[1024,704]{1,0:T(8,128)(2,1)S(1)}, bf16[768,128]{1,0:T(8,128)(2,1)...) custom-call(bf16[1024,768]{1,0:T(8,128)(2,1)S(1)} %bitcast.76, ...), custom_call_target="tpu_custom_call" | custom-call | bytes 221000000 | tf_op jit(solution)/shard_map/layer/pallas_call | solution.py:1134
  118.0 0.0 copy-start.1
  118.0 0.0 copy-start.3
  118.1 0.0 copy-start.4
  118.1 0.0 copy-start.5
  118.1 0.0 copy-start.6
  118.1 0.0 copy-start.7
  118.1 0.0 copy-start.8
  118.1 56.6 %settle.1 = (f32[48,4608]{1,0:T(8,128)S(1)}, bf16[1024,768]{1,0:T(8,128)(2,1)S(1)}, f32[1024,768]{1,0:T(8,128)S(1)}, f32[4,768]{1,0:T(4,128)S(1)}) custom-call(s32[768]{0:T(1024)S(1)} %select_reduce_fusion.inverse_ref, bf16[768,2432]{1,0:T(8,128)(2,1)S(1)} %get-tuple-element.48.mat_ref, bf16[1024,768]{1,0:T(8,128)(2,1)S(1)} %get-tuple-element.49.out_in, ...), custom_call_target="tpu_custom_call" | custom-call | bytes 187000000 | tf_op jit(solution)/shard_map/settle/pallas_call | solution.py:1469
  174.8 0.0 copy-start.11
  174.8 0.0 copy-start.12
  174.8 51.2 %soap.1 = (f32[2304,96]{1,0:T(8,128)}, f32[2304,96]{1,0:T(8,128)}, f32[2304,96]{1,0:T(8,128)}, f32[2304,96]{1,0:T(8,128)}, f32[2304,96]{1,0:T(8,128)}, /*index=5...) custom-call(f32[48,4608]{1,0:T(8,128)S(1)} %get-tuple-element.56.packed_ref, ...), custom_call_target="tpu_custom_call" | custom-call | tf_op jit(solution)/shard_map/soap/pallas_call | solution.py:550
  226.0 0.7 multiply_subtract_fusion
  (11 shorter events, 0.0 us)
Async XLA Ops:
  2.3 2.0 copy-start.9
  4.3 47.5 %copy-start = (bf16[1,1024,768]{2,1,0:T(8,128)(2,1)S(1)}, bf16[1,1024,768]{2,1,0:T(8,128)(2,1)}, u32[]{:S(2)}) copy-start(bf16[1,1024,768]{2,1,0:T(8,128)(2,1)} %param.14) | copy-start | bytes 4718596
  4.3 47.5 %copy-start.10 = (s32[1,1024]{1,0:T(1,128)S(1)}, s32[1,1024]{1,0:T(1,128)}, u32[]{:S(2)}) copy-start(s32[1,1024]{1,0:T(1,128)} %seg_in.1) | copy-start | bytes 12292
  51.8 1.4 copy-start.2
  118.0 56.7 %copy-start.1 = (f32[1,96,48,48]{1,3,2,0:T(8,128)S(1)}, f32[1,96,48,48]{1,3,2,0:T(8,128)}, u32[]{:S(2)}) copy-start(f32[1,96,48,48]{1,3,2,0:T(8,128)} %param.18) | copy-start | bytes 2654212
  118.0 56.7 %copy-start.3 = (f32[1,96,48,48]{1,3,2,0:T(8,128)S(1)}, f32[1,96,48,48]{1,3,2,0:T(8,128)}, u32[]{:S(2)}) copy-start(f32[1,96,48,48]{1,3,2,0:T(8,128)} %param.19) | copy-start | bytes 2654212
  118.1 56.7 %copy-start.4 = (f32[1,96,48,48]{1,3,2,0:T(8,128)S(1)}, f32[1,96,48,48]{1,3,2,0:T(8,128)}, u32[]{:S(2)}) copy-start(f32[1,96,48,48]{1,3,2,0:T(8,128)} %param.20) | copy-start | bytes 2654212
  118.1 56.7 %copy-start.5 = (f32[1,96,48,48]{1,3,2,0:T(8,128)S(1)}, f32[1,96,48,48]{1,3,2,0:T(8,128)}, u32[]{:S(2)}) copy-start(f32[1,96,48,48]{1,3,2,0:T(8,128)} %param.21) | copy-start | bytes 2654212
  118.1 56.7 %copy-start.6 = (f32[1,96,48,48]{1,3,2,0:T(8,128)S(1)}, f32[1,96,48,48]{1,3,2,0:T(8,128)}, u32[]{:S(2)}) copy-start(f32[1,96,48,48]{1,3,2,0:T(8,128)} %param.22) | copy-start | bytes 2654212
  118.1 56.7 %copy-start.7 = (f32[1,96,48,48]{1,3,2,0:T(8,128)S(1)}, f32[1,96,48,48]{1,3,2,0:T(8,128)}, u32[]{:S(2)}) copy-start(f32[1,96,48,48]{1,3,2,0:T(8,128)} %param.23) | copy-start | bytes 2654212
  118.1 56.7 %copy-start.8 = (f32[1,96,48,48]{1,3,2,0:T(8,128)S(1)}, f32[1,96,48,48]{1,3,2,0:T(8,128)}, u32[]{:S(2)}) copy-start(f32[1,96,48,48]{1,3,2,0:T(8,128)} %param.24) | copy-start | bytes 2654212
  174.8 51.2 %copy-start.11 = (f32[384]{0:T(512)S(1)}, f32[384]{0:T(512)}, u32[]{:S(2)}) copy-start(f32[384]{0:T(512)} %param.27) | copy-start | bytes 4612
  174.8 51.2 %copy-start.12 = (f32[384]{0:T(512)S(1)}, f32[384]{0:T(512)}, u32[]{:S(2)}) copy-start(f32[384]{0:T(512)} %param.26) | copy-start | bytes 4612
